TPU v7x, 256 devices: a whole 4x4x8 slice. The times are simulated.
256 devices in a mesh: snap: 64 (over z, x, core), feat: 4 (over y).
Axes of the slice: x: 4, y: 4, z: 8, core: 2. Of those that a mesh axis runs over, the one named last changes fastest.
Arguments:
- node_features: bfloat16 [128, 4096, 256], P('snap', None, 'feat'), may hold values from -6 to 6
- tile_rows: int32 [128, 64], P('snap'), may hold values from 0 to 31
- tile_cols: int32 [128, 64], P('snap'), may hold values from 0 to 31, as said below
- tile_counts: int32 [128], P('snap'), may hold values from 4 to 64, as said below
- tile_values: bfloat16 [128, 64, 128, 128], P('snap'), may hold values from -0.5 to 0.5
- layer_one: bfloat16 [256, 256], replicated, may hold values from -0.375 to 0.375
- layer_two: bfloat16 [256, 256], replicated, may hold values from -0.375 to 0.375
- query_weight: bfloat16 [256, 256], replicated, may hold values from -1.25 to 1.25
- key_weight: bfloat16 [256, 256], replicated, may hold values from -1.25 to 1.25
- value_weight: bfloat16 [256, 256], replicated, may hold values from -0.375 to 0.375
- out_weight: bfloat16 [256, 256], replicated, may hold values from -0.375 to 0.375
Outputs:
- evolved: bfloat16 [128, 4096, 256], P('snap', None, 'feat')
Inputs may be any that keep to these rules, and one draw needn't show every extreme that they name: `tile_cols`: block columns of the tile slots; a coordinate pair may be listed more than once, and such tiles add. `tile_counts`: some snapshot uses all 64 slots.
All inputs are finite; a program needn't handle non-finite values.
Results may differ from a plain program's by a relative error of at most 0.02.
The roundings to bfloat16 on the way count: a program that leaves them out, or rounds other values in their place, can miss the bound.
Values may be sent and summed in bfloat16 or wider, within the bound.
No kernel may reach another device: no remote copies, remote signals or barrier semaphores. Data moves between devices by JAX's collectives and lax.ppermute only.
A program may use at most 64 MiB of HBM per device.

v0:
```python
import functools

import jax
import jax.numpy as jnp
from jax import lax
from jax.experimental import pallas as pl
from jax.experimental.pallas import tpu as pltpu
from jax.sharding import PartitionSpec as P

HEADS = 8
HEAD_DIM = 32
TILE = 128
D = 256
SNAPS = 128
VERT = 4096
BLOCKS = 32
MAXT = 64
F_DEV = 4
S_DEV = 64
F_W = D // F_DEV
V_F = VERT // F_DEV
V_S = V_F // S_DEV
GROUP = 8

masked_score = -1e30
f32 = jnp.float32
bf16 = jnp.bfloat16
NT = (((1,), (1,)), ((), ()))
MIB = 2**20


def params(mib):
    return pltpu.CompilerParams(vmem_limit_bytes=mib * MIB)


def spread_kernel(chunked, counts, rows, cols, x_ref, tiles_ref, out_ref, acc):
    t = pl.program_id(0)
    acc[...] = jnp.zeros_like(acc)
    n = counts[t]

    def group(g, _):
        products = []
        for j in range(GROUP):
            i = g * GROUP + j
            col = cols[t, i]
            if chunked:
                x = x_ref[col // 8, 0, :, pl.ds(pl.multiple_of((col % 8) * TILE, TILE), TILE)]
            else:
                x = x_ref[0, :, pl.ds(pl.multiple_of(col * TILE, TILE), TILE)]
            products.append(
                lax.dot_general(x, tiles_ref[0, i], NT, preferred_element_type=f32)
            )
        for j in range(GROUP):
            i = g * GROUP + j
            row = jnp.where(i < n, rows[t, i], BLOCKS)
            acc[row] += products[j]
        return 0

    lax.fori_loop(0, (n + GROUP - 1) // GROUP, group, 0)
    for b in range(BLOCKS):
        out_ref[b // 8, 0, :, (b % 8) * TILE : (b % 8 + 1) * TILE] = acc[b].astype(bf16)


def spread(x, tiles, rows, cols, counts, chunked):
    if chunked:
        x_spec = pl.BlockSpec((F_DEV, 1, F_W, V_F), lambda t, *_: (0, t, 0, 0))
    else:
        x_spec = pl.BlockSpec((1, F_W, VERT), lambda t, *_: (t, 0, 0))
    return pl.pallas_call(
        functools.partial(spread_kernel, chunked),
        grid_spec=pltpu.PrefetchScalarGridSpec(
            num_scalar_prefetch=3,
            grid=(2,),
            in_specs=[
                x_spec,
                pl.BlockSpec((1, MAXT, TILE, TILE), lambda t, *_: (t, 0, 0, 0)),
            ],
            out_specs=pl.BlockSpec((F_DEV, 1, F_W, V_F), lambda t, *_: (0, t, 0, 0)),
            scratch_shapes=[pltpu.VMEM((BLOCKS + 1, F_W, TILE), f32)],
        ),
        out_shape=jax.ShapeDtypeStruct((F_DEV, 2, F_W, V_F), bf16),
        compiler_params=params(24),
        name="spread",
    )(counts, rows, cols, x, tiles)


def mixed(s_ref, x_ref, w_ref):
    m = jnp.dot(w_ref[...].T, s_ref[...].reshape(D, V_F), preferred_element_type=f32)
    h = x_ref[...].reshape(D, V_F).astype(f32) + jnp.maximum(m, 0.0)
    return h.astype(bf16)


def mix_one_kernel(s_ref, x_ref, w_ref, out_ref):
    out_ref[...] = mixed(s_ref, x_ref, w_ref).reshape(F_DEV, 1, F_W, V_F)


def mix_two_kernel(s_ref, x_ref, w_ref, out_ref):
    out_ref[...] = mixed(s_ref, x_ref, w_ref).T.reshape(S_DEV, V_S, D)


def mix(s, x, w, last):
    chunk = pl.BlockSpec((F_DEV, 1, F_W, V_F), lambda t: (0, t, 0, 0))
    if last:
        out_spec = pl.BlockSpec((S_DEV, V_S, D), lambda t: (0, t, 0))
        out_shape = jax.ShapeDtypeStruct((S_DEV, 2 * V_S, D), bf16)
    else:
        out_spec = chunk
        out_shape = jax.ShapeDtypeStruct((F_DEV, 2, F_W, V_F), bf16)
    return pl.pallas_call(
        mix_two_kernel if last else mix_one_kernel,
        grid=(2,),
        in_specs=[chunk, chunk, pl.BlockSpec((D, D), lambda t: (0, 0))],
        out_specs=out_spec,
        out_shape=out_shape,
        compiler_params=params(24),
        name="mix",
    )(s, x, w)


def attend_kernel(h_ref, wq_ref, wk_ref, wv_ref, wo_ref, out_ref, hs, es, wqt, wvt):
    rows = SNAPS * V_S
    for k in range(2):
        hs[k] = h_ref[:, :, k * 128 : (k + 1) * 128].reshape(rows, 128).astype(f32)
    wqt[...] = wq_ref[...].T
    wvt[...] = wv_ref[...].T
    causal = lax.broadcasted_iota(jnp.int32, (SNAPS, SNAPS), 0) <= lax.broadcasted_iota(
        jnp.int32, (SNAPS, SNAPS), 1
    )
    scale = HEAD_DIM**-0.5

    def vertex(v, _):
        hv = jnp.concatenate([hs[k, pl.ds(v, SNAPS, stride=V_S), :] for k in range(2)], axis=1)
        hb = hv.astype(bf16)
        q_t = lax.dot_general(wqt[...], hb, NT, preferred_element_type=f32).astype(bf16)
        v_t = lax.dot_general(wvt[...], hb, NT, preferred_element_type=f32).astype(bf16)
        key = jnp.dot(hb, wk_ref[...], preferred_element_type=f32).astype(bf16)

        def padded(h):
            parts = [q_t[h * HEAD_DIM : (h + 1) * HEAD_DIM]]
            if h > 0:
                parts.insert(0, jnp.zeros((h * HEAD_DIM, SNAPS), bf16))
            if h < HEADS - 1:
                parts.append(jnp.zeros((D - (h + 1) * HEAD_DIM, SNAPS), bf16))
            return jnp.concatenate(parts, axis=0)

        context = []
        for pair in range(HEADS // 2):
            q_pair = jnp.concatenate([padded(2 * pair), padded(2 * pair + 1)], axis=1)
            scores = jnp.dot(key, q_pair, preferred_element_type=f32)
            for k in range(2):
                h = 2 * pair + k
                s = jnp.where(causal, scores[:, k * SNAPS : (k + 1) * SNAPS], masked_score)
                top = jnp.max(s, axis=0, keepdims=True)
                lifted = jnp.exp((s - top) * scale)
                total = jnp.sum(lifted, axis=0, keepdims=True)
                weights = (lifted * (1.0 / total)).astype(bf16)
                context.append(
                    jnp.dot(
                        v_t[h * HEAD_DIM : (h + 1) * HEAD_DIM],
                        weights,
                        preferred_element_type=f32,
                    ).astype(bf16)
                )
        context = jnp.concatenate(context, axis=0).T
        evolved = hv + jnp.dot(context, wo_ref[...], preferred_element_type=f32)
        for k in range(2):
            es[k, pl.ds(v, SNAPS, stride=V_S), :] = evolved[:, k * 128 : (k + 1) * 128]
        return 0

    lax.fori_loop(0, V_S, vertex, 0)
    low = lax.broadcasted_iota(jnp.int32, (V_S, 128), 1) < F_W

    def pack(s, _):
        for k in range(2):
            base = pl.multiple_of(s * 2 * V_S, 2 * V_S)
            even = es[k, pl.ds(base, V_S), :]
            odd = es[k, pl.ds(base + V_S, V_S), :]
            out_ref[2 * k, s] = jnp.where(low, even, pltpu.roll(odd, F_W, 1)).astype(bf16)
            out_ref[2 * k + 1, s] = jnp.where(low, pltpu.roll(even, F_W, 1), odd).astype(bf16)
        return 0

    lax.fori_loop(0, S_DEV, pack, 0, unroll=4)


def attend(hidden, wq, wk, wv, wo):
    rows = SNAPS * V_S
    return pl.pallas_call(
        attend_kernel,
        out_shape=jax.ShapeDtypeStruct((F_DEV, S_DEV, V_S, 2 * F_W), bf16),
        scratch_shapes=[
            pltpu.VMEM((2, rows, 128), f32),
            pltpu.VMEM((2, rows, 128), f32),
            pltpu.VMEM((D, D), bf16),
            pltpu.VMEM((D, D), bf16),
        ],
        compiler_params=params(32),
        name="attend",
    )(hidden, wq, wk, wv, wo)


def place_kernel(in_ref, out_ref):
    for g in range(8):
        block = in_ref[g * 8 : (g + 1) * 8].reshape(128, 128).T
        out_ref[0, :, g * 128 : (g + 1) * 128] = block[:F_W]
        out_ref[1, :, g * 128 : (g + 1) * 128] = block[F_W:]


def place(pieces):
    return pl.pallas_call(
        place_kernel,
        grid=(4,),
        in_specs=[pl.BlockSpec((S_DEV, V_S, 2 * F_W), lambda g: (g, 0, 0))],
        out_specs=pl.BlockSpec((2, F_W, V_F), lambda g: (0, 0, g)),
        out_shape=jax.ShapeDtypeStruct((2, F_W, VERT), bf16),
        compiler_params=params(24),
        name="place",
    )(pieces)


def on_device(
    node_features,
    tile_rows,
    tile_cols,
    tile_counts,
    tile_values,
    layer_one,
    layer_two,
    query_weight,
    key_weight,
    value_weight,
    out_weight,
):
    x = jnp.swapaxes(node_features, 1, 2)

    def turn(a):
        return lax.all_to_all(a, "feat", split_axis=0, concat_axis=0, tiled=True)

    x_rows = turn(jnp.moveaxis(x.reshape(2, F_W, F_DEV, V_F), 2, 0))
    s_one = spread(x, tile_values, tile_rows, tile_cols, tile_counts, False)
    hidden_one = mix(turn(s_one), x_rows, layer_one, False)
    s_two = spread(turn(hidden_one), tile_values, tile_rows, tile_cols, tile_counts, True)
    hidden_two = mix(turn(s_two), hidden_one, layer_two, True)
    owned = lax.all_to_all(hidden_two, "snap", split_axis=0, concat_axis=0, tiled=True)
    evolved = attend(owned, query_weight, key_weight, value_weight, out_weight)
    pieces = lax.all_to_all(
        evolved.reshape(F_DEV * S_DEV, V_S, 2 * F_W),
        ("feat", "snap"),
        split_axis=0,
        concat_axis=0,
        tiled=True,
    )
    return jnp.swapaxes(place(pieces), 1, 2)


def solution(mesh):
    placed = (
        P("snap", None, "feat"),
        P("snap", None),
        P("snap", None),
        P("snap"),
        P("snap", None, None, None),
        P(),
        P(),
        P(),
        P(),
        P(),
        P(),
    )
    return jax.shard_map(
        on_device, mesh=mesh, in_specs=placed, out_specs=P("snap", None, "feat"), check_vma=False
    )
```

profile of v0, /device:TPU:1, one launch (start us, length us, event | category | flops | bytes accessed | tf_op | source)
XLA Modules:
  0.0 187.9 jit_solution(15917819260543927401)
XLA Ops:
  0.0 2.2 %copy-done = bf16[2,64,128,128]{3,2,1,0:T(8,128)(2,1)S(1)} copy-done((bf16[2,64,128,128]{3,2,1,0:T(8,128)(2,1)S(1)}, bf16[2,64,128,128]{3,2,1,0:T(8,128)(2,1)}, u32[]{:S(2)}) %copy-start) | copy-done | bytes 4194328
  2.2 1.2 copy-done.2
  3.4 0.7 copy-done.10
  4.1 0.7 copy-done.12
  4.8 0.7 copy-done.14
  5.4 2.8 %spread.2 = bf16[4,2,64,1024]{3,2,1,0:T(8,128)(2,1)} custom-call(s32[2]{0:T(128)S(1)} %copy-done.14, s32[2,64]{1,0:T(2,128)S(1)} %copy-done.10, s32[2,64]{1,0:T(2,128)S(1)} %copy-done.12, bf16[2,64,4096]{2,1,0:T(8,128)(2,1)S(1)} %bitcast.11, bf16[2,64,128,128]{3,2,1,0:T(8,128)(2,1)S(1)} %copy-done), custom_call_target="tpu_custom_call" | custom-call | tf_op jit(solution)/shard_map/spread/pallas_call | solution.py:69
  8.3 5.1 %all-to-all-start = ((bf16[4,2,64,1024]{3,2,1,0:T(8,128)(2,1)}), bf16[4,2,64,1024]{3,2,1,0:T(8,128)(2,1)S(1)}, u32[]{:S(2)}, u32[]{:S(2)}) async-start(bf16[4,2,64,1024]{3,2,1,0:T(8,128)(2,1)} %spread.2), calls=%async_computation | async-start | bytes 2097152 | tf_op jit(solution)/shard_map/all_to_all | solution.py:236
  13.4 0.1 copy.15
  13.5 0.0 copy-start.11
  13.5 0.0 copy-start.13
  13.6 13.6 %all-to-all-done.s_ref = bf16[4,2,64,1024]{3,2,1,0:T(8,128)(2,1)S(1)} async-done(((bf16[4,2,64,1024]{3,2,1,0:T(8,128)(2,1)}), bf16[4,2,64,1024]{3,2,1,0:T(8,128)(2,1)S(1)}, u32[]{:S(2)}, u32[]{:S(2)}) %all-to-all-start) | async-done | bytes 1048608 | tf_op jit(solution)/shard_map/all_to_all | solution.py:236
  27.1 15.4 %all_to_all.30.x_ref = bf16[4,2,64,1024]{3,2,1,0:T(8,128)(2,1)S(1)} all-to-all(bf16[4,2,64,1024]{3,2,1,0:T(8,128)(2,1)S(1)} %bitcast.13), channel_id=1, replica_groups=mesh['snap'=64,'feat'=4] {'feat'}, dimensions={0} | all-to-all | bytes 2097152 | tf_op jit(solution)/shard_map/all_to_all | solution.py:236
  42.6 0.9 mix.2.x_ref
  43.5 14.3 %all_to_all.31.x_ref = bf16[4,2,64,1024]{3,2,1,0:T(8,128)(2,1)S(1)} all-to-all(bf16[4,2,64,1024]{3,2,1,0:T(8,128)(2,1)S(1)} %mix.2.x_ref), channel_id=1, replica_groups=mesh['snap'=64,'feat'=4] {'feat'}, dimensions={0} | all-to-all | bytes 2097152 | tf_op jit(solution)/shard_map/all_to_all | solution.py:236
  57.7 0.0 copy-start.5
  57.8 2.2 %spread.3 = bf16[4,2,64,1024]{3,2,1,0:T(8,128)(2,1)S(1)} custom-call(s32[2]{0:T(128)S(1)} %copy-done.15, s32[2,64]{1,0:T(2,128)S(1)} %copy-done.11, s32[2,64]{1,0:T(2,128)S(1)} %copy-done.13, bf16[4,2,64,1024]{3,2,1,0:T(8,128)(2,1)S(1)} %all_to_all.31.x_ref, bf16[2,64,128,128]{3,2,1,0:T(8,128)(2,1)S(1)} %copy-done.1), custom_call_target="tpu_custom_call" | custom-call | tf_op jit(solution)/shard_map/spread/pallas_call | solution.py:69
  60.0 0.0 copy-start.7
  60.0 0.0 copy-start.8
  60.1 13.8 %all_to_all.32.s_ref = bf16[4,2,64,1024]{3,2,1,0:T(8,128)(2,1)S(1)} all-to-all(bf16[4,2,64,1024]{3,2,1,0:T(8,128)(2,1)S(1)} %spread.3), channel_id=1, replica_groups=mesh['snap'=64,'feat'=4] {'feat'}, dimensions={0} | all-to-all | bytes 2097152 | tf_op jit(solution)/shard_map/all_to_all | solution.py:236
  73.8 1.0 mix.3
  74.9 52.9 %all_to_all.33.h_ref = bf16[64,32,256]{2,1,0:T(8,128)(2,1)S(1)} all-to-all(bf16[64,32,256]{2,1,0:T(8,128)(2,1)S(1)} %mix.3), channel_id=1, replica_groups=mesh['snap'=64,'feat'=4] {'snap'}, dimensions={0} | all-to-all | bytes 2097152 | tf_op jit(solution)/shard_map/all_to_all | solution.py:243
  127.7 20.3 %attend.1 = bf16[4,64,16,128]{3,2,1,0:T(8,128)(2,1)S(1)} custom-call(bf16[64,32,256]{2,1,0:T(8,128)(2,1)S(1)} %all_to_all.33.h_ref, bf16[256,256]{1,0:T(8,128)(2,1)S(1)} %copy-done.6, bf16[256,256]{1,0:T(8,128)(2,1)S(1)} %copy-done.7, bf16[256,256]{1,0:T(8,128)(2,1)S(1)} %copy-done.8, bf16[256,256]{1,0:T(8,128)(2,1)S(1)} %copy-done.9), custom_call_target="tpu_custom_call" | custom-call | tf_op jit(solution)/shard_map/attend/pallas_call | solution.py:187
  148.1 38.0 %all_to_all.34.in_ref = bf16[256,16,128]{2,1,0:T(8,128)(2,1)S(1)} all-to-all(bf16[256,16,128]{2,1,0:T(8,128)(2,1)S(1)} %bitcast.10), channel_id=1, replica_groups=mesh['snap'=64,'feat'=4] {'feat','snap'}, dimensions={0} | all-to-all | bytes 2097152 | tf_op jit(solution)/shard_map/all_to_all | solution.py:245
  186.1 1.8 place.1
  (22 shorter events, 0.0 us)
Async XLA Ops:
  0.0 2.2 %copy-start = (bf16[2,64,128,128]{3,2,1,0:T(8,128)(2,1)S(1)}, bf16[2,64,128,128]{3,2,1,0:T(8,128)(2,1)}, u32[]{:S(2)}) copy-start(bf16[2,64,128,128]{3,2,1,0:T(8,128)(2,1)} %tiles_ref.3) | copy-start | bytes 12582916
  2.2 1.2 copy-start.2
  3.4 0.7 copy-start.10
  4.1 0.7 copy-start.12
  4.8 0.7 copy-start.14
  5.4 8.0 %copy-start.3 = (bf16[2,4096,64]{1,2,0:T(8,128)(2,1)S(1)}, bf16[2,4096,64]{1,2,0:T(8,128)(2,1)}, u32[]{:S(2)}) copy-start(bf16[2,4096,64]{1,2,0:T(8,128)(2,1)} %param.11) | copy-start | bytes 3145732
  8.3 34.3 %copy-start.4 = (bf16[256,256]{1,0:T(8,128)(2,1)S(1)}, bf16[256,256]{1,0:T(8,128)(2,1)}, u32[]{:S(2)}) copy-start(bf16[256,256]{1,0:T(8,128)(2,1)} %w_ref.2) | copy-start | bytes 393220
  8.3 18.8 %all-to-all-start = ((bf16[4,2,64,1024]{3,2,1,0:T(8,128)(2,1)}), bf16[4,2,64,1024]{3,2,1,0:T(8,128)(2,1)S(1)}, u32[]{:S(2)}, u32[]{:S(2)}) async-start(bf16[4,2,64,1024]{3,2,1,0:T(8,128)(2,1)} %spread.2), calls=%async_computation | async-start | bytes 2097152 | tf_op jit(solution)/shard_map/all_to_all | solution.py:236
  13.5 44.2 %copy-start.11 = (s32[2,64]{1,0:T(2,128)S(1)}, s32[2,64]{1,0:T(2,128)}, u32[]{:S(2)}) copy-start(s32[2,64]{1,0:T(2,128)} %rows.3) | copy-start | bytes 1540
  13.5 44.2 %copy-start.13 = (s32[2,64]{1,0:T(2,128)S(1)}, s32[2,64]{1,0:T(2,128)}, u32[]{:S(2)}) copy-start(s32[2,64]{1,0:T(2,128)} %cols.3) | copy-start | bytes 1540
  13.5 44.2 %copy-start.15 = (s32[2]{0:T(128)S(1)}, s32[2]{0:T(128)}, u32[]{:S(2)}) copy-start(s32[2]{0:T(128)} %counts.3) | copy-start | bytes 28
  27.1 30.6 %copy-start.1 = (bf16[2,64,128,128]{3,2,1,0:T(8,128)(2,1)S(1)}, bf16[2,64,128,128]{3,2,1,0:T(8,128)(2,1)}, u32[]{:S(2)}) copy-start(bf16[2,64,128,128]{3,2,1,0:T(8,128)(2,1)} %tiles_ref.3) | copy-start | bytes 12582916
  57.7 16.1 %copy-start.5 = (bf16[256,256]{1,0:T(8,128)(2,1)S(1)}, bf16[256,256]{1,0:T(8,128)(2,1)}, u32[]{:S(2)}) copy-start(bf16[256,256]{1,0:T(8,128)(2,1)} %w_ref.3) | copy-start | bytes 393220
  60.0 67.7 %copy-start.6 = (bf16[256,256]{1,0:T(8,128)(2,1)S(1)}, bf16[256,256]{1,0:T(8,128)(2,1)}, u32[]{:S(2)}) copy-start(bf16[256,256]{1,0:T(8,128)(2,1)} %wq_ref.1) | copy-start | bytes 393220
  60.0 67.7 %copy-start.7 = (bf16[256,256]{1,0:T(8,128)(2,1)S(1)}, bf16[256,256]{1,0:T(8,128)(2,1)}, u32[]{:S(2)}) copy-start(bf16[256,256]{1,0:T(8,128)(2,1)} %wk_ref.1) | copy-start | bytes 393220
  60.0 67.7 %copy-start.8 = (bf16[256,256]{1,0:T(8,128)(2,1)S(1)}, bf16[256,256]{1,0:T(8,128)(2,1)}, u32[]{:S(2)}) copy-start(bf16[256,256]{1,0:T(8,128)(2,1)} %wv_ref.1) | copy-start | bytes 393220
  60.0 67.7 %copy-start.9 = (bf16[256,256]{1,0:T(8,128)(2,1)S(1)}, bf16[256,256]{1,0:T(8,128)(2,1)}, u32[]{:S(2)}) copy-start(bf16[256,256]{1,0:T(8,128)(2,1)} %wo_ref.1) | copy-start | bytes 393220
where the time goes:
time: 187 us; the launch traced here: 188 us
  blocking collectives  134 us (72%)
  Pallas kernels  29.1 us (16%)
  waiting for transfers between devices  13.6 us (7%)
  local copies, waits for them, and re-layouts  5.57 us (3%)
  starting transfers between devices  5.14 us (3%)
    all_to_all x1, blocking collectives, on_device(): lax.all_to_all(hidden_two, 'snap', split_axis=0, concat_axis=0, tiled=True)  52.9 us
    all_to_all x3, blocking collectives, turn(): return lax.all_to_all(a, 'feat', split_axis=0, concat_axis=0, tiled=True)  43.5 us
    all_to_all x1, blocking collectives, on_device(): lax.all_to_all(evolved.reshape(F_DEV * S_DEV, V_S, 2 * F_W), ('feat', 'sn...  38 us
    pallas_call x1, Pallas kernels, attend(): pl.pallas_call(attend_kernel, out_shape=jax.ShapeDtypeStruct((F_DEV, S_DE...  20.3 us
    all_to_all x1, waiting for transfers between devices, turn(): return lax.all_to_all(a, 'feat', split_axis=0, concat_axis=0, tiled=True)  13.6 us
    unnamed x32, local copies, waits for them, and re-layouts  5.48 us
    all_to_all x1, starting transfers between devices, turn(): return lax.all_to_all(a, 'feat', split_axis=0, concat_axis=0, tiled=True)  5.14 us
    pallas_call x2, Pallas kernels, spread(): pl.pallas_call(functools.partial(spread_kernel, chunked), grid_spec=pltpu...  5.09 us
  transfers between devices with their start and end apart: 1, of which 1 were waited for; matrix products, arithmetic and copies ran while one was open for 0% of the time, Pallas kernels for 0%

commit v1 on v0

v1 whole, which is shorter than its diff:
```python
import functools

import jax
import jax.numpy as jnp
from jax import lax
from jax.experimental import pallas as pl
from jax.experimental.pallas import tpu as pltpu
from jax.sharding import PartitionSpec as P

HEADS = 8
HEAD_DIM = 32
TILE = 128
D = 256
SNAPS = 128
VERT = 4096
BLOCKS = 32
MAXT = 64
F_DEV = 4
S_DEV = 64
F_W = D // F_DEV
V_F = VERT // F_DEV
V_S = V_F // S_DEV
GROUP = 8

masked_score = -1e30
f32 = jnp.float32
bf16 = jnp.bfloat16
NT = (((1,), (1,)), ((), ()))
MIB = 2**20


def params(mib):
    return pltpu.CompilerParams(vmem_limit_bytes=mib * MIB)


def cut_kernel(me, *refs):
    for k in range(F_DEV):
        refs[F_DEV + k][...] = refs[k][...]


def cut(me, x):
    def block(k):
        return pl.BlockSpec((2, F_W, V_F), lambda i, me: (0, 0, (me[0] + k) % F_DEV))

    return pl.pallas_call(
        cut_kernel,
        grid_spec=pltpu.PrefetchScalarGridSpec(
            num_scalar_prefetch=1,
            grid=(1,),
            in_specs=[block(k) for k in range(F_DEV)],
            out_specs=[pl.BlockSpec((2, F_W, V_F), lambda i, me: (0, 0, 0))] * F_DEV,
        ),
        out_shape=[CHUNK] * F_DEV,
        compiler_params=params(48),
        name="cut",
    )(me, *([x] * F_DEV))


def turn(blocks):
    return [blocks[0]] + [
        lax.ppermute(blocks[k], "feat", [(i, (i + k) % F_DEV) for i in range(F_DEV)])
        for k in (2, 1, 3)
    ]


def unturned(blocks):
    own, two, one, three = blocks
    return [own, one, two, three]


def spread_kernel(chunked, me_ref, counts, rows, cols, *refs):
    me = me_ref[0]
    if chunked:
        x_refs, (tiles_ref, *out_refs), (acc, xs) = refs[:F_DEV], refs[F_DEV : 2 * F_DEV + 1], refs[-2:]
        for k in range(F_DEV):
            xs[(me + F_DEV - k) % F_DEV] = x_refs[k][0]
    else:
        x_ref, tiles_ref, *out_refs, acc = refs
    t = pl.program_id(0)
    acc[...] = jnp.zeros_like(acc)
    n = counts[t]

    def group(g, _):
        products = []
        for j in range(GROUP):
            i = g * GROUP + j
            col = cols[t, i]
            if chunked:
                x = xs[col // 8, :, pl.ds(pl.multiple_of((col % 8) * TILE, TILE), TILE)]
            else:
                x = x_ref[0, :, pl.ds(pl.multiple_of(col * TILE, TILE), TILE)]
            products.append(
                lax.dot_general(x, tiles_ref[0, i], NT, preferred_element_type=f32)
            )
        for j in range(GROUP):
            i = g * GROUP + j
            row = jnp.where(i < n, rows[t, i], BLOCKS)
            acc[row] += products[j]
        return 0

    lax.fori_loop(0, (n + GROUP - 1) // GROUP, group, 0)
    for k in range(F_DEV):
        first = ((me + k) % F_DEV) * 8
        for b in range(8):
            out_refs[k][0, :, b * TILE : (b + 1) * TILE] = acc[first + b].astype(bf16)


CHUNK = jax.ShapeDtypeStruct((2, F_W, V_F), bf16)


def chunk_spec():
    return pl.BlockSpec((1, F_W, V_F), lambda t, *_: (t, 0, 0))


def spread(me, xs, tiles, rows, cols, counts):
    chunked = len(xs) > 1
    scratch = [pltpu.VMEM((BLOCKS + 1, F_W, TILE), f32)]
    if chunked:
        x_specs = [chunk_spec()] * F_DEV
        scratch.append(pltpu.VMEM((F_DEV, F_W, V_F), bf16))
    else:
        x_specs = [pl.BlockSpec((1, F_W, VERT), lambda t, *_: (t, 0, 0))]
    return pl.pallas_call(
        functools.partial(spread_kernel, chunked),
        grid_spec=pltpu.PrefetchScalarGridSpec(
            num_scalar_prefetch=4,
            grid=(2,),
            in_specs=x_specs
            + [pl.BlockSpec((1, MAXT, TILE, TILE), lambda t, *_: (t, 0, 0, 0))],
            out_specs=[chunk_spec()] * F_DEV,
            scratch_shapes=scratch,
        ),
        out_shape=[CHUNK] * F_DEV,
        compiler_params=params(SPREAD_MIB[chunked]),
        name="spread",
    )(me, counts, rows, cols, *xs, tiles)


SPREAD_MIB = (56, 24)


def relu_mix(me, s_refs, w_ref):
    weight = jnp.concatenate(
        [
            w_ref[pl.ds(pl.multiple_of(((me + F_DEV - k) % F_DEV) * F_W, F_W), F_W), :]
            for k in range(F_DEV)
        ],
        axis=0,
    )
    s = jnp.concatenate([r[0] for r in s_refs], axis=0)
    return jnp.maximum(jnp.dot(weight.T, s, preferred_element_type=f32), 0.0)


def mix_one_kernel(me_ref, *refs):
    me = me_ref[0]
    s_refs, x_refs, w_ref, whole_ref, out_refs = refs[:4], refs[4:8], refs[8], refs[9], refs[10:]
    for k in range(F_DEV):
        start = pl.multiple_of(((me + F_DEV - k) % F_DEV) * F_W, F_W)
        whole_ref[0, pl.ds(start, F_W), :] = x_refs[k][0]
    whole_ref[0] = (whole_ref[0].astype(f32) + relu_mix(me, s_refs, w_ref)).astype(bf16)
    for k in range(F_DEV):
        start = pl.multiple_of(((me + k) % F_DEV) * F_W, F_W)
        out_refs[k][0] = whole_ref[0, pl.ds(start, F_W), :]


def mix_two_kernel(me_ref, *refs):
    me = me_ref[0]
    s_refs, h_ref, w_ref, out_ref = refs[:4], refs[4], refs[5], refs[6]
    h = (h_ref[0].astype(f32) + relu_mix(me, s_refs, w_ref)).astype(bf16)
    out_ref[...] = h.T.reshape(S_DEV, V_S, D)


def mix_one(me, s, x, w):
    whole = pl.BlockSpec((1, D, V_F), lambda t, *_: (t, 0, 0))
    first, *rest = pl.pallas_call(
        mix_one_kernel,
        grid_spec=pltpu.PrefetchScalarGridSpec(
            num_scalar_prefetch=1,
            grid=(2,),
            in_specs=[chunk_spec()] * 8 + [pl.BlockSpec((D, D), lambda t, *_: (0, 0))],
            out_specs=[whole] + [chunk_spec()] * F_DEV,
        ),
        out_shape=[jax.ShapeDtypeStruct((2, D, V_F), bf16)] + [CHUNK] * F_DEV,
        compiler_params=params(24),
        name="mix_one",
    )(me, *s, *x, w)
    return first, rest


def mix_two(me, s, h, w):
    return pl.pallas_call(
        mix_two_kernel,
        grid_spec=pltpu.PrefetchScalarGridSpec(
            num_scalar_prefetch=1,
            grid=(2,),
            in_specs=[chunk_spec()] * F_DEV
            + [
                pl.BlockSpec((1, D, V_F), lambda t, *_: (t, 0, 0)),
                pl.BlockSpec((D, D), lambda t, *_: (0, 0)),
            ],
            out_specs=pl.BlockSpec((S_DEV, V_S, D), lambda t, *_: (0, t, 0)),
        ),
        out_shape=jax.ShapeDtypeStruct((S_DEV, 2 * V_S, D), bf16),
        compiler_params=params(24),
        name="mix_two",
    )(me, *s, h, w)


def attend_kernel(h_ref, wq_ref, wk_ref, wv_ref, wo_ref, out_ref, hs, es, hb, qt, vt, ks, ct):
    rows = SNAPS * V_S
    for k in range(2):
        hs[k] = h_ref[:, :, k * 128 : (k + 1) * 128].reshape(rows, 128).astype(f32)
    for v in range(V_S):
        for k in range(2):
            hb[v * SNAPS : (v + 1) * SNAPS, k * 128 : (k + 1) * 128] = hs[
                k, pl.ds(v, SNAPS, stride=V_S), :
            ].astype(bf16)
    wqt = wq_ref[...].T
    wvt = wv_ref[...].T

    def project(c, _):
        at = pl.ds(pl.multiple_of(c * 512, 512), 512)
        x = hb[at, :]
        qt[:, at] = lax.dot_general(wqt, x, NT, preferred_element_type=f32).astype(bf16)
        vt[:, at] = lax.dot_general(wvt, x, NT, preferred_element_type=f32).astype(bf16)
        ks[at, :] = jnp.dot(x, wk_ref[...], preferred_element_type=f32).astype(bf16)
        return 0

    lax.fori_loop(0, rows // 512, project, 0)
    causal = lax.broadcasted_iota(jnp.int32, (SNAPS, SNAPS), 0) <= lax.broadcasted_iota(
        jnp.int32, (SNAPS, SNAPS), 1
    )
    scale = HEAD_DIM**-0.5

    def vertex(v, _):
        at = pl.ds(pl.multiple_of(v * SNAPS, SNAPS), SNAPS)
        key = ks[at, :]

        def padded(h):
            parts = [qt[h * HEAD_DIM : (h + 1) * HEAD_DIM, at]]
            if h > 0:
                parts.insert(0, jnp.zeros((h * HEAD_DIM, SNAPS), bf16))
            if h < HEADS - 1:
                parts.append(jnp.zeros((D - (h + 1) * HEAD_DIM, SNAPS), bf16))
            return jnp.concatenate(parts, axis=0)

        for pair in range(HEADS // 2):
            q_pair = jnp.concatenate([padded(2 * pair), padded(2 * pair + 1)], axis=1)
            scores = jnp.dot(key, q_pair, preferred_element_type=f32)
            for k in range(2):
                head = slice((2 * pair + k) * HEAD_DIM, (2 * pair + k + 1) * HEAD_DIM)
                s = jnp.where(causal, scores[:, k * SNAPS : (k + 1) * SNAPS], masked_score)
                top = jnp.max(s, axis=0, keepdims=True)
                lifted = jnp.exp((s - top) * scale)
                total = jnp.sum(lifted, axis=0, keepdims=True)
                weights = (lifted * (1.0 / total)).astype(bf16)
                ct[head, at] = jnp.dot(
                    vt[head, at], weights, preferred_element_type=f32
                ).astype(bf16)
        return 0

    lax.fori_loop(0, V_S, vertex, 0, unroll=2)
    for v in range(V_S):
        mixed = jnp.dot(
            ct[:, v * SNAPS : (v + 1) * SNAPS].T, wo_ref[...], preferred_element_type=f32
        )
        for k in range(2):
            at = pl.ds(v, SNAPS, stride=V_S)
            es[k, at, :] = hs[k, at, :] + mixed[:, k * 128 : (k + 1) * 128]
    low = lax.broadcasted_iota(jnp.int32, (V_S, 128), 1) < F_W

    def pack(s, _):
        for k in range(2):
            base = pl.multiple_of(s * 2 * V_S, 2 * V_S)
            even = es[k, pl.ds(base, V_S), :]
            odd = es[k, pl.ds(base + V_S, V_S), :]
            out_ref[2 * k, s] = jnp.where(low, even, pltpu.roll(odd, F_W, 1)).astype(bf16)
            out_ref[2 * k + 1, s] = jnp.where(low, pltpu.roll(even, F_W, 1), odd).astype(bf16)
        return 0

    lax.fori_loop(0, S_DEV, pack, 0, unroll=4)


def attend(hidden, wq, wk, wv, wo):
    rows = SNAPS * V_S
    return pl.pallas_call(
        attend_kernel,
        out_shape=jax.ShapeDtypeStruct((F_DEV, S_DEV, V_S, 2 * F_W), bf16),
        scratch_shapes=[
            pltpu.VMEM((2, rows, 128), f32),
            pltpu.VMEM((2, rows, 128), f32),
            pltpu.VMEM((rows, D), bf16),
            pltpu.VMEM((D, rows), bf16),
            pltpu.VMEM((D, rows), bf16),
            pltpu.VMEM((rows, D), bf16),
            pltpu.VMEM((D, rows), bf16),
        ],
        compiler_params=params(32),
        name="attend",
    )(hidden, wq, wk, wv, wo)


def place_kernel(in_ref, out_ref):
    for g in range(8):
        block = in_ref[g * 8 : (g + 1) * 8].reshape(128, 128).T
        out_ref[0, :, g * 128 : (g + 1) * 128] = block[:F_W]
        out_ref[1, :, g * 128 : (g + 1) * 128] = block[F_W:]


def place(pieces):
    return pl.pallas_call(
        place_kernel,
        grid=(4,),
        in_specs=[pl.BlockSpec((S_DEV, V_S, 2 * F_W), lambda g: (g, 0, 0))],
        out_specs=pl.BlockSpec((2, F_W, V_F), lambda g: (0, 0, g)),
        out_shape=jax.ShapeDtypeStruct((2, F_W, VERT), bf16),
        compiler_params=params(24),
        name="place",
    )(pieces)


def on_device(
    node_features,
    tile_rows,
    tile_cols,
    tile_counts,
    tile_values,
    layer_one,
    layer_two,
    query_weight,
    key_weight,
    value_weight,
    out_weight,
):
    x = jnp.swapaxes(node_features, 1, 2)
    me = lax.axis_index("feat").astype(jnp.int32).reshape(1)
    lists = (tile_values, tile_rows, tile_cols, tile_counts)

    x_rows = unturned(turn(cut(me, x)))
    s_one = unturned(turn(spread(me, [x], *lists)))
    hidden_one, h_cut = mix_one(me, s_one, x_rows, layer_one)
    s_two = unturned(turn(spread(me, unturned(turn(h_cut)), *lists)))
    hidden_two = mix_two(me, s_two, hidden_one, layer_two)
    owned = lax.all_to_all(hidden_two, "snap", split_axis=0, concat_axis=0, tiled=True)
    evolved = attend(owned, query_weight, key_weight, value_weight, out_weight)
    pieces = lax.all_to_all(
        evolved.reshape(F_DEV * S_DEV, V_S, 2 * F_W),
        ("feat", "snap"),
        split_axis=0,
        concat_axis=0,
        tiled=True,
    )
    return jnp.swapaxes(place(pieces), 1, 2)


def solution(mesh):
    placed = (
        P("snap", None, "feat"),
        P("snap", None),
        P("snap", None),
        P("snap"),
        P("snap", None, None, None),
        P(),
        P(),
        P(),
        P(),
        P(),
        P(),
    )
    return jax.shard_map(
        on_device, mesh=mesh, in_specs=placed, out_specs=P("snap", None, "feat"), check_vma=False
    )
```

time: 187 us -> 160 us (0.86)
  blocking collectives: 134 us -> 83.5 us
  waiting for transfers between devices: 13.6 us -> 34.9 us
  starting transfers between devices: 5.14 us -> 18 us
  Pallas kernels: 29.1 us -> 21.6 us
  local copies, waits for them, and re-layouts: 5.57 us -> 2.23 us
    all_to_all x3 -> x0, blocking collectives: 43.5 us -> none  [turn(): return lax.all_to_all(a, 'feat', split_axis=0, concat_axis=0, tiled=True)]
    ppermute x0 -> x12, waiting for transfers between devices: none -> 34.9 us  [turn(): lax.ppermute(blocks[k], 'feat', [(i, (i + k) % F_DEV) for i in range(F_DE...]
    ppermute x0 -> x12, starting transfers between devices: none -> 18 us  [turn(): lax.ppermute(blocks[k], 'feat', [(i, (i + k) % F_DEV) for i in range(F_DE...]
    all_to_all x1 -> x0, waiting for transfers between devices: 13.6 us -> none  [turn(): return lax.all_to_all(a, 'feat', split_axis=0, concat_axis=0, tiled=True)]
    pallas_call x1, Pallas kernels: 20.3 us -> 10.9 us  [attend(): pl.pallas_call(attend_kernel, out_shape=jax.ShapeDtypeStruct((F_DEV, S_DE...]
    all_to_all x1, blocking collectives: 52.9 us -> 43.6 us  [on_device(): lax.all_to_all(hidden_two, 'snap', split_axis=0, concat_axis=0, tiled=True)]
    all_to_all x1 -> x0, starting transfers between devices: 5.14 us -> none  [turn(): return lax.all_to_all(a, 'feat', split_axis=0, concat_axis=0, tiled=True)]
    unnamed x32 -> x24, local copies, waits for them, and re-layouts: 5.48 us -> 2.23 us
  transfers between devices with their start and end apart: 1 -> 12, of which waited for: 1 -> 7; matrix products, arithmetic and copies ran while one was open for 0% -> 0% of each run, Pallas kernels for 0% -> 3%
where the time goes in v1:
time: 160 us
  blocking collectives  83.5 us (52%)
  waiting for transfers between devices  34.9 us (22%)
  Pallas kernels  21.6 us (14%)
  starting transfers between devices  18 us (11%)
  local copies, waits for them, and re-layouts  2.23 us (1%)
    all_to_all x1, blocking collectives, on_device(): lax.all_to_all(hidden_two, 'snap', split_axis=0, concat_axis=0, tiled=True)  43.6 us
    all_to_all x1, blocking collectives, on_device(): lax.all_to_all(evolved.reshape(F_DEV * S_DEV, V_S, 2 * F_W), ('feat', 'sn...  39.9 us
    ppermute x12, waiting for transfers between devices, turn(): lax.ppermute(blocks[k], 'feat', [(i, (i + k) % F_DEV) for i in range(F_DE...  34.9 us
    ppermute x12, starting transfers between devices, turn(): lax.ppermute(blocks[k], 'feat', [(i, (i + k) % F_DEV) for i in range(F_DE...  18 us
    pallas_call x1, Pallas kernels, attend(): pl.pallas_call(attend_kernel, out_shape=jax.ShapeDtypeStruct((F_DEV, S_DE...  10.9 us
    pallas_call x2, Pallas kernels, spread(): pl.pallas_call(functools.partial(spread_kernel, chunked), grid_spec=pltpu...  7.09 us
  transfers between devices with their start and end apart: 12, of which 7 were waited for; matrix products, arithmetic and copies ran while one was open for 0% of the time, Pallas kernels for 3%

profile of v1, /device:TPU:1, one launch (start us, length us, event | category | flops | bytes accessed | tf_op | source)
XLA Modules:
  0.0 160.4 jit_solution(14750845032010922091)
XLA Ops:
  0.0 1.2 copy-done
  1.3 2.2 %collective-permute-start.3 = (bf16[2,64,1024]{2,1,0:T(8,128)(2,1)S(1)}, bf16[2,64,1024]{2,1,0:T(8,128)(2,1)S(1)}, u32[]{:S(2)}, u32[]{:S(2)}) collective-permute-start(bf16[2,64,1024]{2,1,0:T(8,128)(2,1)S(1)} %get-tuple-element.27), channel_id=1, source_target_pairs={{0,1},{1,2},{2,3},{3,0},{4,5},{5,6},{6,7},{7,4},{8,9},{9,10},{10,1... | collective-permute-start | bytes 786440 | tf_op jit(solution)/shard_map/ppermute | solution.py:61
  3.6 2.6 %collective-permute-start.4 = (bf16[2,64,1024]{2,1,0:T(8,128)(2,1)S(1)}, bf16[2,64,1024]{2,1,0:T(8,128)(2,1)S(1)}, u32[]{:S(2)}, u32[]{:S(2)}) collective-permute-start(bf16[2,64,1024]{2,1,0:T(8,128)(2,1)S(1)} %get-tuple-element.28), channel_id=1, source_target_pairs={{0,2},{1,3},{2,0},{3,1},{4,6},{5,7},{6,4},{7,5},{8,10},{9,11},{10,... | collective-permute-start | bytes 786440 | tf_op jit(solution)/shard_map/ppermute | solution.py:61
  6.2 1.1 collective-permute-start.5
  7.2 4.9 %spread.2 = (bf16[2,64,1024]{2,1,0:T(8,128)(2,1)}, bf16[2,64,1024]{2,1,0:T(8,128)(2,1)}, bf16[2,64,1024]{2,1,0:T(8,128)(2,1)}, bf16[2,64,1024]{2,1,0:T(8,128)(2,1)}) custom-call(s32[1]{0:T(128)} %bitcast.me_ref.me, s32[2]{0:T(128)} %counts.3, s32[2,64]{1,0:T(2,128)} %rows.3, s32[2,64]{1,0:T(2,128)} %cols.3, bf16[2,64,4096]{2,1,0:T(8,128)(2,1)} %bitcast.4, ...), custom_call_target="tpu_custom_call" | custom-call | tf_op jit(solution)/shard_map/spread/pallas_call | solution.py:123
  13.4 1.7 %collective-permute-start.2 = (bf16[2,64,1024]{2,1,0:T(8,128)(2,1)}, bf16[2,64,1024]{2,1,0:T(8,128)(2,1)S(1)}, u32[]{:S(2)}, u32[]{:S(2)}) collective-permute-start(bf16[2,64,1024]{2,1,0:T(8,128)(2,1)} %get-tuple-element.25), channel_id=1, source_target_pairs={{0,3},{1,0},{2,1},{3,2},{4,7},{5,4},{6,5},{7,6},{8,11},{9,8},{10,9... | collective-permute-start | bytes 786440 | tf_op jit(solution)/shard_map/ppermute | solution.py:61
  15.1 2.4 %collective-permute-done.4.refs_6_ = bf16[2,64,1024]{2,1,0:T(8,128)(2,1)S(1)} collective-permute-done((bf16[2,64,1024]{2,1,0:T(8,128)(2,1)S(1)}, bf16[2,64,1024]{2,1,0:T(8,128)(2,1)S(1)}, u32[]{:S(2)}, u32[]{:S(2)}) %collective-permute-start.4) | collective-permute-done | bytes 262176 | tf_op jit(solution)/shard_map/ppermute | solution.py:61
  17.5 7.0 %collective-permute-done.refs_1_ = bf16[2,64,1024]{2,1,0:T(8,128)(2,1)S(1)} collective-permute-done((bf16[2,64,1024]{2,1,0:T(8,128)(2,1)}, bf16[2,64,1024]{2,1,0:T(8,128)(2,1)S(1)}, u32[]{:S(2)}, u32[]{:S(2)}) %collective-permute-start) | collective-permute-done | bytes 262176 | tf_op jit(solution)/shard_map/ppermute | solution.py:61
  24.5 4.2 %collective-permute-done.1.refs_2_ = bf16[2,64,1024]{2,1,0:T(8,128)(2,1)S(1)} collective-permute-done((bf16[2,64,1024]{2,1,0:T(8,128)(2,1)}, bf16[2,64,1024]{2,1,0:T(8,128)(2,1)S(1)}, u32[]{:S(2)}, u32[]{:S(2)}) %collective-permute-start.1) | collective-permute-done | bytes 262176 | tf_op jit(solution)/shard_map/ppermute | solution.py:61
  28.7 0.9 copy-done.2
  30.5 1.3 collective-permute-start.6
  31.8 2.4 %collective-permute-start.7 = (bf16[2,64,1024]{2,1,0:T(8,128)(2,1)S(1)}, bf16[2,64,1024]{2,1,0:T(8,128)(2,1)S(1)}, u32[]{:S(2)}, u32[]{:S(2)}) collective-permute-start(bf16[2,64,1024]{2,1,0:T(8,128)(2,1)S(1)} %get-tuple-element.32), channel_id=1, source_target_pairs={{0,2},{1,3},{2,0},{3,1},{4,6},{5,7},{6,4},{7,5},{8,10},{9,11},{10,... | collective-permute-start | bytes 786440 | tf_op jit(solution)/shard_map/ppermute | solution.py:61
  34.7 3.3 %collective-permute-done.6.refs_1_ = bf16[2,64,1024]{2,1,0:T(8,128)(2,1)S(1)} collective-permute-done((bf16[2,64,1024]{2,1,0:T(8,128)(2,1)S(1)}, bf16[2,64,1024]{2,1,0:T(8,128)(2,1)S(1)}, u32[]{:S(2)}, u32[]{:S(2)}) %collective-permute-start.6) | collective-permute-done | bytes 262176 | tf_op jit(solution)/shard_map/ppermute | solution.py:61
  38.0 7.2 %collective-permute-done.7.refs_2_ = bf16[2,64,1024]{2,1,0:T(8,128)(2,1)S(1)} collective-permute-done((bf16[2,64,1024]{2,1,0:T(8,128)(2,1)S(1)}, bf16[2,64,1024]{2,1,0:T(8,128)(2,1)S(1)}, u32[]{:S(2)}, u32[]{:S(2)}) %collective-permute-start.7) | collective-permute-done | bytes 262176 | tf_op jit(solution)/shard_map/ppermute | solution.py:61
  45.3 2.2 %spread.3 = (bf16[2,64,1024]{2,1,0:T(8,128)(2,1)S(1)}, bf16[2,64,1024]{2,1,0:T(8,128)(2,1)S(1)}, bf16[2,64,1024]{2,1,0:T(8,128)(2,1)S(1)}, bf16[2,64,1024]{2,1,0:T(8,128)(2,1)S(1)}) custom-call(s32[1]{0:T(128)} %bitcast.me_ref.me, s32[2]{0:T(128)S(1)} %copy-done.11, s32[2,64]{1,0:T(2,128)S(1)} %copy-done.9, s32[2,64]{1,0:T(2,128)S(1)} %copy-done.10, ...), custom_call_target="tpu_custom_call" | custom-call | tf_op jit(solution)/shard_map/spread/pallas_call | solution.py:123
  47.5 2.5 %collective-permute-start.9 = (bf16[2,64,1024]{2,1,0:T(8,128)(2,1)S(1)}, bf16[2,64,1024]{2,1,0:T(8,128)(2,1)S(1)}, u32[]{:S(2)}, u32[]{:S(2)}) collective-permute-start(bf16[2,64,1024]{2,1,0:T(8,128)(2,1)S(1)} %get-tuple-element.35), channel_id=1, source_target_pairs={{0,1},{1,2},{2,3},{3,0},{4,5},{5,6},{6,7},{7,4},{8,9},{9,10},{10,1... | collective-permute-start | bytes 786440 | tf_op jit(solution)/shard_map/ppermute | solution.py:61
  50.0 1.8 %collective-permute-start.10 = (bf16[2,64,1024]{2,1,0:T(8,128)(2,1)S(1)}, bf16[2,64,1024]{2,1,0:T(8,128)(2,1)S(1)}, u32[]{:S(2)}, u32[]{:S(2)}) collective-permute-start(bf16[2,64,1024]{2,1,0:T(8,128)(2,1)S(1)} %get-tuple-element.36), channel_id=1, source_target_pairs={{0,2},{1,3},{2,0},{3,1},{4,6},{5,7},{6,4},{7,5},{8,10},{9,11},{10,... | collective-permute-start | bytes 786440 | tf_op jit(solution)/shard_map/ppermute | solution.py:61
  52.5 3.2 %collective-permute-done.9.refs_1_ = bf16[2,64,1024]{2,1,0:T(8,128)(2,1)S(1)} collective-permute-done((bf16[2,64,1024]{2,1,0:T(8,128)(2,1)S(1)}, bf16[2,64,1024]{2,1,0:T(8,128)(2,1)S(1)}, u32[]{:S(2)}, u32[]{:S(2)}) %collective-permute-start.9) | collective-permute-done | bytes 262176 | tf_op jit(solution)/shard_map/ppermute | solution.py:61
  55.6 7.5 %collective-permute-done.10.refs_2_ = bf16[2,64,1024]{2,1,0:T(8,128)(2,1)S(1)} collective-permute-done((bf16[2,64,1024]{2,1,0:T(8,128)(2,1)S(1)}, bf16[2,64,1024]{2,1,0:T(8,128)(2,1)S(1)}, u32[]{:S(2)}, u32[]{:S(2)}) %collective-permute-start.10) | collective-permute-done | bytes 262176 | tf_op jit(solution)/shard_map/ppermute | solution.py:61
  63.2 0.9 mix_two.1
  64.1 43.6 %all_to_all.10.h_ref = bf16[64,32,256]{2,1,0:T(8,128)(2,1)S(1)} all-to-all(bf16[64,32,256]{2,1,0:T(8,128)(2,1)S(1)} %mix_two.1), channel_id=1, replica_groups=mesh['snap'=64,'feat'=4] {'snap'}, dimensions={0} | all-to-all | bytes 2097152 | tf_op jit(solution)/shard_map/all_to_all | solution.py:344
  107.7 10.9 %attend.1 = bf16[4,64,16,128]{3,2,1,0:T(8,128)(2,1)S(1)} custom-call(bf16[64,32,256]{2,1,0:T(8,128)(2,1)S(1)} %all_to_all.10.h_ref, bf16[256,256]{1,0:T(8,128)(2,1)S(1)} %copy-done.5, bf16[256,256]{1,0:T(8,128)(2,1)S(1)} %copy-done.6, bf16[256,256]{1,0:T(8,128)(2,1)S(1)} %copy-done.7, bf16[256,256]{1,0:T(8,128)(2,1)S(1)} %copy-done.8), custom_call_target="tpu_custom_call" | custom-call | tf_op jit(solution)/shard_map/attend/pallas_call | solution.py:286
  118.7 39.9 %all_to_all.11.in_ref = bf16[256,16,128]{2,1,0:T(8,128)(2,1)S(1)} all-to-all(bf16[256,16,128]{2,1,0:T(8,128)(2,1)S(1)} %bitcast.9), channel_id=1, replica_groups=mesh['snap'=64,'feat'=4] {'feat','snap'}, dimensions={0} | all-to-all | bytes 2097152 | tf_op jit(solution)/shard_map/all_to_all | solution.py:346
  158.6 1.8 %place.1 = bf16[2,64,4096]{2,1,0:T(8,128)(2,1)} custom-call(bf16[256,16,128]{2,1,0:T(8,128)(2,1)S(1)} %all_to_all.11.in_ref), custom_call_target="tpu_custom_call" | custom-call | tf_op jit(solution)/shard_map/place/pallas_call | solution.py:311
  (33 shorter events, 3.3 us)
Async XLA Ops:
  0.0 1.2 copy-start
  1.2 27.5 %copy-start.3 = (bf16[256,256]{1,0:T(8,128)(2,1)S(1)}, bf16[256,256]{1,0:T(8,128)(2,1)}, u32[]{:S(2)}) copy-start(bf16[256,256]{1,0:T(8,128)(2,1)} %refs_8_.1) | copy-start | bytes 393220
  1.3 43.9 %copy-start.1 = (bf16[2,64,128,128]{3,2,1,0:T(8,128)(2,1)S(1)}, bf16[2,64,128,128]{3,2,1,0:T(8,128)(2,1)}, u32[]{:S(2)}) copy-start(bf16[2,64,128,128]{3,2,1,0:T(8,128)(2,1)} %refs_4_.1) | copy-start | bytes 12582916
  1.3 43.9 %copy-start.9 = (s32[2,64]{1,0:T(2,128)S(1)}, s32[2,64]{1,0:T(2,128)}, u32[]{:S(2)}) copy-start(s32[2,64]{1,0:T(2,128)} %rows.3) | copy-start | bytes 1540
  1.3 43.9 %copy-start.10 = (s32[2,64]{1,0:T(2,128)S(1)}, s32[2,64]{1,0:T(2,128)}, u32[]{:S(2)}) copy-start(s32[2,64]{1,0:T(2,128)} %cols.3) | copy-start | bytes 1540
  1.3 43.9 %copy-start.11 = (s32[2]{0:T(128)S(1)}, s32[2]{0:T(128)}, u32[]{:S(2)}) copy-start(s32[2]{0:T(128)} %counts.3) | copy-start | bytes 28
  1.3 12.0 %collective-permute-start.3 = (bf16[2,64,1024]{2,1,0:T(8,128)(2,1)S(1)}, bf16[2,64,1024]{2,1,0:T(8,128)(2,1)S(1)}, u32[]{:S(2)}, u32[]{:S(2)}) collective-permute-start(bf16[2,64,1024]{2,1,0:T(8,128)(2,1)S(1)} %get-tuple-element.27), channel_id=1, source_target_pairs={{0,1},{1,2},{2,3},{3,0},{4,5},{5,6},{6,7},{7,4},{8,9},{9,10},{10,1... | collective-permute-start | bytes 786440 | tf_op jit(solution)/shard_map/ppermute | solution.py:61
  3.6 13.9 %collective-permute-start.4 = (bf16[2,64,1024]{2,1,0:T(8,128)(2,1)S(1)}, bf16[2,64,1024]{2,1,0:T(8,128)(2,1)S(1)}, u32[]{:S(2)}, u32[]{:S(2)}) collective-permute-start(bf16[2,64,1024]{2,1,0:T(8,128)(2,1)S(1)} %get-tuple-element.28), channel_id=1, source_target_pairs={{0,2},{1,3},{2,0},{3,1},{4,6},{5,7},{6,4},{7,5},{8,10},{9,11},{10,... | collective-permute-start | bytes 786440 | tf_op jit(solution)/shard_map/ppermute | solution.py:61
  6.2 11.3 %collective-permute-start.5 = (bf16[2,64,1024]{2,1,0:T(8,128)(2,1)S(1)}, bf16[2,64,1024]{2,1,0:T(8,128)(2,1)S(1)}, u32[]{:S(2)}, u32[]{:S(2)}) collective-permute-start(bf16[2,64,1024]{2,1,0:T(8,128)(2,1)S(1)} %get-tuple-element.29), channel_id=1, source_target_pairs={{0,3},{1,0},{2,1},{3,2},{4,7},{5,4},{6,5},{7,6},{8,11},{9,8},{10,9... | collective-permute-start | bytes 786440 | tf_op jit(solution)/shard_map/ppermute | solution.py:61
  7.2 56.0 %copy-start.4 = (bf16[256,256]{1,0:T(8,128)(2,1)S(1)}, bf16[256,256]{1,0:T(8,128)(2,1)}, u32[]{:S(2)}) copy-start(bf16[256,256]{1,0:T(8,128)(2,1)} %refs_5_.1) | copy-start | bytes 393220
  12.2 12.3 %collective-permute-start = (bf16[2,64,1024]{2,1,0:T(8,128)(2,1)}, bf16[2,64,1024]{2,1,0:T(8,128)(2,1)S(1)}, u32[]{:S(2)}, u32[]{:S(2)}) collective-permute-start(bf16[2,64,1024]{2,1,0:T(8,128)(2,1)} %get-tuple-element.23), channel_id=1, source_target_pairs={{0,1},{1,2},{2,3},{3,0},{4,5},{5,6},{6,7},{7,4},{8,9},{9,10},{10,1... | collective-permute-start | bytes 786440 | tf_op jit(solution)/shard_map/ppermute | solution.py:61
  12.6 16.2 %collective-permute-start.1 = (bf16[2,64,1024]{2,1,0:T(8,128)(2,1)}, bf16[2,64,1024]{2,1,0:T(8,128)(2,1)S(1)}, u32[]{:S(2)}, u32[]{:S(2)}) collective-permute-start(bf16[2,64,1024]{2,1,0:T(8,128)(2,1)} %get-tuple-element.24), channel_id=1, source_target_pairs={{0,2},{1,3},{2,0},{3,1},{4,6},{5,7},{6,4},{7,5},{8,10},{9,11},{10,... | collective-permute-start | bytes 786440 | tf_op jit(solution)/shard_map/ppermute | solution.py:61
  13.4 15.4 %collective-permute-start.2 = (bf16[2,64,1024]{2,1,0:T(8,128)(2,1)}, bf16[2,64,1024]{2,1,0:T(8,128)(2,1)S(1)}, u32[]{:S(2)}, u32[]{:S(2)}) collective-permute-start(bf16[2,64,1024]{2,1,0:T(8,128)(2,1)} %get-tuple-element.25), channel_id=1, source_target_pairs={{0,3},{1,0},{2,1},{3,2},{4,7},{5,4},{6,5},{7,6},{8,11},{9,8},{10,9... | collective-permute-start | bytes 786440 | tf_op jit(solution)/shard_map/ppermute | solution.py:61
  28.7 1.0 copy-start.2
  30.5 7.5 %collective-permute-start.6 = (bf16[2,64,1024]{2,1,0:T(8,128)(2,1)S(1)}, bf16[2,64,1024]{2,1,0:T(8,128)(2,1)S(1)}, u32[]{:S(2)}, u32[]{:S(2)}) collective-permute-start(bf16[2,64,1024]{2,1,0:T(8,128)(2,1)S(1)} %get-tuple-element.31), channel_id=1, source_target_pairs={{0,1},{1,2},{2,3},{3,0},{4,5},{5,6},{6,7},{7,4},{8,9},{9,10},{10,1... | collective-permute-start | bytes 786440 | tf_op jit(solution)/shard_map/ppermute | solution.py:61
  31.8 13.4 %collective-permute-start.7 = (bf16[2,64,1024]{2,1,0:T(8,128)(2,1)S(1)}, bf16[2,64,1024]{2,1,0:T(8,128)(2,1)S(1)}, u32[]{:S(2)}, u32[]{:S(2)}) collective-permute-start(bf16[2,64,1024]{2,1,0:T(8,128)(2,1)S(1)} %get-tuple-element.32), channel_id=1, source_target_pairs={{0,2},{1,3},{2,0},{3,1},{4,6},{5,7},{6,4},{7,5},{8,10},{9,11},{10,... | collective-permute-start | bytes 786440 | tf_op jit(solution)/shard_map/ppermute | solution.py:61
  34.2 11.0 %collective-permute-start.8 = (bf16[2,64,1024]{2,1,0:T(8,128)(2,1)S(1)}, bf16[2,64,1024]{2,1,0:T(8,128)(2,1)S(1)}, u32[]{:S(2)}, u32[]{:S(2)}) collective-permute-start(bf16[2,64,1024]{2,1,0:T(8,128)(2,1)S(1)} %get-tuple-element.33), channel_id=1, source_target_pairs={{0,3},{1,0},{2,1},{3,2},{4,7},{5,4},{6,5},{7,6},{8,11},{9,8},{10,9... | collective-permute-start | bytes 786440 | tf_op jit(solution)/shard_map/ppermute | solution.py:61
  45.3 62.4 %copy-start.5 = (bf16[256,256]{1,0:T(8,128)(2,1)S(1)}, bf16[256,256]{1,0:T(8,128)(2,1)}, u32[]{:S(2)}) copy-start(bf16[256,256]{1,0:T(8,128)(2,1)} %wq_ref.1) | copy-start | bytes 393220
  45.3 62.4 %copy-start.6 = (bf16[256,256]{1,0:T(8,128)(2,1)S(1)}, bf16[256,256]{1,0:T(8,128)(2,1)}, u32[]{:S(2)}) copy-start(bf16[256,256]{1,0:T(8,128)(2,1)} %wk_ref.1) | copy-start | bytes 393220
  45.3 62.4 %copy-start.7 = (bf16[256,256]{1,0:T(8,128)(2,1)S(1)}, bf16[256,256]{1,0:T(8,128)(2,1)}, u32[]{:S(2)}) copy-start(bf16[256,256]{1,0:T(8,128)(2,1)} %wv_ref.1) | copy-start | bytes 393220
  45.3 62.4 %copy-start.8 = (bf16[256,256]{1,0:T(8,128)(2,1)S(1)}, bf16[256,256]{1,0:T(8,128)(2,1)}, u32[]{:S(2)}) copy-start(bf16[256,256]{1,0:T(8,128)(2,1)} %wo_ref.1) | copy-start | bytes 393220
  47.5 8.2 %collective-permute-start.9 = (bf16[2,64,1024]{2,1,0:T(8,128)(2,1)S(1)}, bf16[2,64,1024]{2,1,0:T(8,128)(2,1)S(1)}, u32[]{:S(2)}, u32[]{:S(2)}) collective-permute-start(bf16[2,64,1024]{2,1,0:T(8,128)(2,1)S(1)} %get-tuple-element.35), channel_id=1, source_target_pairs={{0,1},{1,2},{2,3},{3,0},{4,5},{5,6},{6,7},{7,4},{8,9},{9,10},{10,1... | collective-permute-start | bytes 786440 | tf_op jit(solution)/shard_map/ppermute | solution.py:61
  50.0 13.2 %collective-permute-start.10 = (bf16[2,64,1024]{2,1,0:T(8,128)(2,1)S(1)}, bf16[2,64,1024]{2,1,0:T(8,128)(2,1)S(1)}, u32[]{:S(2)}, u32[]{:S(2)}) collective-permute-start(bf16[2,64,1024]{2,1,0:T(8,128)(2,1)S(1)} %get-tuple-element.36), channel_id=1, source_target_pairs={{0,2},{1,3},{2,0},{3,1},{4,6},{5,7},{6,4},{7,5},{8,10},{9,11},{10,... | collective-permute-start | bytes 786440 | tf_op jit(solution)/shard_map/ppermute | solution.py:61
  51.7 11.5 %collective-permute-start.11 = (bf16[2,64,1024]{2,1,0:T(8,128)(2,1)S(1)}, bf16[2,64,1024]{2,1,0:T(8,128)(2,1)S(1)}, u32[]{:S(2)}, u32[]{:S(2)}) collective-permute-start(bf16[2,64,1024]{2,1,0:T(8,128)(2,1)S(1)} %get-tuple-element.37), channel_id=1, source_target_pairs={{0,3},{1,0},{2,1},{3,2},{4,7},{5,4},{6,5},{7,6},{8,11},{9,8},{10,9... | collective-permute-start | bytes 786440 | tf_op jit(solution)/shard_map/ppermute | solution.py:61

commit v2 on v1

v2 whole, which is shorter than its diff:
```python
import functools

import jax
import jax.numpy as jnp
from jax import lax
from jax.experimental import pallas as pl
from jax.experimental.pallas import tpu as pltpu
from jax.sharding import PartitionSpec as P

HEADS = 8
HEAD_DIM = 32
TILE = 128
D = 256
SNAPS = 128
VERT = 4096
BLOCKS = 32
MAXT = 64
F_DEV = 4
S_DEV = 64
F_W = D // F_DEV
V_F = VERT // F_DEV
V_S = V_F // S_DEV
GROUP = 8

masked_score = -1e30
f32 = jnp.float32
bf16 = jnp.bfloat16
NT = (((1,), (1,)), ((), ()))
MIB = 2**20


def params(mib):
    return pltpu.CompilerParams(vmem_limit_bytes=mib * MIB)


GROUPS = MAXT // GROUP
SMEM = pl.BlockSpec(memory_space=pltpu.SMEM)
HBM = pl.BlockSpec(memory_space=pl.ANY)
VMEM = pl.BlockSpec(memory_space=pltpu.VMEM)
CHUNK = jax.ShapeDtypeStruct((F_W, V_F), bf16)
PAIR = jax.ShapeDtypeStruct((2, F_W, V_F), bf16)


def cost(us):
    return pl.CostEstimate(flops=int(us * 1e9), bytes_accessed=2**20, transcendentals=0)


def turn(blocks):
    sent = {
        k: lax.ppermute(blocks[k], "feat", [(i, (i + k) % F_DEV) for i in range(F_DEV)])
        for k in (2, 1, 3)
    }
    return [blocks[0], sent[1], sent[2], sent[3]]


def add_tiles(t, counts, rows, cols, features, tiles, acc, ready):
    n = counts[t]
    acc[...] = jnp.zeros_like(acc)

    def group(g, _):
        ready(g)
        products = []
        for j in range(GROUP):
            i = g * GROUP + j
            products.append(
                lax.dot_general(features(cols[t, i]), tiles(i), NT, preferred_element_type=f32)
            )
        for j in range(GROUP):
            i = g * GROUP + j
            row = jnp.where(i < n, rows[t, i], BLOCKS)
            acc[row] += products[j]
        return 0

    lax.fori_loop(0, (n + GROUP - 1) // GROUP, group, 0)


def spread_one_kernel(t, me_ref, counts, rows, cols, x_hbm, tiles_hbm, *refs):
    out_refs, (acc, x, tiles, x_sem, sems) = refs[:F_DEV], refs[F_DEV:]
    me = me_ref[0]
    fetch_x = pltpu.make_async_copy(x_hbm.at[t], x, x_sem)
    fetch_x.start()

    def fetch(g):
        at = pl.ds(g * GROUP, GROUP)
        return pltpu.make_async_copy(tiles_hbm.at[t, at], tiles.at[at], sems.at[g])

    def start(g, _):
        fetch(g).start()
        return 0

    lax.fori_loop(0, (counts[t] + GROUP - 1) // GROUP, start, 0)
    fetch_x.wait()
    add_tiles(
        t,
        counts,
        rows,
        cols,
        lambda col: x[:, pl.ds(pl.multiple_of(col * TILE, TILE), TILE)],
        lambda i: tiles[i],
        acc,
        lambda g: fetch(g).wait(),
    )
    for k in range(F_DEV):
        block = (me + k) % F_DEV
        out_refs[k][0] = x[:, pl.ds(pl.multiple_of(block * V_F, V_F), V_F)]
        for b in range(8):
            out_refs[k][1, :, b * TILE : (b + 1) * TILE] = acc[block * 8 + b].astype(bf16)


def spread_one(t, me, x, tiles, rows, cols, counts):
    return pl.pallas_call(
        functools.partial(spread_one_kernel, t),
        in_specs=[SMEM] * 4 + [HBM] * 2,
        out_specs=[VMEM] * F_DEV,
        out_shape=[PAIR] * F_DEV,
        scratch_shapes=[
            pltpu.VMEM((BLOCKS + 1, F_W, TILE), f32),
            pltpu.VMEM((F_W, VERT), bf16),
            pltpu.VMEM((MAXT, TILE, TILE), bf16),
            pltpu.SemaphoreType.DMA,
            pltpu.SemaphoreType.DMA((GROUPS,)),
        ],
        compiler_params=params(SPREAD_MIB),
        cost_estimate=cost(4),
        name="spread_one",
    )(me, counts, rows, cols, x, tiles)


SPREAD_MIB = 56


def spread_two_kernel(t, me_ref, counts, rows, cols, *refs):
    h_refs, tiles, out_refs, (acc, h) = refs[:4], refs[4], refs[5:9], refs[9:]
    me = me_ref[0]
    for k in range(F_DEV):
        h[(me + F_DEV - k) % F_DEV] = h_refs[k][...]
    add_tiles(
        t,
        counts,
        rows,
        cols,
        lambda col: h[col // 8, :, pl.ds(pl.multiple_of((col % 8) * TILE, TILE), TILE)],
        lambda i: tiles[0, i],
        acc,
        lambda g: None,
    )
    for k in range(F_DEV):
        block = (me + k) % F_DEV
        for b in range(8):
            out_refs[k][:, b * TILE : (b + 1) * TILE] = acc[block * 8 + b].astype(bf16)


def spread_two(t, me, h, tiles, rows, cols, counts):
    def full(dims):
        return pl.BlockSpec(dims, lambda i: (0,) * len(dims))

    return pl.pallas_call(
        functools.partial(spread_two_kernel, t),
        grid=(1,),
        in_specs=[SMEM] * 4
        + [full((F_W, V_F))] * F_DEV
        + [pl.BlockSpec((1, MAXT, TILE, TILE), lambda i: (t, 0, 0, 0))],
        out_specs=[full((F_W, V_F))] * F_DEV,
        out_shape=[CHUNK] * F_DEV,
        scratch_shapes=[
            pltpu.VMEM((BLOCKS + 1, F_W, TILE), f32),
            pltpu.VMEM((F_DEV, F_W, V_F), bf16),
        ],
        compiler_params=params(20),
        cost_estimate=cost(3),
        name="spread_two",
    )(me, counts, rows, cols, *h, tiles)


def relu_mix(me, parts, w_ref):
    weight = jnp.concatenate(
        [
            w_ref[pl.ds(pl.multiple_of(((me + F_DEV - k) % F_DEV) * F_W, F_W), F_W), :]
            for k in range(F_DEV)
        ],
        axis=0,
    )
    s = jnp.concatenate(parts, axis=0)
    return jnp.maximum(jnp.dot(weight.T, s, preferred_element_type=f32), 0.0)


def mix_one_kernel(me_ref, *refs):
    me = me_ref[0]
    in_refs, w_ref, whole_ref, out_refs = refs[:4], refs[4], refs[5], refs[6:]
    for k in range(F_DEV):
        start = pl.multiple_of(((me + F_DEV - k) % F_DEV) * F_W, F_W)
        whole_ref[pl.ds(start, F_W), :] = in_refs[k][0]
    mixed = relu_mix(me, [r[1] for r in in_refs], w_ref)
    whole_ref[...] = (whole_ref[...].astype(f32) + mixed).astype(bf16)
    for k in range(F_DEV):
        start = pl.multiple_of(((me + k) % F_DEV) * F_W, F_W)
        out_refs[k][...] = whole_ref[pl.ds(start, F_W), :]


def mix_one(me, parts, w):
    first, *rest = pl.pallas_call(
        mix_one_kernel,
        in_specs=[SMEM] + [VMEM] * 5,
        out_specs=[VMEM] * 5,
        out_shape=[jax.ShapeDtypeStruct((D, V_F), bf16)] + [CHUNK] * F_DEV,
        compiler_params=params(16),
        cost_estimate=cost(1),
        name="mix_one",
    )(me, *parts, w)
    return first, rest


def mix_two_kernel(last, me_ref, *refs):
    me = me_ref[0]
    s_refs, h_ref, w_ref, out_ref = refs[:4], refs[4], refs[5], refs[-1]
    mixed = relu_mix(me, [r[...] for r in s_refs], w_ref)
    h = (h_ref[...].astype(f32) + mixed).astype(bf16).T.reshape(S_DEV, V_S, D)
    if last:
        out_ref[:, :V_S, :] = refs[6][...]
        out_ref[:, V_S:, :] = h
    else:
        out_ref[...] = h


def mix_two(me, s, h, w, before):
    last = len(before)
    return pl.pallas_call(
        functools.partial(mix_two_kernel, last),
        in_specs=[SMEM] + [VMEM] * (6 + last),
        out_specs=VMEM,
        out_shape=jax.ShapeDtypeStruct((S_DEV, V_S * (1 + last), D), bf16),
        compiler_params=params(16),
        cost_estimate=cost(1),
        name="mix_two",
    )(me, *s, h, w, *before)


def attend_kernel(h_ref, wq_ref, wk_ref, wv_ref, wo_ref, out_ref, hs, es, hb, qt, vt, ks, ct):
    rows = SNAPS * V_S
    for k in range(2):
        hs[k] = h_ref[:, :, k * 128 : (k + 1) * 128].reshape(rows, 128).astype(f32)
    for v in range(V_S):
        for k in range(2):
            hb[v * SNAPS : (v + 1) * SNAPS, k * 128 : (k + 1) * 128] = hs[
                k, pl.ds(v, SNAPS, stride=V_S), :
            ].astype(bf16)
    wqt = wq_ref[...].T
    wvt = wv_ref[...].T

    def project(c, _):
        at = pl.ds(pl.multiple_of(c * 512, 512), 512)
        x = hb[at, :]
        qt[:, at] = lax.dot_general(wqt, x, NT, preferred_element_type=f32).astype(bf16)
        vt[:, at] = lax.dot_general(wvt, x, NT, preferred_element_type=f32).astype(bf16)
        ks[at, :] = jnp.dot(x, wk_ref[...], preferred_element_type=f32).astype(bf16)
        return 0

    lax.fori_loop(0, rows // 512, project, 0)
    causal = lax.broadcasted_iota(jnp.int32, (SNAPS, SNAPS), 0) <= lax.broadcasted_iota(
        jnp.int32, (SNAPS, SNAPS), 1
    )
    scale = HEAD_DIM**-0.5

    def vertex(v, _):
        at = pl.ds(pl.multiple_of(v * SNAPS, SNAPS), SNAPS)
        key = ks[at, :]

        def padded(h):
            parts = [qt[h * HEAD_DIM : (h + 1) * HEAD_DIM, at]]
            if h > 0:
                parts.insert(0, jnp.zeros((h * HEAD_DIM, SNAPS), bf16))
            if h < HEADS - 1:
                parts.append(jnp.zeros((D - (h + 1) * HEAD_DIM, SNAPS), bf16))
            return jnp.concatenate(parts, axis=0)

        for pair in range(HEADS // 2):
            q_pair = jnp.concatenate([padded(2 * pair), padded(2 * pair + 1)], axis=1)
            scores = jnp.dot(key, q_pair, preferred_element_type=f32)
            for k in range(2):
                head = slice((2 * pair + k) * HEAD_DIM, (2 * pair + k + 1) * HEAD_DIM)
                s = jnp.where(causal, scores[:, k * SNAPS : (k + 1) * SNAPS], masked_score)
                top = jnp.max(s, axis=0, keepdims=True)
                lifted = jnp.exp((s - top) * scale)
                total = jnp.sum(lifted, axis=0, keepdims=True)
                weights = (lifted * (1.0 / total)).astype(bf16)
                ct[head, at] = jnp.dot(
                    vt[head, at], weights, preferred_element_type=f32
                ).astype(bf16)
        return 0

    lax.fori_loop(0, V_S, vertex, 0, unroll=4)
    for v in range(V_S):
        mixed = jnp.dot(
            ct[:, v * SNAPS : (v + 1) * SNAPS].T, wo_ref[...], preferred_element_type=f32
        )
        for k in range(2):
            at = pl.ds(v, SNAPS, stride=V_S)
            es[k, at, :] = hs[k, at, :] + mixed[:, k * 128 : (k + 1) * 128]
    low = lax.broadcasted_iota(jnp.int32, (PACK, V_S, 128), 2) < F_W

    def pack(c, _):
        base = pl.multiple_of(c * PACK * 2 * V_S, PACK * 2 * V_S)
        at = pl.ds(c * PACK, PACK)
        for k in range(2):
            both = es[k, pl.ds(base, PACK * 2 * V_S), :].reshape(PACK, 2, V_S, 128)
            even, odd = both[:, 0], both[:, 1]
            out_ref[2 * k, at] = jnp.where(low, even, pltpu.roll(odd, F_W, 2)).astype(bf16)
            out_ref[2 * k + 1, at] = jnp.where(low, pltpu.roll(even, F_W, 2), odd).astype(bf16)
        return 0

    lax.fori_loop(0, S_DEV // PACK, pack, 0)


PACK = 16


def attend(hidden, wq, wk, wv, wo):
    rows = SNAPS * V_S
    return pl.pallas_call(
        attend_kernel,
        out_shape=jax.ShapeDtypeStruct((F_DEV, S_DEV, V_S, 2 * F_W), bf16),
        scratch_shapes=[
            pltpu.VMEM((2, rows, 128), f32),
            pltpu.VMEM((2, rows, 128), f32),
            pltpu.VMEM((rows, D), bf16),
            pltpu.VMEM((D, rows), bf16),
            pltpu.VMEM((D, rows), bf16),
            pltpu.VMEM((rows, D), bf16),
            pltpu.VMEM((D, rows), bf16),
        ],
        compiler_params=params(32),
        name="attend",
    )(hidden, wq, wk, wv, wo)


def place_kernel(in_ref, out_ref):
    for g in range(8):
        block = in_ref[g * 8 : (g + 1) * 8].reshape(128, 128).T
        out_ref[0, :, g * 128 : (g + 1) * 128] = block[:F_W]
        out_ref[1, :, g * 128 : (g + 1) * 128] = block[F_W:]


def place(pieces):
    return pl.pallas_call(
        place_kernel,
        grid=(4,),
        in_specs=[pl.BlockSpec((S_DEV, V_S, 2 * F_W), lambda g: (g, 0, 0))],
        out_specs=pl.BlockSpec((2, F_W, V_F), lambda g: (0, 0, g)),
        out_shape=jax.ShapeDtypeStruct((2, F_W, VERT), bf16),
        compiler_params=params(24),
        name="place",
    )(pieces)


def on_device(
    node_features,
    tile_rows,
    tile_cols,
    tile_counts,
    tile_values,
    layer_one,
    layer_two,
    query_weight,
    key_weight,
    value_weight,
    out_weight,
):
    x = jnp.swapaxes(node_features, 1, 2)
    me = lax.axis_index("feat").astype(jnp.int32).reshape(1)
    lists = (tile_values, tile_rows, tile_cols, tile_counts)

    both = range(2)
    s_one = [turn(spread_one(t, me, x, *lists)) for t in both]
    ones = [mix_one(me, s_one[t], layer_one) for t in both]
    h_one = [turn(ones[t][1]) for t in both]
    s_two = [turn(spread_two(t, me, h_one[t], *lists)) for t in both]
    hidden = []
    for t in both:
        hidden = [mix_two(me, s_two[t], ones[t][0], layer_two, hidden)]
    owned = lax.all_to_all(hidden[0], "snap", split_axis=0, concat_axis=0, tiled=True)
    evolved = attend(owned, query_weight, key_weight, value_weight, out_weight)
    pieces = lax.all_to_all(
        evolved.reshape(F_DEV * S_DEV, V_S, 2 * F_W),
        ("feat", "snap"),
        split_axis=0,
        concat_axis=0,
        tiled=True,
    )
    return jnp.swapaxes(place(pieces), 1, 2)


def solution(mesh):
    placed = (
        P("snap", None, "feat"),
        P("snap", None),
        P("snap", None),
        P("snap"),
        P("snap", None, None, None),
        P(),
        P(),
        P(),
        P(),
        P(),
        P(),
    )
    return jax.shard_map(
        on_device, mesh=mesh, in_specs=placed, out_specs=P("snap", None, "feat"), check_vma=False
    )
```

time: 160 us -> 149 us (0.931)
  waiting for transfers between devices: 34.9 us -> 14.4 us
  starting transfers between devices: 18 us -> 25.6 us
  blocking collectives: 83.5 us -> 85.7 us
  Pallas kernels: 21.6 us -> 23.3 us
    ppermute x12 -> x18, waiting for transfers between devices: 34.9 us -> 14.4 us  [turn(): lax.ppermute(blocks[k], 'feat', [(i, (i + k) % F_DEV) for i in range(F_DE...]
    ppermute x12 -> x18, starting transfers between devices: 18 us -> 25.6 us  [turn(): lax.ppermute(blocks[k], 'feat', [(i, (i + k) % F_DEV) for i in range(F_DE...]
    pallas_call x5 -> x8, Pallas kernels: 8.85 us -> 12.5 us  [the longest x2 7.72 us: spread_one(): pl.pallas_call(functools.partial(spread_one_kernel, t), in_specs=[SMEM] *...]
    all_to_all x1, blocking collectives: 43.6 us -> 46.2 us  [on_device(): lax.all_to_all(hidden[0], 'snap', split_axis=0, concat_axis=0, tiled=True)]
    pallas_call x1, Pallas kernels: 10.9 us -> 8.94 us  [attend(): pl.pallas_call(attend_kernel, out_shape=jax.ShapeDtypeStruct((F_DEV, S_DE...]
  transfers between devices with their start and end apart: 12 -> 18, of which waited for: 7 -> 6; matrix products, arithmetic and copies ran while one was open for 0% -> 0% of each run, Pallas kernels for 3% -> 6%
where the time goes in v2:
time: 149 us; the launch traced here: 150 us
  blocking collectives  85.7 us (58%)
  starting transfers between devices  25.6 us (17%)
  Pallas kernels  23.3 us (16%)
  waiting for transfers between devices  14.4 us (10%)
    all_to_all x1, blocking collectives, on_device(): lax.all_to_all(hidden[0], 'snap', split_axis=0, concat_axis=0, tiled=True)  46.2 us
    all_to_all x1, blocking collectives, on_device(): lax.all_to_all(evolved.reshape(F_DEV * S_DEV, V_S, 2 * F_W), ('feat', 'sn...  39.5 us
    ppermute x18, starting transfers between devices, turn(): lax.ppermute(blocks[k], 'feat', [(i, (i + k) % F_DEV) for i in range(F_DE...  25.6 us
    ppermute x18, waiting for transfers between devices, turn(): lax.ppermute(blocks[k], 'feat', [(i, (i + k) % F_DEV) for i in range(F_DE...  14.4 us
    pallas_call x1, Pallas kernels, attend(): pl.pallas_call(attend_kernel, out_shape=jax.ShapeDtypeStruct((F_DEV, S_DE...  8.94 us
    pallas_call x2, Pallas kernels, spread_one(): pl.pallas_call(functools.partial(spread_one_kernel, t), in_specs=[SMEM] *...  7.72 us
    pallas_call x2, Pallas kernels, spread_two(): pl.pallas_call(functools.partial(spread_two_kernel, t), grid=(1,), in_spe...  3.24 us
  transfers between devices with their start and end apart: 18, of which 6 were waited for; matrix products, arithmetic and copies ran while one was open for 0% of the time, Pallas kernels for 6%

profile of v2, /device:TPU:1, one launch (start us, length us, event | category | flops | bytes accessed | tf_op | source)
XLA Modules:
  0.0 150.2 jit_solution(14140143178433230187)
XLA Ops:
  0.0 3.3 %spread_one.3 = (bf16[2,64,1024]{2,1,0:T(8,128)(2,1)}, bf16[2,64,1024]{2,1,0:T(8,128)(2,1)}, bf16[2,64,1024]{2,1,0:T(8,128)(2,1)}, bf16[2,64,1024]{2,1,0:T(8,128)(2,1)}) custom-call(s32[1]{0:T(128)} %bitcast.me_ref, s32[2]{0:T(128)} %counts.7, s32[2,64]{1,0:T(2,128)} %rows.7, s32[2,64]{1,0:T(2,128)} %cols.7, bf16[2,64,4096]{2,1,0:T(8,128)(2,1)} %bitcast.5, ...), custom_call_target="tpu_custom_call" | custom-call | flops 4000000000 | bytes 1048576 | tf_op jit(solution)/shard_map/spread_one/pallas_call | solution.py:111
  3.3 2.2 %collective-permute-start.9 = (bf16[2,64,1024]{2,1,0:T(8,128)(2,1)}, bf16[2,64,1024]{2,1,0:T(8,128)(2,1)S(1)}, u32[]{:S(2)}, u32[]{:S(2)}) collective-permute-start(bf16[2,64,1024]{2,1,0:T(8,128)(2,1)} %get-tuple-element.45), channel_id=1, source_target_pairs={{0,1},{1,2},{2,3},{3,0},{4,5},{5,6},{6,7},{7,4},{8,9},{9,10},{10,1... | collective-permute-start | bytes 786440 | tf_op jit(solution)/shard_map/ppermute | solution.py:50
  5.5 2.6 %collective-permute-start.10 = (bf16[2,64,1024]{2,1,0:T(8,128)(2,1)}, bf16[2,64,1024]{2,1,0:T(8,128)(2,1)S(1)}, u32[]{:S(2)}, u32[]{:S(2)}) collective-permute-start(bf16[2,64,1024]{2,1,0:T(8,128)(2,1)} %get-tuple-element.46), channel_id=1, source_target_pairs={{0,2},{1,3},{2,0},{3,1},{4,6},{5,7},{6,4},{7,5},{8,10},{9,11},{10,... | collective-permute-start | bytes 786440 | tf_op jit(solution)/shard_map/ppermute | solution.py:50
  8.1 1.1 collective-permute-start.11
  9.2 4.4 %spread_one.2 = (bf16[2,64,1024]{2,1,0:T(8,128)(2,1)}, bf16[2,64,1024]{2,1,0:T(8,128)(2,1)}, bf16[2,64,1024]{2,1,0:T(8,128)(2,1)}, bf16[2,64,1024]{2,1,0:T(8,128)(2,1)}) custom-call(s32[1]{0:T(128)} %bitcast.me_ref, s32[2]{0:T(128)} %counts.7, s32[2,64]{1,0:T(2,128)} %rows.7, s32[2,64]{1,0:T(2,128)} %cols.7, bf16[2,64,4096]{2,1,0:T(8,128)(2,1)} %bitcast.6, ...), custom_call_target="tpu_custom_call" | custom-call | flops 4000000000 | bytes 1048576 | tf_op jit(solution)/shard_map/spread_one/pallas_call | solution.py:111
  15.1 1.6 %collective-permute-start.2 = (bf16[2,64,1024]{2,1,0:T(8,128)(2,1)}, bf16[2,64,1024]{2,1,0:T(8,128)(2,1)S(1)}, u32[]{:S(2)}, u32[]{:S(2)}) collective-permute-start(bf16[2,64,1024]{2,1,0:T(8,128)(2,1)} %get-tuple-element.34), channel_id=1, source_target_pairs={{0,3},{1,0},{2,1},{3,2},{4,7},{5,4},{6,5},{7,6},{8,11},{9,8},{10,9... | collective-permute-start | bytes 786440 | tf_op jit(solution)/shard_map/ppermute | solution.py:50
  16.7 2.7 %collective-permute-done.10.refs_2_ = bf16[2,64,1024]{2,1,0:T(8,128)(2,1)S(1)} collective-permute-done((bf16[2,64,1024]{2,1,0:T(8,128)(2,1)}, bf16[2,64,1024]{2,1,0:T(8,128)(2,1)S(1)}, u32[]{:S(2)}, u32[]{:S(2)}) %collective-permute-start.10) | collective-permute-done | bytes 262176 | tf_op jit(solution)/shard_map/ppermute | solution.py:50
  19.7 1.8 %collective-permute-start.12 = (bf16[64,1024]{1,0:T(8,128)(2,1)S(1)}, bf16[64,1024]{1,0:T(8,128)(2,1)S(1)}, u32[]{:S(2)}, u32[]{:S(2)}) collective-permute-start(bf16[64,1024]{1,0:T(8,128)(2,1)S(1)} %get-tuple-element.49), channel_id=1, source_target_pairs={{0,1},{1,2},{2,3},{3,0},{4,5},{5,6},{6,7},{7,4},{8,9},{9,10},{10,1... | collective-permute-start | bytes 393224 | tf_op jit(solution)/shard_map/ppermute | solution.py:50
  21.5 2.9 %collective-permute-start.13 = (bf16[64,1024]{1,0:T(8,128)(2,1)S(1)}, bf16[64,1024]{1,0:T(8,128)(2,1)S(1)}, u32[]{:S(2)}, u32[]{:S(2)}) collective-permute-start(bf16[64,1024]{1,0:T(8,128)(2,1)S(1)} %get-tuple-element.50), channel_id=1, source_target_pairs={{0,2},{1,3},{2,0},{3,1},{4,6},{5,7},{6,4},{7,5},{8,10},{9,11},{10,... | collective-permute-start | bytes 393224 | tf_op jit(solution)/shard_map/ppermute | solution.py:50
  24.4 3.3 %collective-permute-done.refs_1_ = bf16[2,64,1024]{2,1,0:T(8,128)(2,1)S(1)} collective-permute-done((bf16[2,64,1024]{2,1,0:T(8,128)(2,1)}, bf16[2,64,1024]{2,1,0:T(8,128)(2,1)S(1)}, u32[]{:S(2)}, u32[]{:S(2)}) %collective-permute-start) | collective-permute-done | bytes 262176 | tf_op jit(solution)/shard_map/ppermute | solution.py:50
  27.7 2.9 %collective-permute-done.1.refs_2_ = bf16[2,64,1024]{2,1,0:T(8,128)(2,1)S(1)} collective-permute-done((bf16[2,64,1024]{2,1,0:T(8,128)(2,1)}, bf16[2,64,1024]{2,1,0:T(8,128)(2,1)S(1)}, u32[]{:S(2)}, u32[]{:S(2)}) %collective-permute-start.1) | collective-permute-done | bytes 262176 | tf_op jit(solution)/shard_map/ppermute | solution.py:50
  32.0 1.7 %collective-permute-start.3 = (bf16[64,1024]{1,0:T(8,128)(2,1)S(1)}, bf16[64,1024]{1,0:T(8,128)(2,1)S(1)}, u32[]{:S(2)}, u32[]{:S(2)}) collective-permute-start(bf16[64,1024]{1,0:T(8,128)(2,1)S(1)} %get-tuple-element.36), channel_id=1, source_target_pairs={{0,1},{1,2},{2,3},{3,0},{4,5},{5,6},{6,7},{7,4},{8,9},{9,10},{10,1... | collective-permute-start | bytes 393224 | tf_op jit(solution)/shard_map/ppermute | solution.py:50
  33.7 2.9 %collective-permute-start.4 = (bf16[64,1024]{1,0:T(8,128)(2,1)S(1)}, bf16[64,1024]{1,0:T(8,128)(2,1)S(1)}, u32[]{:S(2)}, u32[]{:S(2)}) collective-permute-start(bf16[64,1024]{1,0:T(8,128)(2,1)S(1)} %get-tuple-element.37), channel_id=1, source_target_pairs={{0,2},{1,3},{2,0},{3,1},{4,6},{5,7},{6,4},{7,5},{8,10},{9,11},{10,... | collective-permute-start | bytes 393224 | tf_op jit(solution)/shard_map/ppermute | solution.py:50
  36.7 1.0 spread_two.3
  37.7 1.5 %collective-permute-start.15 = (bf16[64,1024]{1,0:T(8,128)(2,1)S(1)}, bf16[64,1024]{1,0:T(8,128)(2,1)S(1)}, u32[]{:S(2)}, u32[]{:S(2)}) collective-permute-start(bf16[64,1024]{1,0:T(8,128)(2,1)S(1)} %get-tuple-element.53), channel_id=1, source_target_pairs={{0,1},{1,2},{2,3},{3,0},{4,5},{5,6},{6,7},{7,4},{8,9},{9,10},{10,1... | collective-permute-start | bytes 393224 | tf_op jit(solution)/shard_map/ppermute | solution.py:50
  39.3 1.8 %collective-permute-start.16 = (bf16[64,1024]{1,0:T(8,128)(2,1)S(1)}, bf16[64,1024]{1,0:T(8,128)(2,1)S(1)}, u32[]{:S(2)}, u32[]{:S(2)}) collective-permute-start(bf16[64,1024]{1,0:T(8,128)(2,1)S(1)} %get-tuple-element.54), channel_id=1, source_target_pairs={{0,2},{1,3},{2,0},{3,1},{4,6},{5,7},{6,4},{7,5},{8,10},{9,11},{10,... | collective-permute-start | bytes 393224 | tf_op jit(solution)/shard_map/ppermute | solution.py:50
  41.8 2.2 %spread_two.2 = (bf16[64,1024]{1,0:T(8,128)(2,1)S(1)}, bf16[64,1024]{1,0:T(8,128)(2,1)S(1)}, bf16[64,1024]{1,0:T(8,128)(2,1)S(1)}, bf16[64,1024]{1,0:T(8,128)(2,1)S(1)}) custom-call(s32[1]{0:T(128)} %bitcast.me_ref, s32[2]{0:T(128)S(1)} %copy-done.9, s32[2,64]{1,0:T(2,128)S(1)} %copy-done.7, s32[2,64]{1,0:T(2,128)S(1)} %copy-done.8, ...), custom_call_target="tpu_custom_call" | custom-call | flops 3000000000 | bytes 1048576 | tf_op jit(solution)/shard_map/spread_two/pallas_call | solution.py:157
  44.8 1.2 collective-permute-start.7
  46.0 1.3 collective-permute-start.8
  48.1 5.0 %collective-permute-done.6.refs_1_ = bf16[64,1024]{1,0:T(8,128)(2,1)S(1)} collective-permute-done((bf16[64,1024]{1,0:T(8,128)(2,1)S(1)}, bf16[64,1024]{1,0:T(8,128)(2,1)S(1)}, u32[]{:S(2)}, u32[]{:S(2)}) %collective-permute-start.6) | collective-permute-done | bytes 131104 | tf_op jit(solution)/shard_map/ppermute | solution.py:50
  53.7 46.2 %all_to_all.10.h_ref = bf16[64,32,256]{2,1,0:T(8,128)(2,1)S(1)} all-to-all(bf16[64,32,256]{2,1,0:T(8,128)(2,1)S(1)} %mix_two.3), channel_id=1, replica_groups=mesh['snap'=64,'feat'=4] {'snap'}, dimensions={0} | all-to-all | bytes 2097152 | tf_op jit(solution)/shard_map/all_to_all | solution.py:380
  99.9 8.9 %attend.1 = bf16[4,64,16,128]{3,2,1,0:T(8,128)(2,1)S(1)} custom-call(bf16[64,32,256]{2,1,0:T(8,128)(2,1)S(1)} %all_to_all.10.h_ref, bf16[256,256]{1,0:T(8,128)(2,1)S(1)} %copy-done, bf16[256,256]{1,0:T(8,128)(2,1)S(1)} %copy-done.1, bf16[256,256]{1,0:T(8,128)(2,1)S(1)} %copy-done.2, bf16[256,256]{1,0:T(8,128)(2,1)S(1)} %copy-done.3), custom_call_target="tpu_custom_call" | custom-call | tf_op jit(solution)/shard_map/attend/pallas_call | solution.py:319
  108.9 39.5 %all_to_all.11.in_ref = bf16[256,16,128]{2,1,0:T(8,128)(2,1)S(1)} all-to-all(bf16[256,16,128]{2,1,0:T(8,128)(2,1)S(1)} %bitcast.4), channel_id=1, replica_groups=mesh['snap'=64,'feat'=4] {'feat','snap'}, dimensions={0} | all-to-all | bytes 2097152 | tf_op jit(solution)/shard_map/all_to_all | solution.py:382
  148.4 1.8 %place.1 = bf16[2,64,4096]{2,1,0:T(8,128)(2,1)} custom-call(bf16[256,16,128]{2,1,0:T(8,128)(2,1)S(1)} %all_to_all.11.in_ref), custom_call_target="tpu_custom_call" | custom-call | tf_op jit(solution)/shard_map/place/pallas_call | solution.py:344
  (48 shorter events, 6.1 us)
Async XLA Ops:
  3.3 11.8 %collective-permute-start.9 = (bf16[2,64,1024]{2,1,0:T(8,128)(2,1)}, bf16[2,64,1024]{2,1,0:T(8,128)(2,1)S(1)}, u32[]{:S(2)}, u32[]{:S(2)}) collective-permute-start(bf16[2,64,1024]{2,1,0:T(8,128)(2,1)} %get-tuple-element.45), channel_id=1, source_target_pairs={{0,1},{1,2},{2,3},{3,0},{4,5},{5,6},{6,7},{7,4},{8,9},{9,10},{10,1... | collective-permute-start | bytes 786440 | tf_op jit(solution)/shard_map/ppermute | solution.py:50
  5.5 13.8 %collective-permute-start.10 = (bf16[2,64,1024]{2,1,0:T(8,128)(2,1)}, bf16[2,64,1024]{2,1,0:T(8,128)(2,1)S(1)}, u32[]{:S(2)}, u32[]{:S(2)}) collective-permute-start(bf16[2,64,1024]{2,1,0:T(8,128)(2,1)} %get-tuple-element.46), channel_id=1, source_target_pairs={{0,2},{1,3},{2,0},{3,1},{4,6},{5,7},{6,4},{7,5},{8,10},{9,11},{10,... | collective-permute-start | bytes 786440 | tf_op jit(solution)/shard_map/ppermute | solution.py:50
  8.1 11.2 %collective-permute-start.11 = (bf16[2,64,1024]{2,1,0:T(8,128)(2,1)}, bf16[2,64,1024]{2,1,0:T(8,128)(2,1)S(1)}, u32[]{:S(2)}, u32[]{:S(2)}) collective-permute-start(bf16[2,64,1024]{2,1,0:T(8,128)(2,1)} %get-tuple-element.47), channel_id=1, source_target_pairs={{0,3},{1,0},{2,1},{3,2},{4,7},{5,4},{6,5},{7,6},{8,11},{9,8},{10,9... | collective-permute-start | bytes 786440 | tf_op jit(solution)/shard_map/ppermute | solution.py:50
  13.6 23.0 %copy-start.4 = (bf16[2,64,128,128]{3,2,1,0:T(8,128)(2,1)S(1)}, bf16[2,64,128,128]{3,2,1,0:T(8,128)(2,1)}, u32[]{:S(2)}) copy-start(bf16[2,64,128,128]{3,2,1,0:T(8,128)(2,1)} %refs_4_.7) | copy-start | bytes 12582916
  13.6 23.0 %copy-start.7 = (s32[2,64]{1,0:T(2,128)S(1)}, s32[2,64]{1,0:T(2,128)}, u32[]{:S(2)}) copy-start(s32[2,64]{1,0:T(2,128)} %rows.7) | copy-start | bytes 1540
  13.7 14.0 %collective-permute-start = (bf16[2,64,1024]{2,1,0:T(8,128)(2,1)}, bf16[2,64,1024]{2,1,0:T(8,128)(2,1)S(1)}, u32[]{:S(2)}, u32[]{:S(2)}) collective-permute-start(bf16[2,64,1024]{2,1,0:T(8,128)(2,1)} %get-tuple-element.32), channel_id=1, source_target_pairs={{0,1},{1,2},{2,3},{3,0},{4,5},{5,6},{6,7},{7,4},{8,9},{9,10},{10,1... | collective-permute-start | bytes 786440 | tf_op jit(solution)/shard_map/ppermute | solution.py:50
  14.2 16.5 %collective-permute-start.1 = (bf16[2,64,1024]{2,1,0:T(8,128)(2,1)}, bf16[2,64,1024]{2,1,0:T(8,128)(2,1)S(1)}, u32[]{:S(2)}, u32[]{:S(2)}) collective-permute-start(bf16[2,64,1024]{2,1,0:T(8,128)(2,1)} %get-tuple-element.33), channel_id=1, source_target_pairs={{0,2},{1,3},{2,0},{3,1},{4,6},{5,7},{6,4},{7,5},{8,10},{9,11},{10,... | collective-permute-start | bytes 786440 | tf_op jit(solution)/shard_map/ppermute | solution.py:50
  15.1 15.5 %collective-permute-start.2 = (bf16[2,64,1024]{2,1,0:T(8,128)(2,1)}, bf16[2,64,1024]{2,1,0:T(8,128)(2,1)S(1)}, u32[]{:S(2)}, u32[]{:S(2)}) collective-permute-start(bf16[2,64,1024]{2,1,0:T(8,128)(2,1)} %get-tuple-element.34), channel_id=1, source_target_pairs={{0,3},{1,0},{2,1},{3,2},{4,7},{5,4},{6,5},{7,6},{8,11},{9,8},{10,9... | collective-permute-start | bytes 786440 | tf_op jit(solution)/shard_map/ppermute | solution.py:50
  19.7 16.9 %collective-permute-start.12 = (bf16[64,1024]{1,0:T(8,128)(2,1)S(1)}, bf16[64,1024]{1,0:T(8,128)(2,1)S(1)}, u32[]{:S(2)}, u32[]{:S(2)}) collective-permute-start(bf16[64,1024]{1,0:T(8,128)(2,1)S(1)} %get-tuple-element.49), channel_id=1, source_target_pairs={{0,1},{1,2},{2,3},{3,0},{4,5},{5,6},{6,7},{7,4},{8,9},{9,10},{10,1... | collective-permute-start | bytes 393224 | tf_op jit(solution)/shard_map/ppermute | solution.py:50
  21.5 15.1 %collective-permute-start.13 = (bf16[64,1024]{1,0:T(8,128)(2,1)S(1)}, bf16[64,1024]{1,0:T(8,128)(2,1)S(1)}, u32[]{:S(2)}, u32[]{:S(2)}) collective-permute-start(bf16[64,1024]{1,0:T(8,128)(2,1)S(1)} %get-tuple-element.50), channel_id=1, source_target_pairs={{0,2},{1,3},{2,0},{3,1},{4,6},{5,7},{6,4},{7,5},{8,10},{9,11},{10,... | collective-permute-start | bytes 393224 | tf_op jit(solution)/shard_map/ppermute | solution.py:50
  27.7 8.9 %collective-permute-start.14 = (bf16[64,1024]{1,0:T(8,128)(2,1)S(1)}, bf16[64,1024]{1,0:T(8,128)(2,1)S(1)}, u32[]{:S(2)}, u32[]{:S(2)}) collective-permute-start(bf16[64,1024]{1,0:T(8,128)(2,1)S(1)} %get-tuple-element.51), channel_id=1, source_target_pairs={{0,3},{1,0},{2,1},{3,2},{4,7},{5,4},{6,5},{7,6},{8,11},{9,8},{10,9... | collective-permute-start | bytes 393224 | tf_op jit(solution)/shard_map/ppermute | solution.py:50
  32.0 9.1 %collective-permute-start.3 = (bf16[64,1024]{1,0:T(8,128)(2,1)S(1)}, bf16[64,1024]{1,0:T(8,128)(2,1)S(1)}, u32[]{:S(2)}, u32[]{:S(2)}) collective-permute-start(bf16[64,1024]{1,0:T(8,128)(2,1)S(1)} %get-tuple-element.36), channel_id=1, source_target_pairs={{0,1},{1,2},{2,3},{3,0},{4,5},{5,6},{6,7},{7,4},{8,9},{9,10},{10,1... | collective-permute-start | bytes 393224 | tf_op jit(solution)/shard_map/ppermute | solution.py:50
  33.7 8.1 %collective-permute-start.4 = (bf16[64,1024]{1,0:T(8,128)(2,1)S(1)}, bf16[64,1024]{1,0:T(8,128)(2,1)S(1)}, u32[]{:S(2)}, u32[]{:S(2)}) collective-permute-start(bf16[64,1024]{1,0:T(8,128)(2,1)S(1)} %get-tuple-element.37), channel_id=1, source_target_pairs={{0,2},{1,3},{2,0},{3,1},{4,6},{5,7},{6,4},{7,5},{8,10},{9,11},{10,... | collective-permute-start | bytes 393224 | tf_op jit(solution)/shard_map/ppermute | solution.py:50
  36.6 5.1 %collective-permute-start.5 = (bf16[64,1024]{1,0:T(8,128)(2,1)S(1)}, bf16[64,1024]{1,0:T(8,128)(2,1)S(1)}, u32[]{:S(2)}, u32[]{:S(2)}) collective-permute-start(bf16[64,1024]{1,0:T(8,128)(2,1)S(1)} %get-tuple-element.38), channel_id=1, source_target_pairs={{0,3},{1,0},{2,1},{3,2},{4,7},{5,4},{6,5},{7,6},{8,11},{9,8},{10,9... | collective-permute-start | bytes 393224 | tf_op jit(solution)/shard_map/ppermute | solution.py:50
  37.7 8.3 %collective-permute-start.15 = (bf16[64,1024]{1,0:T(8,128)(2,1)S(1)}, bf16[64,1024]{1,0:T(8,128)(2,1)S(1)}, u32[]{:S(2)}, u32[]{:S(2)}) collective-permute-start(bf16[64,1024]{1,0:T(8,128)(2,1)S(1)} %get-tuple-element.53), channel_id=1, source_target_pairs={{0,1},{1,2},{2,3},{3,0},{4,5},{5,6},{6,7},{7,4},{8,9},{9,10},{10,1... | collective-permute-start | bytes 393224 | tf_op jit(solution)/shard_map/ppermute | solution.py:50
  39.3 8.3 %collective-permute-start.16 = (bf16[64,1024]{1,0:T(8,128)(2,1)S(1)}, bf16[64,1024]{1,0:T(8,128)(2,1)S(1)}, u32[]{:S(2)}, u32[]{:S(2)}) collective-permute-start(bf16[64,1024]{1,0:T(8,128)(2,1)S(1)} %get-tuple-element.54), channel_id=1, source_target_pairs={{0,2},{1,3},{2,0},{3,1},{4,6},{5,7},{6,4},{7,5},{8,10},{9,11},{10,... | collective-permute-start | bytes 393224 | tf_op jit(solution)/shard_map/ppermute | solution.py:50
  41.0 6.6 %collective-permute-start.17 = (bf16[64,1024]{1,0:T(8,128)(2,1)S(1)}, bf16[64,1024]{1,0:T(8,128)(2,1)S(1)}, u32[]{:S(2)}, u32[]{:S(2)}) collective-permute-start(bf16[64,1024]{1,0:T(8,128)(2,1)S(1)} %get-tuple-element.55), channel_id=1, source_target_pairs={{0,3},{1,0},{2,1},{3,2},{4,7},{5,4},{6,5},{7,6},{8,11},{9,8},{10,9... | collective-permute-start | bytes 393224 | tf_op jit(solution)/shard_map/ppermute | solution.py:50
  44.0 9.1 %collective-permute-start.6 = (bf16[64,1024]{1,0:T(8,128)(2,1)S(1)}, bf16[64,1024]{1,0:T(8,128)(2,1)S(1)}, u32[]{:S(2)}, u32[]{:S(2)}) collective-permute-start(bf16[64,1024]{1,0:T(8,128)(2,1)S(1)} %get-tuple-element.40), channel_id=1, source_target_pairs={{0,1},{1,2},{2,3},{3,0},{4,5},{5,6},{6,7},{7,4},{8,9},{9,10},{10,1... | collective-permute-start | bytes 393224 | tf_op jit(solution)/shard_map/ppermute | solution.py:50
  44.8 8.3 %collective-permute-start.7 = (bf16[64,1024]{1,0:T(8,128)(2,1)S(1)}, bf16[64,1024]{1,0:T(8,128)(2,1)S(1)}, u32[]{:S(2)}, u32[]{:S(2)}) collective-permute-start(bf16[64,1024]{1,0:T(8,128)(2,1)S(1)} %get-tuple-element.41), channel_id=1, source_target_pairs={{0,2},{1,3},{2,0},{3,1},{4,6},{5,7},{6,4},{7,5},{8,10},{9,11},{10,... | collective-permute-start | bytes 393224 | tf_op jit(solution)/shard_map/ppermute | solution.py:50
  46.0 7.3 %collective-permute-start.8 = (bf16[64,1024]{1,0:T(8,128)(2,1)S(1)}, bf16[64,1024]{1,0:T(8,128)(2,1)S(1)}, u32[]{:S(2)}, u32[]{:S(2)}) collective-permute-start(bf16[64,1024]{1,0:T(8,128)(2,1)S(1)} %get-tuple-element.42), channel_id=1, source_target_pairs={{0,3},{1,0},{2,1},{3,2},{4,7},{5,4},{6,5},{7,6},{8,11},{9,8},{10,9... | collective-permute-start | bytes 393224 | tf_op jit(solution)/shard_map/ppermute | solution.py:50
  47.6 52.3 %copy-start = (bf16[256,256]{1,0:T(8,128)(2,1)S(1)}, bf16[256,256]{1,0:T(8,128)(2,1)}, u32[]{:S(2)}) copy-start(bf16[256,256]{1,0:T(8,128)(2,1)} %wq_ref.1) | copy-start | bytes 393220
  47.6 52.3 %copy-start.1 = (bf16[256,256]{1,0:T(8,128)(2,1)S(1)}, bf16[256,256]{1,0:T(8,128)(2,1)}, u32[]{:S(2)}) copy-start(bf16[256,256]{1,0:T(8,128)(2,1)} %wk_ref.1) | copy-start | bytes 393220
  47.6 52.3 %copy-start.2 = (bf16[256,256]{1,0:T(8,128)(2,1)S(1)}, bf16[256,256]{1,0:T(8,128)(2,1)}, u32[]{:S(2)}) copy-start(bf16[256,256]{1,0:T(8,128)(2,1)} %wv_ref.1) | copy-start | bytes 393220
  47.6 52.3 %copy-start.3 = (bf16[256,256]{1,0:T(8,128)(2,1)S(1)}, bf16[256,256]{1,0:T(8,128)(2,1)}, u32[]{:S(2)}) copy-start(bf16[256,256]{1,0:T(8,128)(2,1)} %wo_ref.1) | copy-start | bytes 393220
  (6 other events, 75.3 us)

commit v3 on v2

--- a/solution.py
+++ b/solution.py
@@ -23,6 +23,7 @@
 GROUP = 8
 
 masked_score = -1e30
+LOG2_E = 1.4426950408889634
 f32 = jnp.float32
 bf16 = jnp.bfloat16
 NT = (((1,), (1,)), ((), ()))
@@ -120,13 +121,13 @@
             pltpu.SemaphoreType.DMA,
             pltpu.SemaphoreType.DMA((GROUPS,)),
         ],
-        compiler_params=params(SPREAD_MIB),
+        compiler_params=params(SPREAD_MIB[t]),
         cost_estimate=cost(4),
         name="spread_one",
     )(me, counts, rows, cols, x, tiles)
 
 
-SPREAD_MIB = 56
+SPREAD_MIB = (56, 52)
 
 
 def spread_two_kernel(t, me_ref, counts, rows, cols, *refs):
@@ -259,7 +260,7 @@
     causal = lax.broadcasted_iota(jnp.int32, (SNAPS, SNAPS), 0) <= lax.broadcasted_iota(
         jnp.int32, (SNAPS, SNAPS), 1
     )
-    scale = HEAD_DIM**-0.5
+    scale = HEAD_DIM**-0.5 * LOG2_E
 
     def vertex(v, _):
         at = pl.ds(pl.multiple_of(v * SNAPS, SNAPS), SNAPS)
@@ -280,7 +281,7 @@
                 head = slice((2 * pair + k) * HEAD_DIM, (2 * pair + k + 1) * HEAD_DIM)
                 s = jnp.where(causal, scores[:, k * SNAPS : (k + 1) * SNAPS], masked_score)
                 top = jnp.max(s, axis=0, keepdims=True)
-                lifted = jnp.exp((s - top) * scale)
+                lifted = jnp.exp2((s - top) * scale)
                 total = jnp.sum(lifted, axis=0, keepdims=True)
                 weights = (lifted * (1.0 / total)).astype(bf16)
                 ct[head, at] = jnp.dot(
@@ -288,7 +289,7 @@
                 ).astype(bf16)
         return 0
 
-    lax.fori_loop(0, V_S, vertex, 0, unroll=4)
+    lax.fori_loop(0, V_S, vertex, 0, unroll=8)
     for v in range(V_S):
         mixed = jnp.dot(
             ct[:, v * SNAPS : (v + 1) * SNAPS].T, wo_ref[...], preferred_element_type=f32
@@ -334,7 +335,7 @@
 
 
 def place_kernel(in_ref, out_ref):
-    for g in range(8):
+    for g in range(16):
         block = in_ref[g * 8 : (g + 1) * 8].reshape(128, 128).T
         out_ref[0, :, g * 128 : (g + 1) * 128] = block[:F_W]
         out_ref[1, :, g * 128 : (g + 1) * 128] = block[F_W:]
@@ -343,9 +344,9 @@
 def place(pieces):
     return pl.pallas_call(
         place_kernel,
-        grid=(4,),
-        in_specs=[pl.BlockSpec((S_DEV, V_S, 2 * F_W), lambda g: (g, 0, 0))],
-        out_specs=pl.BlockSpec((2, F_W, V_F), lambda g: (0, 0, g)),
+        grid=(2,),
+        in_specs=[pl.BlockSpec((S_DEV * 2, V_S, 2 * F_W), lambda g: (g, 0, 0))],
+        out_specs=pl.BlockSpec((2, F_W, V_F * 2), lambda g: (0, 0, g)),
         out_shape=jax.ShapeDtypeStruct((2, F_W, VERT), bf16),
         compiler_params=params(24),
         name="place",

time: 149 us -> 146 us (0.980)
  Pallas kernels: 23.3 us -> 21.2 us
  transfers between devices with their start and end apart: 18 -> 18, of which waited for: 6 -> 7; matrix products, arithmetic and copies ran while one was open for 0% -> 0% of each run, Pallas kernels for 6% -> 6%
where the time goes in v3:
time: 146 us
  blocking collectives  84.5 us (58%)
  starting transfers between devices  26.9 us (18%)
  Pallas kernels  21.2 us (15%)
  waiting for transfers between devices  13.7 us (9%)
    all_to_all x1, blocking collectives, on_device(): lax.all_to_all(hidden[0], 'snap', split_axis=0, concat_axis=0, tiled=True)  45 us
    all_to_all x1, blocking collectives, on_device(): lax.all_to_all(evolved.reshape(F_DEV * S_DEV, V_S, 2 * F_W), ('feat', 'sn...  39.5 us
    ppermute x18, starting transfers between devices, turn(): lax.ppermute(blocks[k], 'feat', [(i, (i + k) % F_DEV) for i in range(F_DE...  26.9 us
    ppermute x18, waiting for transfers between devices, turn(): lax.ppermute(blocks[k], 'feat', [(i, (i + k) % F_DEV) for i in range(F_DE...  13.7 us
    pallas_call x1, Pallas kernels, attend(): pl.pallas_call(attend_kernel, out_shape=jax.ShapeDtypeStruct((F_DEV, S_DE...  7.86 us
    pallas_call x2, Pallas kernels, spread_one(): pl.pallas_call(functools.partial(spread_one_kernel, t), in_specs=[SMEM] *...  7 us
    pallas_call x2, Pallas kernels, spread_two(): pl.pallas_call(functools.partial(spread_two_kernel, t), grid=(1,), in_spe...  3.52 us
  transfers between devices with their start and end apart: 18, of which 7 were waited for; matrix products, arithmetic and copies ran while one was open for 0% of the time, Pallas kernels for 6%

profile of v3, /device:TPU:1, one launch (start us, length us, event | category | flops | bytes accessed | tf_op | source)
XLA Modules:
  0.0 146.5 jit_solution(3552173737485743402)
XLA Ops:
  0.0 3.4 %spread_one.3 = (bf16[2,64,1024]{2,1,0:T(8,128)(2,1)}, bf16[2,64,1024]{2,1,0:T(8,128)(2,1)}, bf16[2,64,1024]{2,1,0:T(8,128)(2,1)}, bf16[2,64,1024]{2,1,0:T(8,128)(2,1)}) custom-call(s32[1]{0:T(128)} %bitcast.me_ref, s32[2]{0:T(128)} %counts.7, s32[2,64]{1,0:T(2,128)} %rows.7, s32[2,64]{1,0:T(2,128)} %cols.7, bf16[2,64,4096]{2,1,0:T(8,128)(2,1)} %bitcast.5, ...), custom_call_target="tpu_custom_call" | custom-call | flops 4000000000 | bytes 1048576 | tf_op jit(solution)/shard_map/spread_one/pallas_call | solution.py:112
  3.4 2.2 %collective-permute-start.9 = (bf16[2,64,1024]{2,1,0:T(8,128)(2,1)}, bf16[2,64,1024]{2,1,0:T(8,128)(2,1)S(1)}, u32[]{:S(2)}, u32[]{:S(2)}) collective-permute-start(bf16[2,64,1024]{2,1,0:T(8,128)(2,1)} %get-tuple-element.45), channel_id=1, source_target_pairs={{0,1},{1,2},{2,3},{3,0},{4,5},{5,6},{6,7},{7,4},{8,9},{9,10},{10,1... | collective-permute-start | bytes 786440 | tf_op jit(solution)/shard_map/ppermute | solution.py:51
  5.6 2.6 %collective-permute-start.10 = (bf16[2,64,1024]{2,1,0:T(8,128)(2,1)}, bf16[2,64,1024]{2,1,0:T(8,128)(2,1)S(1)}, u32[]{:S(2)}, u32[]{:S(2)}) collective-permute-start(bf16[2,64,1024]{2,1,0:T(8,128)(2,1)} %get-tuple-element.46), channel_id=1, source_target_pairs={{0,2},{1,3},{2,0},{3,1},{4,6},{5,7},{6,4},{7,5},{8,10},{9,11},{10,... | collective-permute-start | bytes 786440 | tf_op jit(solution)/shard_map/ppermute | solution.py:51
  8.2 1.1 collective-permute-start.11
  9.3 3.6 %spread_one.2 = (bf16[2,64,1024]{2,1,0:T(8,128)(2,1)S(1)}, bf16[2,64,1024]{2,1,0:T(8,128)(2,1)S(1)}, bf16[2,64,1024]{2,1,0:T(8,128)(2,1)S(1)}, bf16[2,64,1024]{2,1,0:T(8,128)(2,1)S(1)}) custom-call(s32[1]{0:T(128)} %bitcast.me_ref, s32[2]{0:T(128)S(1)} %copy-done.9, s32[2,64]{1,0:T(2,128)S(1)} %copy-done.7, s32[2,64]{1,0:T(2,128)S(1)} %copy-done.8, ...), custom_call_target="tpu_custom_call" | custom-call | flops 4000000000 | bytes 1048576 | tf_op jit(solution)/shard_map/spread_one/pallas_call | solution.py:112
  14.2 1.7 %collective-permute-start.2 = (bf16[2,64,1024]{2,1,0:T(8,128)(2,1)S(1)}, bf16[2,64,1024]{2,1,0:T(8,128)(2,1)S(1)}, u32[]{:S(2)}, u32[]{:S(2)}) collective-permute-start(bf16[2,64,1024]{2,1,0:T(8,128)(2,1)S(1)} %get-tuple-element.34), channel_id=1, source_target_pairs={{0,3},{1,0},{2,1},{3,2},{4,7},{5,4},{6,5},{7,6},{8,11},{9,8},{10,9... | collective-permute-start | bytes 786440 | tf_op jit(solution)/shard_map/ppermute | solution.py:51
  15.9 3.9 %collective-permute-done.10.refs_2_ = bf16[2,64,1024]{2,1,0:T(8,128)(2,1)S(1)} collective-permute-done((bf16[2,64,1024]{2,1,0:T(8,128)(2,1)}, bf16[2,64,1024]{2,1,0:T(8,128)(2,1)S(1)}, u32[]{:S(2)}, u32[]{:S(2)}) %collective-permute-start.10) | collective-permute-done | bytes 262176 | tf_op jit(solution)/shard_map/ppermute | solution.py:51
  21.5 4.7 %collective-permute-start.13 = (bf16[64,1024]{1,0:T(8,128)(2,1)S(1)}, bf16[64,1024]{1,0:T(8,128)(2,1)S(1)}, u32[]{:S(2)}, u32[]{:S(2)}) collective-permute-start(bf16[64,1024]{1,0:T(8,128)(2,1)S(1)} %get-tuple-element.50), channel_id=1, source_target_pairs={{0,2},{1,3},{2,0},{3,1},{4,6},{5,7},{6,4},{7,5},{8,10},{9,11},{10,... | collective-permute-start | bytes 393224 | tf_op jit(solution)/shard_map/ppermute | solution.py:51
  26.2 1.4 collective-permute-done.refs_1_
  27.6 3.5 %collective-permute-done.1.refs_2_ = bf16[2,64,1024]{2,1,0:T(8,128)(2,1)S(1)} collective-permute-done((bf16[2,64,1024]{2,1,0:T(8,128)(2,1)S(1)}, bf16[2,64,1024]{2,1,0:T(8,128)(2,1)S(1)}, u32[]{:S(2)}, u32[]{:S(2)}) %collective-permute-start.1) | collective-permute-done | bytes 262176 | tf_op jit(solution)/shard_map/ppermute | solution.py:51
  31.7 1.0 collective-permute-start.3
  32.7 3.8 %collective-permute-start.4 = (bf16[64,1024]{1,0:T(8,128)(2,1)S(1)}, bf16[64,1024]{1,0:T(8,128)(2,1)S(1)}, u32[]{:S(2)}, u32[]{:S(2)}) collective-permute-start(bf16[64,1024]{1,0:T(8,128)(2,1)S(1)} %get-tuple-element.37), channel_id=1, source_target_pairs={{0,2},{1,3},{2,0},{3,1},{4,6},{5,7},{6,4},{7,5},{8,10},{9,11},{10,... | collective-permute-start | bytes 393224 | tf_op jit(solution)/shard_map/ppermute | solution.py:51
  36.7 1.0 spread_two.3
  37.8 1.4 collective-permute-start.15
  39.1 2.3 %collective-permute-start.16 = (bf16[64,1024]{1,0:T(8,128)(2,1)S(1)}, bf16[64,1024]{1,0:T(8,128)(2,1)S(1)}, u32[]{:S(2)}, u32[]{:S(2)}) collective-permute-start(bf16[64,1024]{1,0:T(8,128)(2,1)S(1)} %get-tuple-element.54), channel_id=1, source_target_pairs={{0,2},{1,3},{2,0},{3,1},{4,6},{5,7},{6,4},{7,5},{8,10},{9,11},{10,... | collective-permute-start | bytes 393224 | tf_op jit(solution)/shard_map/ppermute | solution.py:51
  41.9 2.5 %spread_two.2 = (bf16[64,1024]{1,0:T(8,128)(2,1)S(1)}, bf16[64,1024]{1,0:T(8,128)(2,1)S(1)}, bf16[64,1024]{1,0:T(8,128)(2,1)S(1)}, bf16[64,1024]{1,0:T(8,128)(2,1)S(1)}) custom-call(s32[1]{0:T(128)} %bitcast.me_ref, s32[2]{0:T(128)S(1)} %copy-done.9, s32[2,64]{1,0:T(2,128)S(1)} %copy-done.7, s32[2,64]{1,0:T(2,128)S(1)} %copy-done.8, ...), custom_call_target="tpu_custom_call" | custom-call | flops 3000000000 | bytes 1048576 | tf_op jit(solution)/shard_map/spread_two/pallas_call | solution.py:158
  44.4 1.1 collective-permute-start.6
  45.5 1.0 collective-permute-start.7
  46.4 2.0 %collective-permute-start.8 = (bf16[64,1024]{1,0:T(8,128)(2,1)S(1)}, bf16[64,1024]{1,0:T(8,128)(2,1)S(1)}, u32[]{:S(2)}, u32[]{:S(2)}) collective-permute-start(bf16[64,1024]{1,0:T(8,128)(2,1)S(1)} %get-tuple-element.42), channel_id=1, source_target_pairs={{0,3},{1,0},{2,1},{3,2},{4,7},{5,4},{6,5},{7,6},{8,11},{9,8},{10,9... | collective-permute-start | bytes 393224 | tf_op jit(solution)/shard_map/ppermute | solution.py:51
  48.9 3.6 %collective-permute-done.6.refs_1_ = bf16[64,1024]{1,0:T(8,128)(2,1)S(1)} collective-permute-done((bf16[64,1024]{1,0:T(8,128)(2,1)S(1)}, bf16[64,1024]{1,0:T(8,128)(2,1)S(1)}, u32[]{:S(2)}, u32[]{:S(2)}) %collective-permute-start.6) | collective-permute-done | bytes 131104 | tf_op jit(solution)/shard_map/ppermute | solution.py:51
  52.9 45.0 %all_to_all.10.h_ref = bf16[64,32,256]{2,1,0:T(8,128)(2,1)S(1)} all-to-all(bf16[64,32,256]{2,1,0:T(8,128)(2,1)S(1)} %mix_two.3), channel_id=1, replica_groups=mesh['snap'=64,'feat'=4] {'snap'}, dimensions={0} | all-to-all | bytes 2097152 | tf_op jit(solution)/shard_map/all_to_all | solution.py:381
  97.9 7.9 %attend.1 = bf16[4,64,16,128]{3,2,1,0:T(8,128)(2,1)S(1)} custom-call(bf16[64,32,256]{2,1,0:T(8,128)(2,1)S(1)} %all_to_all.10.h_ref, bf16[256,256]{1,0:T(8,128)(2,1)S(1)} %copy-done, bf16[256,256]{1,0:T(8,128)(2,1)S(1)} %copy-done.1, bf16[256,256]{1,0:T(8,128)(2,1)S(1)} %copy-done.2, bf16[256,256]{1,0:T(8,128)(2,1)S(1)} %copy-done.3), custom_call_target="tpu_custom_call" | custom-call | tf_op jit(solution)/shard_map/attend/pallas_call | solution.py:320
  105.8 39.5 %all_to_all.11.in_ref = bf16[256,16,128]{2,1,0:T(8,128)(2,1)S(1)} all-to-all(bf16[256,16,128]{2,1,0:T(8,128)(2,1)S(1)} %bitcast.4), channel_id=1, replica_groups=mesh['snap'=64,'feat'=4] {'feat','snap'}, dimensions={0} | all-to-all | bytes 2097152 | tf_op jit(solution)/shard_map/all_to_all | solution.py:383
  145.3 1.2 place.1
  (46 shorter events, 5.2 us)
Async XLA Ops:
  3.4 10.8 %collective-permute-start.9 = (bf16[2,64,1024]{2,1,0:T(8,128)(2,1)}, bf16[2,64,1024]{2,1,0:T(8,128)(2,1)S(1)}, u32[]{:S(2)}, u32[]{:S(2)}) collective-permute-start(bf16[2,64,1024]{2,1,0:T(8,128)(2,1)} %get-tuple-element.45), channel_id=1, source_target_pairs={{0,1},{1,2},{2,3},{3,0},{4,5},{5,6},{6,7},{7,4},{8,9},{9,10},{10,1... | collective-permute-start | bytes 786440 | tf_op jit(solution)/shard_map/ppermute | solution.py:51
  5.6 14.2 %collective-permute-start.10 = (bf16[2,64,1024]{2,1,0:T(8,128)(2,1)}, bf16[2,64,1024]{2,1,0:T(8,128)(2,1)S(1)}, u32[]{:S(2)}, u32[]{:S(2)}) collective-permute-start(bf16[2,64,1024]{2,1,0:T(8,128)(2,1)} %get-tuple-element.46), channel_id=1, source_target_pairs={{0,2},{1,3},{2,0},{3,1},{4,6},{5,7},{6,4},{7,5},{8,10},{9,11},{10,... | collective-permute-start | bytes 786440 | tf_op jit(solution)/shard_map/ppermute | solution.py:51
  8.2 12.5 %copy-start.10 = (bf16[2,64,1024]{2,1,0:T(8,128)(2,1)S(1)}, bf16[2,64,1024]{2,1,0:T(8,128)(2,1)}, u32[]{:S(2)}) copy-start(bf16[2,64,1024]{2,1,0:T(8,128)(2,1)} %get-tuple-element.44.refs_0_) | copy-start | bytes 786436
  8.2 12.5 %collective-permute-start.11 = (bf16[2,64,1024]{2,1,0:T(8,128)(2,1)}, bf16[2,64,1024]{2,1,0:T(8,128)(2,1)S(1)}, u32[]{:S(2)}, u32[]{:S(2)}) collective-permute-start(bf16[2,64,1024]{2,1,0:T(8,128)(2,1)} %get-tuple-element.47), channel_id=1, source_target_pairs={{0,3},{1,0},{2,1},{3,2},{4,7},{5,4},{6,5},{7,6},{8,11},{9,8},{10,9... | collective-permute-start | bytes 786440 | tf_op jit(solution)/shard_map/ppermute | solution.py:51
  12.9 23.8 %copy-start.4 = (bf16[2,64,128,128]{3,2,1,0:T(8,128)(2,1)S(1)}, bf16[2,64,128,128]{3,2,1,0:T(8,128)(2,1)}, u32[]{:S(2)}) copy-start(bf16[2,64,128,128]{3,2,1,0:T(8,128)(2,1)} %refs_4_.7) | copy-start | bytes 12582916
  12.9 14.6 %collective-permute-start = (bf16[2,64,1024]{2,1,0:T(8,128)(2,1)S(1)}, bf16[2,64,1024]{2,1,0:T(8,128)(2,1)S(1)}, u32[]{:S(2)}, u32[]{:S(2)}) collective-permute-start(bf16[2,64,1024]{2,1,0:T(8,128)(2,1)S(1)} %get-tuple-element.32), channel_id=1, source_target_pairs={{0,1},{1,2},{2,3},{3,0},{4,5},{5,6},{6,7},{7,4},{8,9},{9,10},{10,1... | collective-permute-start | bytes 786440 | tf_op jit(solution)/shard_map/ppermute | solution.py:51
  13.4 17.7 %collective-permute-start.1 = (bf16[2,64,1024]{2,1,0:T(8,128)(2,1)S(1)}, bf16[2,64,1024]{2,1,0:T(8,128)(2,1)S(1)}, u32[]{:S(2)}, u32[]{:S(2)}) collective-permute-start(bf16[2,64,1024]{2,1,0:T(8,128)(2,1)S(1)} %get-tuple-element.33), channel_id=1, source_target_pairs={{0,2},{1,3},{2,0},{3,1},{4,6},{5,7},{6,4},{7,5},{8,10},{9,11},{10,... | collective-permute-start | bytes 786440 | tf_op jit(solution)/shard_map/ppermute | solution.py:51
  14.2 17.1 %collective-permute-start.2 = (bf16[2,64,1024]{2,1,0:T(8,128)(2,1)S(1)}, bf16[2,64,1024]{2,1,0:T(8,128)(2,1)S(1)}, u32[]{:S(2)}, u32[]{:S(2)}) collective-permute-start(bf16[2,64,1024]{2,1,0:T(8,128)(2,1)S(1)} %get-tuple-element.34), channel_id=1, source_target_pairs={{0,3},{1,0},{2,1},{3,2},{4,7},{5,4},{6,5},{7,6},{8,11},{9,8},{10,9... | collective-permute-start | bytes 786440 | tf_op jit(solution)/shard_map/ppermute | solution.py:51
  21.1 15.4 %collective-permute-start.12 = (bf16[64,1024]{1,0:T(8,128)(2,1)S(1)}, bf16[64,1024]{1,0:T(8,128)(2,1)S(1)}, u32[]{:S(2)}, u32[]{:S(2)}) collective-permute-start(bf16[64,1024]{1,0:T(8,128)(2,1)S(1)} %get-tuple-element.49), channel_id=1, source_target_pairs={{0,1},{1,2},{2,3},{3,0},{4,5},{5,6},{6,7},{7,4},{8,9},{9,10},{10,1... | collective-permute-start | bytes 393224 | tf_op jit(solution)/shard_map/ppermute | solution.py:51
  21.5 15.2 %collective-permute-start.13 = (bf16[64,1024]{1,0:T(8,128)(2,1)S(1)}, bf16[64,1024]{1,0:T(8,128)(2,1)S(1)}, u32[]{:S(2)}, u32[]{:S(2)}) collective-permute-start(bf16[64,1024]{1,0:T(8,128)(2,1)S(1)} %get-tuple-element.50), channel_id=1, source_target_pairs={{0,2},{1,3},{2,0},{3,1},{4,6},{5,7},{6,4},{7,5},{8,10},{9,11},{10,... | collective-permute-start | bytes 393224 | tf_op jit(solution)/shard_map/ppermute | solution.py:51
  27.6 9.2 %collective-permute-start.14 = (bf16[64,1024]{1,0:T(8,128)(2,1)S(1)}, bf16[64,1024]{1,0:T(8,128)(2,1)S(1)}, u32[]{:S(2)}, u32[]{:S(2)}) collective-permute-start(bf16[64,1024]{1,0:T(8,128)(2,1)S(1)} %get-tuple-element.51), channel_id=1, source_target_pairs={{0,3},{1,0},{2,1},{3,2},{4,7},{5,4},{6,5},{7,6},{8,11},{9,8},{10,9... | collective-permute-start | bytes 393224 | tf_op jit(solution)/shard_map/ppermute | solution.py:51
  31.7 9.7 %collective-permute-start.3 = (bf16[64,1024]{1,0:T(8,128)(2,1)S(1)}, bf16[64,1024]{1,0:T(8,128)(2,1)S(1)}, u32[]{:S(2)}, u32[]{:S(2)}) collective-permute-start(bf16[64,1024]{1,0:T(8,128)(2,1)S(1)} %get-tuple-element.36), channel_id=1, source_target_pairs={{0,1},{1,2},{2,3},{3,0},{4,5},{5,6},{6,7},{7,4},{8,9},{9,10},{10,1... | collective-permute-start | bytes 393224 | tf_op jit(solution)/shard_map/ppermute | solution.py:51
  32.7 9.2 %collective-permute-start.4 = (bf16[64,1024]{1,0:T(8,128)(2,1)S(1)}, bf16[64,1024]{1,0:T(8,128)(2,1)S(1)}, u32[]{:S(2)}, u32[]{:S(2)}) collective-permute-start(bf16[64,1024]{1,0:T(8,128)(2,1)S(1)} %get-tuple-element.37), channel_id=1, source_target_pairs={{0,2},{1,3},{2,0},{3,1},{4,6},{5,7},{6,4},{7,5},{8,10},{9,11},{10,... | collective-permute-start | bytes 393224 | tf_op jit(solution)/shard_map/ppermute | solution.py:51
  36.5 5.4 %collective-permute-start.5 = (bf16[64,1024]{1,0:T(8,128)(2,1)S(1)}, bf16[64,1024]{1,0:T(8,128)(2,1)S(1)}, u32[]{:S(2)}, u32[]{:S(2)}) collective-permute-start(bf16[64,1024]{1,0:T(8,128)(2,1)S(1)} %get-tuple-element.38), channel_id=1, source_target_pairs={{0,3},{1,0},{2,1},{3,2},{4,7},{5,4},{6,5},{7,6},{8,11},{9,8},{10,9... | collective-permute-start | bytes 393224 | tf_op jit(solution)/shard_map/ppermute | solution.py:51
  37.8 8.7 %collective-permute-start.15 = (bf16[64,1024]{1,0:T(8,128)(2,1)S(1)}, bf16[64,1024]{1,0:T(8,128)(2,1)S(1)}, u32[]{:S(2)}, u32[]{:S(2)}) collective-permute-start(bf16[64,1024]{1,0:T(8,128)(2,1)S(1)} %get-tuple-element.53), channel_id=1, source_target_pairs={{0,1},{1,2},{2,3},{3,0},{4,5},{5,6},{6,7},{7,4},{8,9},{9,10},{10,1... | collective-permute-start | bytes 393224 | tf_op jit(solution)/shard_map/ppermute | solution.py:51
  39.1 9.3 %collective-permute-start.16 = (bf16[64,1024]{1,0:T(8,128)(2,1)S(1)}, bf16[64,1024]{1,0:T(8,128)(2,1)S(1)}, u32[]{:S(2)}, u32[]{:S(2)}) collective-permute-start(bf16[64,1024]{1,0:T(8,128)(2,1)S(1)} %get-tuple-element.54), channel_id=1, source_target_pairs={{0,2},{1,3},{2,0},{3,1},{4,6},{5,7},{6,4},{7,5},{8,10},{9,11},{10,... | collective-permute-start | bytes 393224 | tf_op jit(solution)/shard_map/ppermute | solution.py:51
  41.4 7.0 %collective-permute-start.17 = (bf16[64,1024]{1,0:T(8,128)(2,1)S(1)}, bf16[64,1024]{1,0:T(8,128)(2,1)S(1)}, u32[]{:S(2)}, u32[]{:S(2)}) collective-permute-start(bf16[64,1024]{1,0:T(8,128)(2,1)S(1)} %get-tuple-element.55), channel_id=1, source_target_pairs={{0,3},{1,0},{2,1},{3,2},{4,7},{5,4},{6,5},{7,6},{8,11},{9,8},{10,9... | collective-permute-start | bytes 393224 | tf_op jit(solution)/shard_map/ppermute | solution.py:51
  44.4 8.1 %collective-permute-start.6 = (bf16[64,1024]{1,0:T(8,128)(2,1)S(1)}, bf16[64,1024]{1,0:T(8,128)(2,1)S(1)}, u32[]{:S(2)}, u32[]{:S(2)}) collective-permute-start(bf16[64,1024]{1,0:T(8,128)(2,1)S(1)} %get-tuple-element.40), channel_id=1, source_target_pairs={{0,1},{1,2},{2,3},{3,0},{4,5},{5,6},{6,7},{7,4},{8,9},{9,10},{10,1... | collective-permute-start | bytes 393224 | tf_op jit(solution)/shard_map/ppermute | solution.py:51
  45.5 7.0 %collective-permute-start.7 = (bf16[64,1024]{1,0:T(8,128)(2,1)S(1)}, bf16[64,1024]{1,0:T(8,128)(2,1)S(1)}, u32[]{:S(2)}, u32[]{:S(2)}) collective-permute-start(bf16[64,1024]{1,0:T(8,128)(2,1)S(1)} %get-tuple-element.41), channel_id=1, source_target_pairs={{0,2},{1,3},{2,0},{3,1},{4,6},{5,7},{6,4},{7,5},{8,10},{9,11},{10,... | collective-permute-start | bytes 393224 | tf_op jit(solution)/shard_map/ppermute | solution.py:51
  46.4 6.0 %collective-permute-start.8 = (bf16[64,1024]{1,0:T(8,128)(2,1)S(1)}, bf16[64,1024]{1,0:T(8,128)(2,1)S(1)}, u32[]{:S(2)}, u32[]{:S(2)}) collective-permute-start(bf16[64,1024]{1,0:T(8,128)(2,1)S(1)} %get-tuple-element.42), channel_id=1, source_target_pairs={{0,3},{1,0},{2,1},{3,2},{4,7},{5,4},{6,5},{7,6},{8,11},{9,8},{10,9... | collective-permute-start | bytes 393224 | tf_op jit(solution)/shard_map/ppermute | solution.py:51
  48.4 49.5 %copy-start = (bf16[256,256]{1,0:T(8,128)(2,1)S(1)}, bf16[256,256]{1,0:T(8,128)(2,1)}, u32[]{:S(2)}) copy-start(bf16[256,256]{1,0:T(8,128)(2,1)} %wq_ref.1) | copy-start | bytes 393220
  48.4 49.5 %copy-start.1 = (bf16[256,256]{1,0:T(8,128)(2,1)S(1)}, bf16[256,256]{1,0:T(8,128)(2,1)}, u32[]{:S(2)}) copy-start(bf16[256,256]{1,0:T(8,128)(2,1)} %wk_ref.1) | copy-start | bytes 393220
  48.4 49.4 %copy-start.2 = (bf16[256,256]{1,0:T(8,128)(2,1)S(1)}, bf16[256,256]{1,0:T(8,128)(2,1)}, u32[]{:S(2)}) copy-start(bf16[256,256]{1,0:T(8,128)(2,1)} %wv_ref.1) | copy-start | bytes 393220
  48.5 49.4 %copy-start.3 = (bf16[256,256]{1,0:T(8,128)(2,1)S(1)}, bf16[256,256]{1,0:T(8,128)(2,1)}, u32[]{:S(2)}) copy-start(bf16[256,256]{1,0:T(8,128)(2,1)} %wo_ref.1) | copy-start | bytes 393220
  (5 other events, 46.9 us)

commit v4 on v3

--- a/solution.py
+++ b/solution.py
@@ -236,30 +236,40 @@
     )(me, *s, h, w, *before)
 
 
-def attend_kernel(h_ref, wq_ref, wk_ref, wv_ref, wo_ref, out_ref, hs, es, hb, qt, vt, ks, ct):
+def attend_kernel(wq_ref, wk_ref, wv_ref, wo_ref, *refs):
+    *h_refs, out_ref, hs, es, qt, vt, ks, ct = refs
     rows = SNAPS * V_S
-    for k in range(2):
-        hs[k] = h_ref[:, :, k * 128 : (k + 1) * 128].reshape(rows, 128).astype(f32)
-    for v in range(V_S):
+    for parity in range(2):
+        half = h_refs[parity][...] if len(h_refs) == 2 else h_refs[0][:, parity * V_S : (parity + 1) * V_S, :]
         for k in range(2):
-            hb[v * SNAPS : (v + 1) * SNAPS, k * 128 : (k + 1) * 128] = hs[
-                k, pl.ds(v, SNAPS, stride=V_S), :
-            ].astype(bf16)
+            hs[k, parity] = half[:, :, k * 128 : (k + 1) * 128].reshape(S_DEV * V_S, 128).astype(f32)
     wqt = wq_ref[...].T
     wvt = wv_ref[...].T
 
     def project(c, _):
-        at = pl.ds(pl.multiple_of(c * 512, 512), 512)
-        x = hb[at, :]
+        at = pl.ds(pl.multiple_of(c * 4 * SNAPS, 4 * SNAPS), 4 * SNAPS)
+        x = jnp.concatenate(
+            [
+                jnp.concatenate(
+                    [hs[k, parity, pl.ds(c * 4 + v, S_DEV, stride=V_S), :] for k in range(2)], axis=1
+                ).astype(bf16)
+                for v in range(4)
+                for parity in range(2)
+            ],
+            axis=0,
+        )
         qt[:, at] = lax.dot_general(wqt, x, NT, preferred_element_type=f32).astype(bf16)
         vt[:, at] = lax.dot_general(wvt, x, NT, preferred_element_type=f32).astype(bf16)
         ks[at, :] = jnp.dot(x, wk_ref[...], preferred_element_type=f32).astype(bf16)
         return 0
 
-    lax.fori_loop(0, rows // 512, project, 0)
-    causal = lax.broadcasted_iota(jnp.int32, (SNAPS, SNAPS), 0) <= lax.broadcasted_iota(
-        jnp.int32, (SNAPS, SNAPS), 1
-    )
+    lax.fori_loop(0, rows // 512, project, 0, unroll=4)
+
+    def time(dim):
+        r = lax.broadcasted_iota(jnp.int32, (SNAPS, SNAPS), dim)
+        return jnp.where(r < S_DEV, 2 * r, 2 * r - (SNAPS - 1))
+
+    causal = time(0) <= time(1)
     scale = HEAD_DIM**-0.5 * LOG2_E
 
     def vertex(v, _):
@@ -290,40 +300,29 @@
         return 0
 
     lax.fori_loop(0, V_S, vertex, 0, unroll=8)
+    low = lax.broadcasted_iota(jnp.int32, (S_DEV, 128), 1) < F_W
     for v in range(V_S):
+        at = pl.ds(v, S_DEV, stride=V_S)
         mixed = jnp.dot(
             ct[:, v * SNAPS : (v + 1) * SNAPS].T, wo_ref[...], preferred_element_type=f32
         )
         for k in range(2):
-            at = pl.ds(v, SNAPS, stride=V_S)
-            es[k, at, :] = hs[k, at, :] + mixed[:, k * 128 : (k + 1) * 128]
-    low = lax.broadcasted_iota(jnp.int32, (PACK, V_S, 128), 2) < F_W
-
-    def pack(c, _):
-        base = pl.multiple_of(c * PACK * 2 * V_S, PACK * 2 * V_S)
-        at = pl.ds(c * PACK, PACK)
-        for k in range(2):
-            both = es[k, pl.ds(base, PACK * 2 * V_S), :].reshape(PACK, 2, V_S, 128)
-            even, odd = both[:, 0], both[:, 1]
-            out_ref[2 * k, at] = jnp.where(low, even, pltpu.roll(odd, F_W, 2)).astype(bf16)
-            out_ref[2 * k + 1, at] = jnp.where(low, pltpu.roll(even, F_W, 2), odd).astype(bf16)
-        return 0
-
-    lax.fori_loop(0, S_DEV // PACK, pack, 0)
-
-
-PACK = 16
-
-
-def attend(hidden, wq, wk, wv, wo):
+            even = hs[k, 0, at, :] + mixed[:S_DEV, k * 128 : (k + 1) * 128]
+            odd = hs[k, 1, at, :] + mixed[S_DEV:, k * 128 : (k + 1) * 128]
+            es[2 * k, at, :] = jnp.where(low, even, pltpu.roll(odd, F_W, 1))
+            es[2 * k + 1, at, :] = jnp.where(low, pltpu.roll(even, F_W, 1), odd)
+    for f in range(F_DEV):
+        out_ref[f] = es[f].reshape(S_DEV, V_S, 128).astype(bf16)
+
+
+def attend(wq, wk, wv, wo, *hidden):
     rows = SNAPS * V_S
     return pl.pallas_call(
         attend_kernel,
         out_shape=jax.ShapeDtypeStruct((F_DEV, S_DEV, V_S, 2 * F_W), bf16),
         scratch_shapes=[
-            pltpu.VMEM((2, rows, 128), f32),
-            pltpu.VMEM((2, rows, 128), f32),
-            pltpu.VMEM((rows, D), bf16),
+            pltpu.VMEM((2, 2, S_DEV * V_S, 128), f32),
+            pltpu.VMEM((F_DEV, S_DEV * V_S, 128), f32),
             pltpu.VMEM((D, rows), bf16),
             pltpu.VMEM((D, rows), bf16),
             pltpu.VMEM((rows, D), bf16),
@@ -331,7 +330,7 @@
         ],
         compiler_params=params(32),
         name="attend",
-    )(hidden, wq, wk, wv, wo)
+    )(wq, wk, wv, wo, *hidden)
 
 
 def place_kernel(in_ref, out_ref):
@@ -379,7 +378,7 @@
     for t in both:
         hidden = [mix_two(me, s_two[t], ones[t][0], layer_two, hidden)]
     owned = lax.all_to_all(hidden[0], "snap", split_axis=0, concat_axis=0, tiled=True)
-    evolved = attend(owned, query_weight, key_weight, value_weight, out_weight)
+    evolved = attend(query_weight, key_weight, value_weight, out_weight, owned)
     pieces = lax.all_to_all(
         evolved.reshape(F_DEV * S_DEV, V_S, 2 * F_W),
         ("feat", "snap"),

time: 146 us -> 147 us (level)
  blocking collectives: 84.5 us -> 80.6 us
  Pallas kernels: 21.2 us -> 24.2 us
  waiting for transfers between devices: 13.7 us -> 15.6 us
    all_to_all x1, blocking collectives: 45 us -> 41.1 us  [on_device(): lax.all_to_all(hidden[0], 'snap', split_axis=0, concat_axis=0, tiled=True)]
    pallas_call x2, Pallas kernels: 3.52 us -> 5.55 us  [spread_two(): pl.pallas_call(functools.partial(spread_two_kernel, t), grid=(1,), in_spe...]
    pallas_call x2, Pallas kernels: 7 us -> 9.02 us  [spread_one(): pl.pallas_call(functools.partial(spread_one_kernel, t), in_specs=[SMEM] *...]
    ppermute x18, waiting for transfers between devices: 13.7 us -> 15.6 us  [turn(): lax.ppermute(blocks[k], 'feat', [(i, (i + k) % F_DEV) for i in range(F_DE...]
  transfers between devices with their start and end apart: 18 -> 18, of which waited for: 7 -> 5; matrix products, arithmetic and copies ran while one was open for 0% -> 0% of each run, Pallas kernels for 6% -> 7%
where the time goes in v4:
time: 147 us
  blocking collectives  80.6 us (55%)
  starting transfers between devices  26.2 us (18%)
  Pallas kernels  24.2 us (16%)
  waiting for transfers between devices  15.6 us (11%)
    all_to_all x1, blocking collectives, on_device(): lax.all_to_all(hidden[0], 'snap', split_axis=0, concat_axis=0, tiled=True)  41.1 us
    all_to_all x1, blocking collectives, on_device(): lax.all_to_all(evolved.reshape(F_DEV * S_DEV, V_S, 2 * F_W), ('feat', 'sn...  39.5 us
    ppermute x18, starting transfers between devices, turn(): lax.ppermute(blocks[k], 'feat', [(i, (i + k) % F_DEV) for i in range(F_DE...  26.2 us
    ppermute x18, waiting for transfers between devices, turn(): lax.ppermute(blocks[k], 'feat', [(i, (i + k) % F_DEV) for i in range(F_DE...  15.6 us
    pallas_call x2, Pallas kernels, spread_one(): pl.pallas_call(functools.partial(spread_one_kernel, t), in_specs=[SMEM] *...  9.02 us
    pallas_call x1, Pallas kernels, attend(): pl.pallas_call(attend_kernel, out_shape=jax.ShapeDtypeStruct((F_DEV, S_DE...  6.81 us
    pallas_call x2, Pallas kernels, spread_two(): pl.pallas_call(functools.partial(spread_two_kernel, t), grid=(1,), in_spe...  5.55 us
  transfers between devices with their start and end apart: 18, of which 5 were waited for; matrix products, arithmetic and copies ran while one was open for 0% of the time, Pallas kernels for 7%

profile of v4, /device:TPU:1, one launch (start us, length us, event | category | flops | bytes accessed | tf_op | source)
XLA Modules:
  0.0 146.8 jit_solution(14369614180801222348)
XLA Ops:
  0.0 5.4 %spread_one.3 = (bf16[2,64,1024]{2,1,0:T(8,128)(2,1)}, bf16[2,64,1024]{2,1,0:T(8,128)(2,1)}, bf16[2,64,1024]{2,1,0:T(8,128)(2,1)}, bf16[2,64,1024]{2,1,0:T(8,128)(2,1)}) custom-call(s32[1]{0:T(128)} %bitcast.me_ref, s32[2]{0:T(128)} %counts.7, s32[2,64]{1,0:T(2,128)} %rows.7, s32[2,64]{1,0:T(2,128)} %cols.7, bf16[2,64,4096]{2,1,0:T(8,128)(2,1)} %bitcast.5, ...), custom_call_target="tpu_custom_call" | custom-call | flops 4000000000 | bytes 1048576 | tf_op jit(solution)/shard_map/spread_one/pallas_call | solution.py:112
  5.4 2.2 %collective-permute-start.9 = (bf16[2,64,1024]{2,1,0:T(8,128)(2,1)}, bf16[2,64,1024]{2,1,0:T(8,128)(2,1)S(1)}, u32[]{:S(2)}, u32[]{:S(2)}) collective-permute-start(bf16[2,64,1024]{2,1,0:T(8,128)(2,1)} %get-tuple-element.45), channel_id=1, source_target_pairs={{0,1},{1,2},{2,3},{3,0},{4,5},{5,6},{6,7},{7,4},{8,9},{9,10},{10,1... | collective-permute-start | bytes 786440 | tf_op jit(solution)/shard_map/ppermute | solution.py:51
  7.6 2.6 %collective-permute-start.10 = (bf16[2,64,1024]{2,1,0:T(8,128)(2,1)}, bf16[2,64,1024]{2,1,0:T(8,128)(2,1)S(1)}, u32[]{:S(2)}, u32[]{:S(2)}) collective-permute-start(bf16[2,64,1024]{2,1,0:T(8,128)(2,1)} %get-tuple-element.46), channel_id=1, source_target_pairs={{0,2},{1,3},{2,0},{3,1},{4,6},{5,7},{6,4},{7,5},{8,10},{9,11},{10,... | collective-permute-start | bytes 786440 | tf_op jit(solution)/shard_map/ppermute | solution.py:51
  10.3 1.1 collective-permute-start.11
  11.3 3.6 %spread_one.2 = (bf16[2,64,1024]{2,1,0:T(8,128)(2,1)S(1)}, bf16[2,64,1024]{2,1,0:T(8,128)(2,1)S(1)}, bf16[2,64,1024]{2,1,0:T(8,128)(2,1)S(1)}, bf16[2,64,1024]{2,1,0:T(8,128)(2,1)S(1)}) custom-call(s32[1]{0:T(128)} %bitcast.me_ref, s32[2]{0:T(128)S(1)} %copy-done.9, s32[2,64]{1,0:T(2,128)S(1)} %copy-done.7, s32[2,64]{1,0:T(2,128)S(1)} %copy-done.8, ...), custom_call_target="tpu_custom_call" | custom-call | flops 4000000000 | bytes 1048576 | tf_op jit(solution)/shard_map/spread_one/pallas_call | solution.py:112
  16.3 1.7 %collective-permute-start.2 = (bf16[2,64,1024]{2,1,0:T(8,128)(2,1)S(1)}, bf16[2,64,1024]{2,1,0:T(8,128)(2,1)S(1)}, u32[]{:S(2)}, u32[]{:S(2)}) collective-permute-start(bf16[2,64,1024]{2,1,0:T(8,128)(2,1)S(1)} %get-tuple-element.34), channel_id=1, source_target_pairs={{0,3},{1,0},{2,1},{3,2},{4,7},{5,4},{6,5},{7,6},{8,11},{9,8},{10,9... | collective-permute-start | bytes 786440 | tf_op jit(solution)/shard_map/ppermute | solution.py:51
  17.9 4.7 %collective-permute-done.10.refs_2_ = bf16[2,64,1024]{2,1,0:T(8,128)(2,1)S(1)} collective-permute-done((bf16[2,64,1024]{2,1,0:T(8,128)(2,1)}, bf16[2,64,1024]{2,1,0:T(8,128)(2,1)S(1)}, u32[]{:S(2)}, u32[]{:S(2)}) %collective-permute-start.10) | collective-permute-done | bytes 262176 | tf_op jit(solution)/shard_map/ppermute | solution.py:51
  23.1 1.4 collective-permute-start.12
  24.4 3.0 %collective-permute-start.13 = (bf16[64,1024]{1,0:T(8,128)(2,1)S(1)}, bf16[64,1024]{1,0:T(8,128)(2,1)S(1)}, u32[]{:S(2)}, u32[]{:S(2)}) collective-permute-start(bf16[64,1024]{1,0:T(8,128)(2,1)S(1)} %get-tuple-element.50), channel_id=1, source_target_pairs={{0,2},{1,3},{2,0},{3,1},{4,6},{5,7},{6,4},{7,5},{8,10},{9,11},{10,... | collective-permute-start | bytes 393224 | tf_op jit(solution)/shard_map/ppermute | solution.py:51
  27.4 1.1 collective-permute-done.refs_1_
  28.9 5.1 %collective-permute-done.1.refs_2_ = bf16[2,64,1024]{2,1,0:T(8,128)(2,1)S(1)} collective-permute-done((bf16[2,64,1024]{2,1,0:T(8,128)(2,1)S(1)}, bf16[2,64,1024]{2,1,0:T(8,128)(2,1)S(1)}, u32[]{:S(2)}, u32[]{:S(2)}) %collective-permute-start.1) | collective-permute-done | bytes 262176 | tf_op jit(solution)/shard_map/ppermute | solution.py:51
  34.3 1.3 collective-permute-start.3
  35.6 3.0 %collective-permute-start.4 = (bf16[64,1024]{1,0:T(8,128)(2,1)S(1)}, bf16[64,1024]{1,0:T(8,128)(2,1)S(1)}, u32[]{:S(2)}, u32[]{:S(2)}) collective-permute-start(bf16[64,1024]{1,0:T(8,128)(2,1)S(1)} %get-tuple-element.37), channel_id=1, source_target_pairs={{0,2},{1,3},{2,0},{3,1},{4,6},{5,7},{6,4},{7,5},{8,10},{9,11},{10,... | collective-permute-start | bytes 393224 | tf_op jit(solution)/shard_map/ppermute | solution.py:51
  39.0 3.1 %spread_two.3 = (bf16[64,1024]{1,0:T(8,128)(2,1)S(1)}, bf16[64,1024]{1,0:T(8,128)(2,1)S(1)}, bf16[64,1024]{1,0:T(8,128)(2,1)S(1)}, bf16[64,1024]{1,0:T(8,128)(2,1)S(1)}) custom-call(s32[1]{0:T(128)} %bitcast.me_ref, s32[2]{0:T(128)S(1)} %copy-done.9, s32[2,64]{1,0:T(2,128)S(1)} %copy-done.7, s32[2,64]{1,0:T(2,128)S(1)} %copy-done.8, ...), custom_call_target="tpu_custom_call" | custom-call | flops 3000000000 | bytes 1048576 | tf_op jit(solution)/shard_map/spread_two/pallas_call | solution.py:158
  42.1 1.6 %collective-permute-start.15 = (bf16[64,1024]{1,0:T(8,128)(2,1)S(1)}, bf16[64,1024]{1,0:T(8,128)(2,1)S(1)}, u32[]{:S(2)}, u32[]{:S(2)}) collective-permute-start(bf16[64,1024]{1,0:T(8,128)(2,1)S(1)} %get-tuple-element.53), channel_id=1, source_target_pairs={{0,1},{1,2},{2,3},{3,0},{4,5},{5,6},{6,7},{7,4},{8,9},{9,10},{10,1... | collective-permute-start | bytes 393224 | tf_op jit(solution)/shard_map/ppermute | solution.py:51
  43.7 2.3 %collective-permute-start.16 = (bf16[64,1024]{1,0:T(8,128)(2,1)S(1)}, bf16[64,1024]{1,0:T(8,128)(2,1)S(1)}, u32[]{:S(2)}, u32[]{:S(2)}) collective-permute-start(bf16[64,1024]{1,0:T(8,128)(2,1)S(1)} %get-tuple-element.54), channel_id=1, source_target_pairs={{0,2},{1,3},{2,0},{3,1},{4,6},{5,7},{6,4},{7,5},{8,10},{9,11},{10,... | collective-permute-start | bytes 393224 | tf_op jit(solution)/shard_map/ppermute | solution.py:51
  46.8 2.5 %spread_two.2 = (bf16[64,1024]{1,0:T(8,128)(2,1)S(1)}, bf16[64,1024]{1,0:T(8,128)(2,1)S(1)}, bf16[64,1024]{1,0:T(8,128)(2,1)S(1)}, bf16[64,1024]{1,0:T(8,128)(2,1)S(1)}) custom-call(s32[1]{0:T(128)} %bitcast.me_ref, s32[2]{0:T(128)S(1)} %copy-done.9, s32[2,64]{1,0:T(2,128)S(1)} %copy-done.7, s32[2,64]{1,0:T(2,128)S(1)} %copy-done.8, ...), custom_call_target="tpu_custom_call" | custom-call | flops 3000000000 | bytes 1048576 | tf_op jit(solution)/shard_map/spread_two/pallas_call | solution.py:158
  50.0 1.0 collective-permute-start.7
  51.0 1.5 %collective-permute-start.8 = (bf16[64,1024]{1,0:T(8,128)(2,1)S(1)}, bf16[64,1024]{1,0:T(8,128)(2,1)S(1)}, u32[]{:S(2)}, u32[]{:S(2)}) collective-permute-start(bf16[64,1024]{1,0:T(8,128)(2,1)S(1)} %get-tuple-element.42), channel_id=1, source_target_pairs={{0,3},{1,0},{2,1},{3,2},{4,7},{5,4},{6,5},{7,6},{8,11},{9,8},{10,9... | collective-permute-start | bytes 393224 | tf_op jit(solution)/shard_map/ppermute | solution.py:51
  53.0 4.2 %collective-permute-done.6.refs_1_ = bf16[64,1024]{1,0:T(8,128)(2,1)S(1)} collective-permute-done((bf16[64,1024]{1,0:T(8,128)(2,1)S(1)}, bf16[64,1024]{1,0:T(8,128)(2,1)S(1)}, u32[]{:S(2)}, u32[]{:S(2)}) %collective-permute-start.6) | collective-permute-done | bytes 131104 | tf_op jit(solution)/shard_map/ppermute | solution.py:51
  58.2 41.1 %all_to_all.10.refs_0_ = bf16[64,32,256]{2,1,0:T(8,128)(2,1)S(1)} all-to-all(bf16[64,32,256]{2,1,0:T(8,128)(2,1)S(1)} %mix_two.3), channel_id=1, replica_groups=mesh['snap'=64,'feat'=4] {'snap'}, dimensions={0} | all-to-all | bytes 2097152 | tf_op jit(solution)/shard_map/all_to_all | solution.py:380
  99.3 6.8 %attend.1 = bf16[4,64,16,128]{3,2,1,0:T(8,128)(2,1)S(1)} custom-call(bf16[256,256]{1,0:T(8,128)(2,1)S(1)} %copy-done, bf16[256,256]{1,0:T(8,128)(2,1)S(1)} %copy-done.1, bf16[256,256]{1,0:T(8,128)(2,1)S(1)} %copy-done.2, bf16[256,256]{1,0:T(8,128)(2,1)S(1)} %copy-done.3, bf16[64,32,256]{2,1,0:T(8,128)(2,1)S(1)} %all_to_all.10.refs_0_), custom_call_target="tpu_custom_call" | custom-call | tf_op jit(solution)/shard_map/attend/pallas_call | solution.py:320
  106.1 39.5 %all_to_all.11.in_ref = bf16[256,16,128]{2,1,0:T(8,128)(2,1)S(1)} all-to-all(bf16[256,16,128]{2,1,0:T(8,128)(2,1)S(1)} %bitcast.4), channel_id=1, replica_groups=mesh['snap'=64,'feat'=4] {'feat','snap'}, dimensions={0} | all-to-all | bytes 2097152 | tf_op jit(solution)/shard_map/all_to_all | solution.py:382
  145.6 1.2 place.1
  (46 shorter events, 5.8 us)
Async XLA Ops:
  5.4 10.8 %collective-permute-start.9 = (bf16[2,64,1024]{2,1,0:T(8,128)(2,1)}, bf16[2,64,1024]{2,1,0:T(8,128)(2,1)S(1)}, u32[]{:S(2)}, u32[]{:S(2)}) collective-permute-start(bf16[2,64,1024]{2,1,0:T(8,128)(2,1)} %get-tuple-element.45), channel_id=1, source_target_pairs={{0,1},{1,2},{2,3},{3,0},{4,5},{5,6},{6,7},{7,4},{8,9},{9,10},{10,1... | collective-permute-start | bytes 786440 | tf_op jit(solution)/shard_map/ppermute | solution.py:51
  7.6 15.0 %collective-permute-start.10 = (bf16[2,64,1024]{2,1,0:T(8,128)(2,1)}, bf16[2,64,1024]{2,1,0:T(8,128)(2,1)S(1)}, u32[]{:S(2)}, u32[]{:S(2)}) collective-permute-start(bf16[2,64,1024]{2,1,0:T(8,128)(2,1)} %get-tuple-element.46), channel_id=1, source_target_pairs={{0,2},{1,3},{2,0},{3,1},{4,6},{5,7},{6,4},{7,5},{8,10},{9,11},{10,... | collective-permute-start | bytes 786440 | tf_op jit(solution)/shard_map/ppermute | solution.py:51
  10.3 12.4 %copy-start.10 = (bf16[2,64,1024]{2,1,0:T(8,128)(2,1)S(1)}, bf16[2,64,1024]{2,1,0:T(8,128)(2,1)}, u32[]{:S(2)}) copy-start(bf16[2,64,1024]{2,1,0:T(8,128)(2,1)} %get-tuple-element.44.refs_0_) | copy-start | bytes 786436
  10.3 12.4 %collective-permute-start.11 = (bf16[2,64,1024]{2,1,0:T(8,128)(2,1)}, bf16[2,64,1024]{2,1,0:T(8,128)(2,1)S(1)}, u32[]{:S(2)}, u32[]{:S(2)}) collective-permute-start(bf16[2,64,1024]{2,1,0:T(8,128)(2,1)} %get-tuple-element.47), channel_id=1, source_target_pairs={{0,3},{1,0},{2,1},{3,2},{4,7},{5,4},{6,5},{7,6},{8,11},{9,8},{10,9... | collective-permute-start | bytes 786440 | tf_op jit(solution)/shard_map/ppermute | solution.py:51
  15.0 24.1 %copy-start.4 = (bf16[2,64,128,128]{3,2,1,0:T(8,128)(2,1)S(1)}, bf16[2,64,128,128]{3,2,1,0:T(8,128)(2,1)}, u32[]{:S(2)}) copy-start(bf16[2,64,128,128]{3,2,1,0:T(8,128)(2,1)} %refs_4_.7) | copy-start | bytes 12582916
  15.0 13.5 %collective-permute-start = (bf16[2,64,1024]{2,1,0:T(8,128)(2,1)S(1)}, bf16[2,64,1024]{2,1,0:T(8,128)(2,1)S(1)}, u32[]{:S(2)}, u32[]{:S(2)}) collective-permute-start(bf16[2,64,1024]{2,1,0:T(8,128)(2,1)S(1)} %get-tuple-element.32), channel_id=1, source_target_pairs={{0,1},{1,2},{2,3},{3,0},{4,5},{5,6},{6,7},{7,4},{8,9},{9,10},{10,1... | collective-permute-start | bytes 786440 | tf_op jit(solution)/shard_map/ppermute | solution.py:51
  15.4 18.5 %collective-permute-start.1 = (bf16[2,64,1024]{2,1,0:T(8,128)(2,1)S(1)}, bf16[2,64,1024]{2,1,0:T(8,128)(2,1)S(1)}, u32[]{:S(2)}, u32[]{:S(2)}) collective-permute-start(bf16[2,64,1024]{2,1,0:T(8,128)(2,1)S(1)} %get-tuple-element.33), channel_id=1, source_target_pairs={{0,2},{1,3},{2,0},{3,1},{4,6},{5,7},{6,4},{7,5},{8,10},{9,11},{10,... | collective-permute-start | bytes 786440 | tf_op jit(solution)/shard_map/ppermute | solution.py:51
  16.3 17.7 %collective-permute-start.2 = (bf16[2,64,1024]{2,1,0:T(8,128)(2,1)S(1)}, bf16[2,64,1024]{2,1,0:T(8,128)(2,1)S(1)}, u32[]{:S(2)}, u32[]{:S(2)}) collective-permute-start(bf16[2,64,1024]{2,1,0:T(8,128)(2,1)S(1)} %get-tuple-element.34), channel_id=1, source_target_pairs={{0,3},{1,0},{2,1},{3,2},{4,7},{5,4},{6,5},{7,6},{8,11},{9,8},{10,9... | collective-permute-start | bytes 786440 | tf_op jit(solution)/shard_map/ppermute | solution.py:51
  23.1 15.6 %collective-permute-start.12 = (bf16[64,1024]{1,0:T(8,128)(2,1)S(1)}, bf16[64,1024]{1,0:T(8,128)(2,1)S(1)}, u32[]{:S(2)}, u32[]{:S(2)}) collective-permute-start(bf16[64,1024]{1,0:T(8,128)(2,1)S(1)} %get-tuple-element.49), channel_id=1, source_target_pairs={{0,1},{1,2},{2,3},{3,0},{4,5},{5,6},{6,7},{7,4},{8,9},{9,10},{10,1... | collective-permute-start | bytes 393224 | tf_op jit(solution)/shard_map/ppermute | solution.py:51
  24.4 14.6 %collective-permute-start.13 = (bf16[64,1024]{1,0:T(8,128)(2,1)S(1)}, bf16[64,1024]{1,0:T(8,128)(2,1)S(1)}, u32[]{:S(2)}, u32[]{:S(2)}) collective-permute-start(bf16[64,1024]{1,0:T(8,128)(2,1)S(1)} %get-tuple-element.50), channel_id=1, source_target_pairs={{0,2},{1,3},{2,0},{3,1},{4,6},{5,7},{6,4},{7,5},{8,10},{9,11},{10,... | collective-permute-start | bytes 393224 | tf_op jit(solution)/shard_map/ppermute | solution.py:51
  28.5 10.5 %collective-permute-start.14 = (bf16[64,1024]{1,0:T(8,128)(2,1)S(1)}, bf16[64,1024]{1,0:T(8,128)(2,1)S(1)}, u32[]{:S(2)}, u32[]{:S(2)}) collective-permute-start(bf16[64,1024]{1,0:T(8,128)(2,1)S(1)} %get-tuple-element.51), channel_id=1, source_target_pairs={{0,3},{1,0},{2,1},{3,2},{4,7},{5,4},{6,5},{7,6},{8,11},{9,8},{10,9... | collective-permute-start | bytes 393224 | tf_op jit(solution)/shard_map/ppermute | solution.py:51
  34.3 11.6 %collective-permute-start.3 = (bf16[64,1024]{1,0:T(8,128)(2,1)S(1)}, bf16[64,1024]{1,0:T(8,128)(2,1)S(1)}, u32[]{:S(2)}, u32[]{:S(2)}) collective-permute-start(bf16[64,1024]{1,0:T(8,128)(2,1)S(1)} %get-tuple-element.36), channel_id=1, source_target_pairs={{0,1},{1,2},{2,3},{3,0},{4,5},{5,6},{6,7},{7,4},{8,9},{9,10},{10,1... | collective-permute-start | bytes 393224 | tf_op jit(solution)/shard_map/ppermute | solution.py:51
  35.6 11.2 %collective-permute-start.4 = (bf16[64,1024]{1,0:T(8,128)(2,1)S(1)}, bf16[64,1024]{1,0:T(8,128)(2,1)S(1)}, u32[]{:S(2)}, u32[]{:S(2)}) collective-permute-start(bf16[64,1024]{1,0:T(8,128)(2,1)S(1)} %get-tuple-element.37), channel_id=1, source_target_pairs={{0,2},{1,3},{2,0},{3,1},{4,6},{5,7},{6,4},{7,5},{8,10},{9,11},{10,... | collective-permute-start | bytes 393224 | tf_op jit(solution)/shard_map/ppermute | solution.py:51
  38.6 8.2 %collective-permute-start.5 = (bf16[64,1024]{1,0:T(8,128)(2,1)S(1)}, bf16[64,1024]{1,0:T(8,128)(2,1)S(1)}, u32[]{:S(2)}, u32[]{:S(2)}) collective-permute-start(bf16[64,1024]{1,0:T(8,128)(2,1)S(1)} %get-tuple-element.38), channel_id=1, source_target_pairs={{0,3},{1,0},{2,1},{3,2},{4,7},{5,4},{6,5},{7,6},{8,11},{9,8},{10,9... | collective-permute-start | bytes 393224 | tf_op jit(solution)/shard_map/ppermute | solution.py:51
  42.1 8.9 %collective-permute-start.15 = (bf16[64,1024]{1,0:T(8,128)(2,1)S(1)}, bf16[64,1024]{1,0:T(8,128)(2,1)S(1)}, u32[]{:S(2)}, u32[]{:S(2)}) collective-permute-start(bf16[64,1024]{1,0:T(8,128)(2,1)S(1)} %get-tuple-element.53), channel_id=1, source_target_pairs={{0,1},{1,2},{2,3},{3,0},{4,5},{5,6},{6,7},{7,4},{8,9},{9,10},{10,1... | collective-permute-start | bytes 393224 | tf_op jit(solution)/shard_map/ppermute | solution.py:51
  43.7 8.8 %collective-permute-start.16 = (bf16[64,1024]{1,0:T(8,128)(2,1)S(1)}, bf16[64,1024]{1,0:T(8,128)(2,1)S(1)}, u32[]{:S(2)}, u32[]{:S(2)}) collective-permute-start(bf16[64,1024]{1,0:T(8,128)(2,1)S(1)} %get-tuple-element.54), channel_id=1, source_target_pairs={{0,2},{1,3},{2,0},{3,1},{4,6},{5,7},{6,4},{7,5},{8,10},{9,11},{10,... | collective-permute-start | bytes 393224 | tf_op jit(solution)/shard_map/ppermute | solution.py:51
  46.0 6.5 %collective-permute-start.17 = (bf16[64,1024]{1,0:T(8,128)(2,1)S(1)}, bf16[64,1024]{1,0:T(8,128)(2,1)S(1)}, u32[]{:S(2)}, u32[]{:S(2)}) collective-permute-start(bf16[64,1024]{1,0:T(8,128)(2,1)S(1)} %get-tuple-element.55), channel_id=1, source_target_pairs={{0,3},{1,0},{2,1},{3,2},{4,7},{5,4},{6,5},{7,6},{8,11},{9,8},{10,9... | collective-permute-start | bytes 393224 | tf_op jit(solution)/shard_map/ppermute | solution.py:51
  49.3 7.9 %collective-permute-start.6 = (bf16[64,1024]{1,0:T(8,128)(2,1)S(1)}, bf16[64,1024]{1,0:T(8,128)(2,1)S(1)}, u32[]{:S(2)}, u32[]{:S(2)}) collective-permute-start(bf16[64,1024]{1,0:T(8,128)(2,1)S(1)} %get-tuple-element.40), channel_id=1, source_target_pairs={{0,1},{1,2},{2,3},{3,0},{4,5},{5,6},{6,7},{7,4},{8,9},{9,10},{10,1... | collective-permute-start | bytes 393224 | tf_op jit(solution)/shard_map/ppermute | solution.py:51
  50.0 7.2 %collective-permute-start.7 = (bf16[64,1024]{1,0:T(8,128)(2,1)S(1)}, bf16[64,1024]{1,0:T(8,128)(2,1)S(1)}, u32[]{:S(2)}, u32[]{:S(2)}) collective-permute-start(bf16[64,1024]{1,0:T(8,128)(2,1)S(1)} %get-tuple-element.41), channel_id=1, source_target_pairs={{0,2},{1,3},{2,0},{3,1},{4,6},{5,7},{6,4},{7,5},{8,10},{9,11},{10,... | collective-permute-start | bytes 393224 | tf_op jit(solution)/shard_map/ppermute | solution.py:51
  51.0 6.8 %collective-permute-start.8 = (bf16[64,1024]{1,0:T(8,128)(2,1)S(1)}, bf16[64,1024]{1,0:T(8,128)(2,1)S(1)}, u32[]{:S(2)}, u32[]{:S(2)}) collective-permute-start(bf16[64,1024]{1,0:T(8,128)(2,1)S(1)} %get-tuple-element.42), channel_id=1, source_target_pairs={{0,3},{1,0},{2,1},{3,2},{4,7},{5,4},{6,5},{7,6},{8,11},{9,8},{10,9... | collective-permute-start | bytes 393224 | tf_op jit(solution)/shard_map/ppermute | solution.py:51
  52.5 46.7 %copy-start = (bf16[256,256]{1,0:T(8,128)(2,1)S(1)}, bf16[256,256]{1,0:T(8,128)(2,1)}, u32[]{:S(2)}) copy-start(bf16[256,256]{1,0:T(8,128)(2,1)} %wq_ref.1) | copy-start | bytes 393220
  52.6 46.7 %copy-start.1 = (bf16[256,256]{1,0:T(8,128)(2,1)S(1)}, bf16[256,256]{1,0:T(8,128)(2,1)}, u32[]{:S(2)}) copy-start(bf16[256,256]{1,0:T(8,128)(2,1)} %wk_ref.1) | copy-start | bytes 393220
  52.6 46.7 %copy-start.2 = (bf16[256,256]{1,0:T(8,128)(2,1)S(1)}, bf16[256,256]{1,0:T(8,128)(2,1)}, u32[]{:S(2)}) copy-start(bf16[256,256]{1,0:T(8,128)(2,1)} %wv_ref.1) | copy-start | bytes 393220
  52.6 46.7 %copy-start.3 = (bf16[256,256]{1,0:T(8,128)(2,1)S(1)}, bf16[256,256]{1,0:T(8,128)(2,1)}, u32[]{:S(2)}) copy-start(bf16[256,256]{1,0:T(8,128)(2,1)} %wo_ref.1) | copy-start | bytes 393220
  (5 other events, 52.2 us)

commit v5 on v4

--- a/solution.py
+++ b/solution.py
@@ -56,7 +56,6 @@
 
 def add_tiles(t, counts, rows, cols, features, tiles, acc, ready):
     n = counts[t]
-    acc[...] = jnp.zeros_like(acc)
 
     def group(g, _):
         ready(g)
@@ -90,7 +89,11 @@
         return 0
 
     lax.fori_loop(0, (counts[t] + GROUP - 1) // GROUP, start, 0)
+    acc[...] = jnp.zeros_like(acc)
     fetch_x.wait()
+    for k in range(F_DEV):
+        block = (me + k) % F_DEV
+        out_refs[k][0] = x[:, pl.ds(pl.multiple_of(block * V_F, V_F), V_F)]
     add_tiles(
         t,
         counts,
@@ -103,7 +106,6 @@
     )
     for k in range(F_DEV):
         block = (me + k) % F_DEV
-        out_refs[k][0] = x[:, pl.ds(pl.multiple_of(block * V_F, V_F), V_F)]
         for b in range(8):
             out_refs[k][1, :, b * TILE : (b + 1) * TILE] = acc[block * 8 + b].astype(bf16)
 
@@ -135,6 +137,7 @@
     me = me_ref[0]
     for k in range(F_DEV):
         h[(me + F_DEV - k) % F_DEV] = h_refs[k][...]
+    acc[...] = jnp.zeros_like(acc)
     add_tiles(
         t,
         counts,

time: 147 us -> 146 us (level)
  Pallas kernels: 24.2 us -> 21.2 us
  waiting for transfers between devices: 15.6 us -> 18.1 us
    ppermute x18, waiting for transfers between devices: 15.6 us -> 18.1 us  [turn(): lax.ppermute(blocks[k], 'feat', [(i, (i + k) % F_DEV) for i in range(F_DE...]
    pallas_call x2, Pallas kernels: 9.02 us -> 7.49 us  [spread_one(): pl.pallas_call(functools.partial(spread_one_kernel, t), in_specs=[SMEM] *...]
  transfers between devices with their start and end apart: 18 -> 18, of which waited for: 5 -> 9; matrix products, arithmetic and copies ran while one was open for 0% -> 0% of each run, Pallas kernels for 7% -> 5%
where the time goes in v5:
time: 146 us
  blocking collectives  79.6 us (55%)
  starting transfers between devices  26.7 us (18%)
  Pallas kernels  21.2 us (15%)
  waiting for transfers between devices  18.1 us (12%)
    all_to_all x1, blocking collectives, on_device(): lax.all_to_all(hidden[0], 'snap', split_axis=0, concat_axis=0, tiled=True)  40.1 us
    all_to_all x1, blocking collectives, on_device(): lax.all_to_all(evolved.reshape(F_DEV * S_DEV, V_S, 2 * F_W), ('feat', 'sn...  39.5 us
    ppermute x18, starting transfers between devices, turn(): lax.ppermute(blocks[k], 'feat', [(i, (i + k) % F_DEV) for i in range(F_DE...  26.7 us
    ppermute x18, waiting for transfers between devices, turn(): lax.ppermute(blocks[k], 'feat', [(i, (i + k) % F_DEV) for i in range(F_DE...  18.1 us
    pallas_call x2, Pallas kernels, spread_one(): pl.pallas_call(functools.partial(spread_one_kernel, t), in_specs=[SMEM] *...  7.49 us
    pallas_call x1, Pallas kernels, attend(): pl.pallas_call(attend_kernel, out_shape=jax.ShapeDtypeStruct((F_DEV, S_DE...  6.81 us
    pallas_call x2, Pallas kernels, spread_two(): pl.pallas_call(functools.partial(spread_two_kernel, t), grid=(1,), in_spe...  4.11 us
  transfers between devices with their start and end apart: 18, of which 9 were waited for; matrix products, arithmetic and copies ran while one was open for 0% of the time, Pallas kernels for 5%

profile of v5, /device:TPU:1, one launch (start us, length us, event | category | flops | bytes accessed | tf_op | source)
XLA Modules:
  0.0 145.8 jit_solution(11389432574603749846)
XLA Ops:
  0.0 5.4 %spread_one.3 = (bf16[2,64,1024]{2,1,0:T(8,128)(2,1)}, bf16[2,64,1024]{2,1,0:T(8,128)(2,1)}, bf16[2,64,1024]{2,1,0:T(8,128)(2,1)}, bf16[2,64,1024]{2,1,0:T(8,128)(2,1)}) custom-call(s32[1]{0:T(128)} %bitcast.me_ref, s32[2]{0:T(128)} %counts.7, s32[2,64]{1,0:T(2,128)} %rows.7, s32[2,64]{1,0:T(2,128)} %cols.7, bf16[2,64,4096]{2,1,0:T(8,128)(2,1)} %bitcast.5, ...), custom_call_target="tpu_custom_call" | custom-call | flops 4000000000 | bytes 1048576 | tf_op jit(solution)/shard_map/spread_one/pallas_call | solution.py:114
  5.4 2.2 %collective-permute-start.9 = (bf16[2,64,1024]{2,1,0:T(8,128)(2,1)}, bf16[2,64,1024]{2,1,0:T(8,128)(2,1)S(1)}, u32[]{:S(2)}, u32[]{:S(2)}) collective-permute-start(bf16[2,64,1024]{2,1,0:T(8,128)(2,1)} %get-tuple-element.45), channel_id=1, source_target_pairs={{0,1},{1,2},{2,3},{3,0},{4,5},{5,6},{6,7},{7,4},{8,9},{9,10},{10,1... | collective-permute-start | bytes 786440 | tf_op jit(solution)/shard_map/ppermute | solution.py:51
  7.6 2.6 %collective-permute-start.10 = (bf16[2,64,1024]{2,1,0:T(8,128)(2,1)}, bf16[2,64,1024]{2,1,0:T(8,128)(2,1)S(1)}, u32[]{:S(2)}, u32[]{:S(2)}) collective-permute-start(bf16[2,64,1024]{2,1,0:T(8,128)(2,1)} %get-tuple-element.46), channel_id=1, source_target_pairs={{0,2},{1,3},{2,0},{3,1},{4,6},{5,7},{6,4},{7,5},{8,10},{9,11},{10,... | collective-permute-start | bytes 786440 | tf_op jit(solution)/shard_map/ppermute | solution.py:51
  10.2 1.1 collective-permute-start.11
  11.3 2.1 %spread_one.2 = (bf16[2,64,1024]{2,1,0:T(8,128)(2,1)S(1)}, bf16[2,64,1024]{2,1,0:T(8,128)(2,1)S(1)}, bf16[2,64,1024]{2,1,0:T(8,128)(2,1)S(1)}, bf16[2,64,1024]{2,1,0:T(8,128)(2,1)S(1)}) custom-call(s32[1]{0:T(128)} %bitcast.me_ref, s32[2]{0:T(128)S(1)} %copy-done.9, s32[2,64]{1,0:T(2,128)S(1)} %copy-done.7, s32[2,64]{1,0:T(2,128)S(1)} %copy-done.8, ...), custom_call_target="tpu_custom_call" | custom-call | flops 4000000000 | bytes 1048576 | tf_op jit(solution)/shard_map/spread_one/pallas_call | solution.py:114
  15.3 2.2 %collective-permute-start.2 = (bf16[2,64,1024]{2,1,0:T(8,128)(2,1)S(1)}, bf16[2,64,1024]{2,1,0:T(8,128)(2,1)S(1)}, u32[]{:S(2)}, u32[]{:S(2)}) collective-permute-start(bf16[2,64,1024]{2,1,0:T(8,128)(2,1)S(1)} %get-tuple-element.34), channel_id=1, source_target_pairs={{0,3},{1,0},{2,1},{3,2},{4,7},{5,4},{6,5},{7,6},{8,11},{9,8},{10,9... | collective-permute-start | bytes 786440 | tf_op jit(solution)/shard_map/ppermute | solution.py:51
  17.5 5.1 %collective-permute-done.10.refs_2_ = bf16[2,64,1024]{2,1,0:T(8,128)(2,1)S(1)} collective-permute-done((bf16[2,64,1024]{2,1,0:T(8,128)(2,1)}, bf16[2,64,1024]{2,1,0:T(8,128)(2,1)S(1)}, u32[]{:S(2)}, u32[]{:S(2)}) %collective-permute-start.10) | collective-permute-done | bytes 262176 | tf_op jit(solution)/shard_map/ppermute | solution.py:51
  23.0 1.3 collective-permute-start.12
  24.4 3.0 %collective-permute-start.13 = (bf16[64,1024]{1,0:T(8,128)(2,1)S(1)}, bf16[64,1024]{1,0:T(8,128)(2,1)S(1)}, u32[]{:S(2)}, u32[]{:S(2)}) collective-permute-start(bf16[64,1024]{1,0:T(8,128)(2,1)S(1)} %get-tuple-element.50), channel_id=1, source_target_pairs={{0,2},{1,3},{2,0},{3,1},{4,6},{5,7},{6,4},{7,5},{8,10},{9,11},{10,... | collective-permute-start | bytes 393224 | tf_op jit(solution)/shard_map/ppermute | solution.py:51
  27.4 1.0 collective-permute-done.refs_1_
  28.8 5.1 %collective-permute-done.1.refs_2_ = bf16[2,64,1024]{2,1,0:T(8,128)(2,1)S(1)} collective-permute-done((bf16[2,64,1024]{2,1,0:T(8,128)(2,1)S(1)}, bf16[2,64,1024]{2,1,0:T(8,128)(2,1)S(1)}, u32[]{:S(2)}, u32[]{:S(2)}) %collective-permute-start.1) | collective-permute-done | bytes 262176 | tf_op jit(solution)/shard_map/ppermute | solution.py:51
  34.3 1.3 collective-permute-start.3
  35.5 3.0 %collective-permute-start.4 = (bf16[64,1024]{1,0:T(8,128)(2,1)S(1)}, bf16[64,1024]{1,0:T(8,128)(2,1)S(1)}, u32[]{:S(2)}, u32[]{:S(2)}) collective-permute-start(bf16[64,1024]{1,0:T(8,128)(2,1)S(1)} %get-tuple-element.37), channel_id=1, source_target_pairs={{0,2},{1,3},{2,0},{3,1},{4,6},{5,7},{6,4},{7,5},{8,10},{9,11},{10,... | collective-permute-start | bytes 393224 | tf_op jit(solution)/shard_map/ppermute | solution.py:51
  39.0 3.1 %spread_two.3 = (bf16[64,1024]{1,0:T(8,128)(2,1)S(1)}, bf16[64,1024]{1,0:T(8,128)(2,1)S(1)}, bf16[64,1024]{1,0:T(8,128)(2,1)S(1)}, bf16[64,1024]{1,0:T(8,128)(2,1)S(1)}) custom-call(s32[1]{0:T(128)} %bitcast.me_ref, s32[2]{0:T(128)S(1)} %copy-done.9, s32[2,64]{1,0:T(2,128)S(1)} %copy-done.7, s32[2,64]{1,0:T(2,128)S(1)} %copy-done.8, ...), custom_call_target="tpu_custom_call" | custom-call | flops 3000000000 | bytes 1048576 | tf_op jit(solution)/shard_map/spread_two/pallas_call | solution.py:161
  42.0 1.6 %collective-permute-start.15 = (bf16[64,1024]{1,0:T(8,128)(2,1)S(1)}, bf16[64,1024]{1,0:T(8,128)(2,1)S(1)}, u32[]{:S(2)}, u32[]{:S(2)}) collective-permute-start(bf16[64,1024]{1,0:T(8,128)(2,1)S(1)} %get-tuple-element.53), channel_id=1, source_target_pairs={{0,1},{1,2},{2,3},{3,0},{4,5},{5,6},{6,7},{7,4},{8,9},{9,10},{10,1... | collective-permute-start | bytes 393224 | tf_op jit(solution)/shard_map/ppermute | solution.py:51
  43.7 2.3 %collective-permute-start.16 = (bf16[64,1024]{1,0:T(8,128)(2,1)S(1)}, bf16[64,1024]{1,0:T(8,128)(2,1)S(1)}, u32[]{:S(2)}, u32[]{:S(2)}) collective-permute-start(bf16[64,1024]{1,0:T(8,128)(2,1)S(1)} %get-tuple-element.54), channel_id=1, source_target_pairs={{0,2},{1,3},{2,0},{3,1},{4,6},{5,7},{6,4},{7,5},{8,10},{9,11},{10,... | collective-permute-start | bytes 393224 | tf_op jit(solution)/shard_map/ppermute | solution.py:51
  46.8 1.0 spread_two.2
  49.5 1.5 %collective-permute-start.8 = (bf16[64,1024]{1,0:T(8,128)(2,1)S(1)}, bf16[64,1024]{1,0:T(8,128)(2,1)S(1)}, u32[]{:S(2)}, u32[]{:S(2)}) collective-permute-start(bf16[64,1024]{1,0:T(8,128)(2,1)S(1)} %get-tuple-element.42), channel_id=1, source_target_pairs={{0,3},{1,0},{2,1},{3,2},{4,7},{5,4},{6,5},{7,6},{8,11},{9,8},{10,9... | collective-permute-start | bytes 393224 | tf_op jit(solution)/shard_map/ppermute | solution.py:51
  52.2 2.1 %collective-permute-done.6.refs_1_ = bf16[64,1024]{1,0:T(8,128)(2,1)S(1)} collective-permute-done((bf16[64,1024]{1,0:T(8,128)(2,1)S(1)}, bf16[64,1024]{1,0:T(8,128)(2,1)S(1)}, u32[]{:S(2)}, u32[]{:S(2)}) %collective-permute-start.6) | collective-permute-done | bytes 131104 | tf_op jit(solution)/shard_map/ppermute | solution.py:51
  54.3 2.7 %collective-permute-done.7.refs_2_ = bf16[64,1024]{1,0:T(8,128)(2,1)S(1)} collective-permute-done((bf16[64,1024]{1,0:T(8,128)(2,1)S(1)}, bf16[64,1024]{1,0:T(8,128)(2,1)S(1)}, u32[]{:S(2)}, u32[]{:S(2)}) %collective-permute-start.7) | collective-permute-done | bytes 131104 | tf_op jit(solution)/shard_map/ppermute | solution.py:51
  58.1 40.1 %all_to_all.10.refs_0_ = bf16[64,32,256]{2,1,0:T(8,128)(2,1)S(1)} all-to-all(bf16[64,32,256]{2,1,0:T(8,128)(2,1)S(1)} %mix_two.3), channel_id=1, replica_groups=mesh['snap'=64,'feat'=4] {'snap'}, dimensions={0} | all-to-all | bytes 2097152 | tf_op jit(solution)/shard_map/all_to_all | solution.py:383
  98.2 6.8 %attend.1 = bf16[4,64,16,128]{3,2,1,0:T(8,128)(2,1)S(1)} custom-call(bf16[256,256]{1,0:T(8,128)(2,1)S(1)} %copy-done, bf16[256,256]{1,0:T(8,128)(2,1)S(1)} %copy-done.1, bf16[256,256]{1,0:T(8,128)(2,1)S(1)} %copy-done.2, bf16[256,256]{1,0:T(8,128)(2,1)S(1)} %copy-done.3, bf16[64,32,256]{2,1,0:T(8,128)(2,1)S(1)} %all_to_all.10.refs_0_), custom_call_target="tpu_custom_call" | custom-call | tf_op jit(solution)/shard_map/attend/pallas_call | solution.py:323
  105.1 39.5 %all_to_all.11.in_ref = bf16[256,16,128]{2,1,0:T(8,128)(2,1)S(1)} all-to-all(bf16[256,16,128]{2,1,0:T(8,128)(2,1)S(1)} %bitcast.4), channel_id=1, replica_groups=mesh['snap'=64,'feat'=4] {'feat','snap'}, dimensions={0} | all-to-all | bytes 2097152 | tf_op jit(solution)/shard_map/all_to_all | solution.py:385
  144.6 1.2 place.1
  (46 shorter events, 8.1 us)
Async XLA Ops:
  5.4 10.0 %collective-permute-start.9 = (bf16[2,64,1024]{2,1,0:T(8,128)(2,1)}, bf16[2,64,1024]{2,1,0:T(8,128)(2,1)S(1)}, u32[]{:S(2)}, u32[]{:S(2)}) collective-permute-start(bf16[2,64,1024]{2,1,0:T(8,128)(2,1)} %get-tuple-element.45), channel_id=1, source_target_pairs={{0,1},{1,2},{2,3},{3,0},{4,5},{5,6},{6,7},{7,4},{8,9},{9,10},{10,1... | collective-permute-start | bytes 786440 | tf_op jit(solution)/shard_map/ppermute | solution.py:51
  7.6 15.0 %collective-permute-start.10 = (bf16[2,64,1024]{2,1,0:T(8,128)(2,1)}, bf16[2,64,1024]{2,1,0:T(8,128)(2,1)S(1)}, u32[]{:S(2)}, u32[]{:S(2)}) collective-permute-start(bf16[2,64,1024]{2,1,0:T(8,128)(2,1)} %get-tuple-element.46), channel_id=1, source_target_pairs={{0,2},{1,3},{2,0},{3,1},{4,6},{5,7},{6,4},{7,5},{8,10},{9,11},{10,... | collective-permute-start | bytes 786440 | tf_op jit(solution)/shard_map/ppermute | solution.py:51
  10.2 12.4 %copy-start.10 = (bf16[2,64,1024]{2,1,0:T(8,128)(2,1)S(1)}, bf16[2,64,1024]{2,1,0:T(8,128)(2,1)}, u32[]{:S(2)}) copy-start(bf16[2,64,1024]{2,1,0:T(8,128)(2,1)} %get-tuple-element.44.refs_0_) | copy-start | bytes 786436
  10.2 12.4 %collective-permute-start.11 = (bf16[2,64,1024]{2,1,0:T(8,128)(2,1)}, bf16[2,64,1024]{2,1,0:T(8,128)(2,1)S(1)}, u32[]{:S(2)}, u32[]{:S(2)}) collective-permute-start(bf16[2,64,1024]{2,1,0:T(8,128)(2,1)} %get-tuple-element.47), channel_id=1, source_target_pairs={{0,3},{1,0},{2,1},{3,2},{4,7},{5,4},{6,5},{7,6},{8,11},{9,8},{10,9... | collective-permute-start | bytes 786440 | tf_op jit(solution)/shard_map/ppermute | solution.py:51
  13.4 25.5 %copy-start.4 = (bf16[2,64,128,128]{3,2,1,0:T(8,128)(2,1)S(1)}, bf16[2,64,128,128]{3,2,1,0:T(8,128)(2,1)}, u32[]{:S(2)}) copy-start(bf16[2,64,128,128]{3,2,1,0:T(8,128)(2,1)} %refs_4_.7) | copy-start | bytes 12582916
  13.4 15.0 %collective-permute-start = (bf16[2,64,1024]{2,1,0:T(8,128)(2,1)S(1)}, bf16[2,64,1024]{2,1,0:T(8,128)(2,1)S(1)}, u32[]{:S(2)}, u32[]{:S(2)}) collective-permute-start(bf16[2,64,1024]{2,1,0:T(8,128)(2,1)S(1)} %get-tuple-element.32), channel_id=1, source_target_pairs={{0,1},{1,2},{2,3},{3,0},{4,5},{5,6},{6,7},{7,4},{8,9},{9,10},{10,1... | collective-permute-start | bytes 786440 | tf_op jit(solution)/shard_map/ppermute | solution.py:51
  13.9 20.0 %collective-permute-start.1 = (bf16[2,64,1024]{2,1,0:T(8,128)(2,1)S(1)}, bf16[2,64,1024]{2,1,0:T(8,128)(2,1)S(1)}, u32[]{:S(2)}, u32[]{:S(2)}) collective-permute-start(bf16[2,64,1024]{2,1,0:T(8,128)(2,1)S(1)} %get-tuple-element.33), channel_id=1, source_target_pairs={{0,2},{1,3},{2,0},{3,1},{4,6},{5,7},{6,4},{7,5},{8,10},{9,11},{10,... | collective-permute-start | bytes 786440 | tf_op jit(solution)/shard_map/ppermute | solution.py:51
  15.3 18.6 %collective-permute-start.2 = (bf16[2,64,1024]{2,1,0:T(8,128)(2,1)S(1)}, bf16[2,64,1024]{2,1,0:T(8,128)(2,1)S(1)}, u32[]{:S(2)}, u32[]{:S(2)}) collective-permute-start(bf16[2,64,1024]{2,1,0:T(8,128)(2,1)S(1)} %get-tuple-element.34), channel_id=1, source_target_pairs={{0,3},{1,0},{2,1},{3,2},{4,7},{5,4},{6,5},{7,6},{8,11},{9,8},{10,9... | collective-permute-start | bytes 786440 | tf_op jit(solution)/shard_map/ppermute | solution.py:51
  23.0 15.6 %collective-permute-start.12 = (bf16[64,1024]{1,0:T(8,128)(2,1)S(1)}, bf16[64,1024]{1,0:T(8,128)(2,1)S(1)}, u32[]{:S(2)}, u32[]{:S(2)}) collective-permute-start(bf16[64,1024]{1,0:T(8,128)(2,1)S(1)} %get-tuple-element.49), channel_id=1, source_target_pairs={{0,1},{1,2},{2,3},{3,0},{4,5},{5,6},{6,7},{7,4},{8,9},{9,10},{10,1... | collective-permute-start | bytes 393224 | tf_op jit(solution)/shard_map/ppermute | solution.py:51
  24.4 14.6 %collective-permute-start.13 = (bf16[64,1024]{1,0:T(8,128)(2,1)S(1)}, bf16[64,1024]{1,0:T(8,128)(2,1)S(1)}, u32[]{:S(2)}, u32[]{:S(2)}) collective-permute-start(bf16[64,1024]{1,0:T(8,128)(2,1)S(1)} %get-tuple-element.50), channel_id=1, source_target_pairs={{0,2},{1,3},{2,0},{3,1},{4,6},{5,7},{6,4},{7,5},{8,10},{9,11},{10,... | collective-permute-start | bytes 393224 | tf_op jit(solution)/shard_map/ppermute | solution.py:51
  28.4 10.5 %collective-permute-start.14 = (bf16[64,1024]{1,0:T(8,128)(2,1)S(1)}, bf16[64,1024]{1,0:T(8,128)(2,1)S(1)}, u32[]{:S(2)}, u32[]{:S(2)}) collective-permute-start(bf16[64,1024]{1,0:T(8,128)(2,1)S(1)} %get-tuple-element.51), channel_id=1, source_target_pairs={{0,3},{1,0},{2,1},{3,2},{4,7},{5,4},{6,5},{7,6},{8,11},{9,8},{10,9... | collective-permute-start | bytes 393224 | tf_op jit(solution)/shard_map/ppermute | solution.py:51
  34.3 11.6 %collective-permute-start.3 = (bf16[64,1024]{1,0:T(8,128)(2,1)S(1)}, bf16[64,1024]{1,0:T(8,128)(2,1)S(1)}, u32[]{:S(2)}, u32[]{:S(2)}) collective-permute-start(bf16[64,1024]{1,0:T(8,128)(2,1)S(1)} %get-tuple-element.36), channel_id=1, source_target_pairs={{0,1},{1,2},{2,3},{3,0},{4,5},{5,6},{6,7},{7,4},{8,9},{9,10},{10,1... | collective-permute-start | bytes 393224 | tf_op jit(solution)/shard_map/ppermute | solution.py:51
  35.5 11.2 %collective-permute-start.4 = (bf16[64,1024]{1,0:T(8,128)(2,1)S(1)}, bf16[64,1024]{1,0:T(8,128)(2,1)S(1)}, u32[]{:S(2)}, u32[]{:S(2)}) collective-permute-start(bf16[64,1024]{1,0:T(8,128)(2,1)S(1)} %get-tuple-element.37), channel_id=1, source_target_pairs={{0,2},{1,3},{2,0},{3,1},{4,6},{5,7},{6,4},{7,5},{8,10},{9,11},{10,... | collective-permute-start | bytes 393224 | tf_op jit(solution)/shard_map/ppermute | solution.py:51
  38.6 8.2 %collective-permute-start.5 = (bf16[64,1024]{1,0:T(8,128)(2,1)S(1)}, bf16[64,1024]{1,0:T(8,128)(2,1)S(1)}, u32[]{:S(2)}, u32[]{:S(2)}) collective-permute-start(bf16[64,1024]{1,0:T(8,128)(2,1)S(1)} %get-tuple-element.38), channel_id=1, source_target_pairs={{0,3},{1,0},{2,1},{3,2},{4,7},{5,4},{6,5},{7,6},{8,11},{9,8},{10,9... | collective-permute-start | bytes 393224 | tf_op jit(solution)/shard_map/ppermute | solution.py:51
  42.0 7.5 %collective-permute-start.15 = (bf16[64,1024]{1,0:T(8,128)(2,1)S(1)}, bf16[64,1024]{1,0:T(8,128)(2,1)S(1)}, u32[]{:S(2)}, u32[]{:S(2)}) collective-permute-start(bf16[64,1024]{1,0:T(8,128)(2,1)S(1)} %get-tuple-element.53), channel_id=1, source_target_pairs={{0,1},{1,2},{2,3},{3,0},{4,5},{5,6},{6,7},{7,4},{8,9},{9,10},{10,1... | collective-permute-start | bytes 393224 | tf_op jit(solution)/shard_map/ppermute | solution.py:51
  43.7 7.7 %collective-permute-start.16 = (bf16[64,1024]{1,0:T(8,128)(2,1)S(1)}, bf16[64,1024]{1,0:T(8,128)(2,1)S(1)}, u32[]{:S(2)}, u32[]{:S(2)}) collective-permute-start(bf16[64,1024]{1,0:T(8,128)(2,1)S(1)} %get-tuple-element.54), channel_id=1, source_target_pairs={{0,2},{1,3},{2,0},{3,1},{4,6},{5,7},{6,4},{7,5},{8,10},{9,11},{10,... | collective-permute-start | bytes 393224 | tf_op jit(solution)/shard_map/ppermute | solution.py:51
  45.9 5.8 %collective-permute-start.17 = (bf16[64,1024]{1,0:T(8,128)(2,1)S(1)}, bf16[64,1024]{1,0:T(8,128)(2,1)S(1)}, u32[]{:S(2)}, u32[]{:S(2)}) collective-permute-start(bf16[64,1024]{1,0:T(8,128)(2,1)S(1)} %get-tuple-element.55), channel_id=1, source_target_pairs={{0,3},{1,0},{2,1},{3,2},{4,7},{5,4},{6,5},{7,6},{8,11},{9,8},{10,9... | collective-permute-start | bytes 393224 | tf_op jit(solution)/shard_map/ppermute | solution.py:51
  47.8 6.5 %collective-permute-start.6 = (bf16[64,1024]{1,0:T(8,128)(2,1)S(1)}, bf16[64,1024]{1,0:T(8,128)(2,1)S(1)}, u32[]{:S(2)}, u32[]{:S(2)}) collective-permute-start(bf16[64,1024]{1,0:T(8,128)(2,1)S(1)} %get-tuple-element.40), channel_id=1, source_target_pairs={{0,1},{1,2},{2,3},{3,0},{4,5},{5,6},{6,7},{7,4},{8,9},{9,10},{10,1... | collective-permute-start | bytes 393224 | tf_op jit(solution)/shard_map/ppermute | solution.py:51
  48.6 8.5 %collective-permute-start.7 = (bf16[64,1024]{1,0:T(8,128)(2,1)S(1)}, bf16[64,1024]{1,0:T(8,128)(2,1)S(1)}, u32[]{:S(2)}, u32[]{:S(2)}) collective-permute-start(bf16[64,1024]{1,0:T(8,128)(2,1)S(1)} %get-tuple-element.41), channel_id=1, source_target_pairs={{0,2},{1,3},{2,0},{3,1},{4,6},{5,7},{6,4},{7,5},{8,10},{9,11},{10,... | collective-permute-start | bytes 393224 | tf_op jit(solution)/shard_map/ppermute | solution.py:51
  49.5 8.2 %collective-permute-start.8 = (bf16[64,1024]{1,0:T(8,128)(2,1)S(1)}, bf16[64,1024]{1,0:T(8,128)(2,1)S(1)}, u32[]{:S(2)}, u32[]{:S(2)}) collective-permute-start(bf16[64,1024]{1,0:T(8,128)(2,1)S(1)} %get-tuple-element.42), channel_id=1, source_target_pairs={{0,3},{1,0},{2,1},{3,2},{4,7},{5,4},{6,5},{7,6},{8,11},{9,8},{10,9... | collective-permute-start | bytes 393224 | tf_op jit(solution)/shard_map/ppermute | solution.py:51
  51.7 46.5 %copy-start = (bf16[256,256]{1,0:T(8,128)(2,1)S(1)}, bf16[256,256]{1,0:T(8,128)(2,1)}, u32[]{:S(2)}) copy-start(bf16[256,256]{1,0:T(8,128)(2,1)} %wq_ref.1) | copy-start | bytes 393220
  51.7 46.5 %copy-start.1 = (bf16[256,256]{1,0:T(8,128)(2,1)S(1)}, bf16[256,256]{1,0:T(8,128)(2,1)}, u32[]{:S(2)}) copy-start(bf16[256,256]{1,0:T(8,128)(2,1)} %wk_ref.1) | copy-start | bytes 393220
  51.7 46.5 %copy-start.2 = (bf16[256,256]{1,0:T(8,128)(2,1)S(1)}, bf16[256,256]{1,0:T(8,128)(2,1)}, u32[]{:S(2)}) copy-start(bf16[256,256]{1,0:T(8,128)(2,1)} %wv_ref.1) | copy-start | bytes 393220
  51.8 46.5 %copy-start.3 = (bf16[256,256]{1,0:T(8,128)(2,1)S(1)}, bf16[256,256]{1,0:T(8,128)(2,1)}, u32[]{:S(2)}) copy-start(bf16[256,256]{1,0:T(8,128)(2,1)} %wo_ref.1) | copy-start | bytes 393220
  (5 other events, 51.2 us)

commit v6 on v4

--- a/solution.py
+++ b/solution.py
@@ -370,8 +370,12 @@
     lists = (tile_values, tile_rows, tile_cols, tile_counts)
 
     both = range(2)
-    s_one = [turn(spread_one(t, me, x, *lists)) for t in both]
-    ones = [mix_one(me, s_one[t], layer_one) for t in both]
+    s_one = [turn(spread_one(0, me, x, *lists))]
+    other = list(spread_one(1, me, x, *lists))
+    ones = [mix_one(me, s_one[0], layer_one)]
+    other[2], _ = lax.optimization_barrier((other[2], ones[0][1][0]))
+    s_one.append(turn(other))
+    ones.append(mix_one(me, s_one[1], layer_one))
     h_one = [turn(ones[t][1]) for t in both]
     s_two = [turn(spread_two(t, me, h_one[t], *lists)) for t in both]
     hidden = []

time: 147 us -> 147 us (level)
  blocking collectives: 80.6 us -> 84.7 us
  Pallas kernels: 24.2 us -> 21.3 us
    all_to_all x1, blocking collectives: 41.1 us -> 45.2 us  [on_device(): lax.all_to_all(hidden[0], 'snap', split_axis=0, concat_axis=0, tiled=True)]
  transfers between devices with their start and end apart: 18 -> 18, of which waited for: 5 -> 7; matrix products, arithmetic and copies ran while one was open for 0% -> 0% of each run, Pallas kernels for 7% -> 6%
where the time goes in v6:
time: 147 us
  blocking collectives  84.7 us (58%)
  starting transfers between devices  26.5 us (18%)
  Pallas kernels  21.3 us (14%)
  waiting for transfers between devices  14.3 us (10%)
    all_to_all x1, blocking collectives, on_device(): lax.all_to_all(hidden[0], 'snap', split_axis=0, concat_axis=0, tiled=True)  45.2 us
    all_to_all x1, blocking collectives, on_device(): lax.all_to_all(evolved.reshape(F_DEV * S_DEV, V_S, 2 * F_W), ('feat', 'sn...  39.5 us
    ppermute x18, starting transfers between devices, turn(): lax.ppermute(blocks[k], 'feat', [(i, (i + k) % F_DEV) for i in range(F_DE...  26.5 us
    ppermute x18, waiting for transfers between devices, turn(): lax.ppermute(blocks[k], 'feat', [(i, (i + k) % F_DEV) for i in range(F_DE...  14.3 us
    pallas_call x2, Pallas kernels, spread_one(): pl.pallas_call(functools.partial(spread_one_kernel, t), in_specs=[SMEM] *...  7.58 us
    pallas_call x1, Pallas kernels, attend(): pl.pallas_call(attend_kernel, out_shape=jax.ShapeDtypeStruct((F_DEV, S_DE...  6.81 us
    pallas_call x2, Pallas kernels, spread_two(): pl.pallas_call(functools.partial(spread_two_kernel, t), grid=(1,), in_spe...  4.08 us
  transfers between devices with their start and end apart: 18, of which 7 were waited for; matrix products, arithmetic and copies ran while one was open for 0% of the time, Pallas kernels for 6%

profile of v6, /device:TPU:1, one launch (start us, length us, event | category | flops | bytes accessed | tf_op | source)
XLA Modules:
  0.0 147.0 jit_solution(10759988489440411403)
XLA Ops:
  0.0 3.4 %spread_one.3 = (bf16[2,64,1024]{2,1,0:T(8,128)(2,1)}, bf16[2,64,1024]{2,1,0:T(8,128)(2,1)}, bf16[2,64,1024]{2,1,0:T(8,128)(2,1)}, bf16[2,64,1024]{2,1,0:T(8,128)(2,1)}) custom-call(s32[1]{0:T(128)} %bitcast.me_ref, s32[2]{0:T(128)} %counts.7, s32[2,64]{1,0:T(2,128)} %rows.7, s32[2,64]{1,0:T(2,128)} %cols.7, bf16[2,64,4096]{2,1,0:T(8,128)(2,1)} %bitcast.5, ...), custom_call_target="tpu_custom_call" | custom-call | flops 4000000000 | bytes 1048576 | tf_op jit(solution)/shard_map/spread_one/pallas_call | solution.py:112
  3.4 2.2 %collective-permute-start.1 = (bf16[2,64,1024]{2,1,0:T(8,128)(2,1)}, bf16[2,64,1024]{2,1,0:T(8,128)(2,1)S(1)}, u32[]{:S(2)}, u32[]{:S(2)}) collective-permute-start(bf16[2,64,1024]{2,1,0:T(8,128)(2,1)} %get-tuple-element.36), channel_id=1, source_target_pairs={{0,1},{1,2},{2,3},{3,0},{4,5},{5,6},{6,7},{7,4},{8,9},{9,10},{10,1... | collective-permute-start | bytes 786440 | tf_op jit(solution)/shard_map/ppermute | solution.py:51
  5.6 2.6 %collective-permute-start.2 = (bf16[2,64,1024]{2,1,0:T(8,128)(2,1)}, bf16[2,64,1024]{2,1,0:T(8,128)(2,1)S(1)}, u32[]{:S(2)}, u32[]{:S(2)}) collective-permute-start(bf16[2,64,1024]{2,1,0:T(8,128)(2,1)} %get-tuple-element.37), channel_id=1, source_target_pairs={{0,2},{1,3},{2,0},{3,1},{4,6},{5,7},{6,4},{7,5},{8,10},{9,11},{10,... | collective-permute-start | bytes 786440 | tf_op jit(solution)/shard_map/ppermute | solution.py:51
  9.3 4.2 %spread_one.2 = (bf16[2,64,1024]{2,1,0:T(8,128)(2,1)S(1)}, bf16[2,64,1024]{2,1,0:T(8,128)(2,1)S(1)}, bf16[2,64,1024]{2,1,0:T(8,128)(2,1)S(1)}, bf16[2,64,1024]{2,1,0:T(8,128)(2,1)S(1)}) custom-call(s32[1]{0:T(128)} %bitcast.me_ref, s32[2]{0:T(128)S(1)} %copy-done.9, s32[2,64]{1,0:T(2,128)S(1)} %copy-done.7, s32[2,64]{1,0:T(2,128)S(1)} %copy-done.8, ...), custom_call_target="tpu_custom_call" | custom-call | flops 4000000000 | bytes 1048576 | tf_op jit(solution)/shard_map/spread_one/pallas_call | solution.py:112
  14.0 2.3 %collective-permute-start.5 = (bf16[2,64,1024]{2,1,0:T(8,128)(2,1)S(1)}, bf16[2,64,1024]{2,1,0:T(8,128)(2,1)S(1)}, u32[]{:S(2)}, u32[]{:S(2)}) collective-permute-start(bf16[2,64,1024]{2,1,0:T(8,128)(2,1)S(1)} %get-tuple-element.41), channel_id=1, source_target_pairs={{0,3},{1,0},{2,1},{3,2},{4,7},{5,4},{6,5},{7,6},{8,11},{9,8},{10,9... | collective-permute-start | bytes 786440 | tf_op jit(solution)/shard_map/ppermute | solution.py:51
  16.3 3.2 %collective-permute-done.2.refs_2_ = bf16[2,64,1024]{2,1,0:T(8,128)(2,1)S(1)} collective-permute-done((bf16[2,64,1024]{2,1,0:T(8,128)(2,1)}, bf16[2,64,1024]{2,1,0:T(8,128)(2,1)S(1)}, u32[]{:S(2)}, u32[]{:S(2)}) %collective-permute-start.2) | collective-permute-done | bytes 262176 | tf_op jit(solution)/shard_map/ppermute | solution.py:51
  19.9 2.1 %collective-permute-start.4 = (bf16[2,64,1024]{2,1,0:T(8,128)(2,1)S(1)}, bf16[2,64,1024]{2,1,0:T(8,128)(2,1)S(1)}, u32[]{:S(2)}, u32[]{:S(2)}) collective-permute-start(bf16[2,64,1024]{2,1,0:T(8,128)(2,1)S(1)} %get-tuple-element.40), channel_id=1, source_target_pairs={{0,2},{1,3},{2,0},{3,1},{4,6},{5,7},{6,4},{7,5},{8,10},{9,11},{10,... | collective-permute-start | bytes 786440 | tf_op jit(solution)/shard_map/ppermute | solution.py:51
  23.0 2.1 %collective-permute-start.13 = (bf16[64,1024]{1,0:T(8,128)(2,1)S(1)}, bf16[64,1024]{1,0:T(8,128)(2,1)S(1)}, u32[]{:S(2)}, u32[]{:S(2)}) collective-permute-start(bf16[64,1024]{1,0:T(8,128)(2,1)S(1)} %get-tuple-element.52), channel_id=1, source_target_pairs={{0,2},{1,3},{2,0},{3,1},{4,6},{5,7},{6,4},{7,5},{8,10},{9,11},{10,... | collective-permute-start | bytes 393224 | tf_op jit(solution)/shard_map/ppermute | solution.py:51
  25.1 2.5 %collective-permute-done.refs_1_ = bf16[2,64,1024]{2,1,0:T(8,128)(2,1)S(1)} collective-permute-done((bf16[2,64,1024]{2,1,0:T(8,128)(2,1)S(1)}, bf16[2,64,1024]{2,1,0:T(8,128)(2,1)S(1)}, u32[]{:S(2)}, u32[]{:S(2)}) %collective-permute-start) | collective-permute-done | bytes 262176 | tf_op jit(solution)/shard_map/ppermute | solution.py:51
  27.6 2.4 %collective-permute-done.4.refs_2_ = bf16[2,64,1024]{2,1,0:T(8,128)(2,1)S(1)} collective-permute-done((bf16[2,64,1024]{2,1,0:T(8,128)(2,1)S(1)}, bf16[2,64,1024]{2,1,0:T(8,128)(2,1)S(1)}, u32[]{:S(2)}, u32[]{:S(2)}) %collective-permute-start.4) | collective-permute-done | bytes 262176 | tf_op jit(solution)/shard_map/ppermute | solution.py:51
  30.4 2.3 %collective-permute-start.6 = (bf16[64,1024]{1,0:T(8,128)(2,1)S(1)}, bf16[64,1024]{1,0:T(8,128)(2,1)S(1)}, u32[]{:S(2)}, u32[]{:S(2)}) collective-permute-start(bf16[64,1024]{1,0:T(8,128)(2,1)S(1)} %get-tuple-element.43), channel_id=1, source_target_pairs={{0,1},{1,2},{2,3},{3,0},{4,5},{5,6},{6,7},{7,4},{8,9},{9,10},{10,1... | collective-permute-start | bytes 393224 | tf_op jit(solution)/shard_map/ppermute | solution.py:51
  32.7 1.3 collective-permute-start.7
  34.0 2.0 %collective-permute-done.12.refs_1_ = bf16[64,1024]{1,0:T(8,128)(2,1)S(1)} collective-permute-done((bf16[64,1024]{1,0:T(8,128)(2,1)S(1)}, bf16[64,1024]{1,0:T(8,128)(2,1)S(1)}, u32[]{:S(2)}, u32[]{:S(2)}) %collective-permute-start.12) | collective-permute-done | bytes 131104 | tf_op jit(solution)/shard_map/ppermute | solution.py:51
  36.0 1.2 collective-permute-done.14.refs_3_
  38.6 4.7 %collective-permute-start.16 = (bf16[64,1024]{1,0:T(8,128)(2,1)S(1)}, bf16[64,1024]{1,0:T(8,128)(2,1)S(1)}, u32[]{:S(2)}, u32[]{:S(2)}) collective-permute-start(bf16[64,1024]{1,0:T(8,128)(2,1)S(1)} %get-tuple-element.56), channel_id=1, source_target_pairs={{0,2},{1,3},{2,0},{3,1},{4,6},{5,7},{6,4},{7,5},{8,10},{9,11},{10,... | collective-permute-start | bytes 393224 | tf_op jit(solution)/shard_map/ppermute | solution.py:51
  43.3 3.0 %spread_two.2 = (bf16[64,1024]{1,0:T(8,128)(2,1)S(1)}, bf16[64,1024]{1,0:T(8,128)(2,1)S(1)}, bf16[64,1024]{1,0:T(8,128)(2,1)S(1)}, bf16[64,1024]{1,0:T(8,128)(2,1)S(1)}) custom-call(s32[1]{0:T(128)} %bitcast.me_ref, s32[2]{0:T(128)S(1)} %copy-done.9, s32[2,64]{1,0:T(2,128)S(1)} %copy-done.7, s32[2,64]{1,0:T(2,128)S(1)} %copy-done.8, ...), custom_call_target="tpu_custom_call" | custom-call | flops 3000000000 | bytes 1048576 | tf_op jit(solution)/shard_map/spread_two/pallas_call | solution.py:158
  46.4 1.5 %collective-permute-start.9 = (bf16[64,1024]{1,0:T(8,128)(2,1)S(1)}, bf16[64,1024]{1,0:T(8,128)(2,1)S(1)}, u32[]{:S(2)}, u32[]{:S(2)}) collective-permute-start(bf16[64,1024]{1,0:T(8,128)(2,1)S(1)} %get-tuple-element.47), channel_id=1, source_target_pairs={{0,1},{1,2},{2,3},{3,0},{4,5},{5,6},{6,7},{7,4},{8,9},{9,10},{10,1... | collective-permute-start | bytes 393224 | tf_op jit(solution)/shard_map/ppermute | solution.py:51
  47.9 2.5 %collective-permute-start.11 = (bf16[64,1024]{1,0:T(8,128)(2,1)S(1)}, bf16[64,1024]{1,0:T(8,128)(2,1)S(1)}, u32[]{:S(2)}, u32[]{:S(2)}) collective-permute-start(bf16[64,1024]{1,0:T(8,128)(2,1)S(1)} %get-tuple-element.49), channel_id=1, source_target_pairs={{0,3},{1,0},{2,1},{3,2},{4,7},{5,4},{6,5},{7,6},{8,11},{9,8},{10,9... | collective-permute-start | bytes 393224 | tf_op jit(solution)/shard_map/ppermute | solution.py:51
  50.9 1.1 collective-permute-done.9.refs_1_
  52.0 1.8 %collective-permute-done.10.refs_2_ = bf16[64,1024]{1,0:T(8,128)(2,1)S(1)} collective-permute-done((bf16[64,1024]{1,0:T(8,128)(2,1)S(1)}, bf16[64,1024]{1,0:T(8,128)(2,1)S(1)}, u32[]{:S(2)}, u32[]{:S(2)}) %collective-permute-start.10) | collective-permute-done | bytes 131104 | tf_op jit(solution)/shard_map/ppermute | solution.py:51
  54.2 45.2 %all_to_all.10.refs_0_ = bf16[64,32,256]{2,1,0:T(8,128)(2,1)S(1)} all-to-all(bf16[64,32,256]{2,1,0:T(8,128)(2,1)S(1)} %mix_two.3), channel_id=1, replica_groups=mesh['snap'=64,'feat'=4] {'snap'}, dimensions={0} | all-to-all | bytes 2097152 | tf_op jit(solution)/shard_map/all_to_all | solution.py:384
  99.5 6.8 %attend.1 = bf16[4,64,16,128]{3,2,1,0:T(8,128)(2,1)S(1)} custom-call(bf16[256,256]{1,0:T(8,128)(2,1)S(1)} %copy-done, bf16[256,256]{1,0:T(8,128)(2,1)S(1)} %copy-done.1, bf16[256,256]{1,0:T(8,128)(2,1)S(1)} %copy-done.2, bf16[256,256]{1,0:T(8,128)(2,1)S(1)} %copy-done.3, bf16[64,32,256]{2,1,0:T(8,128)(2,1)S(1)} %all_to_all.10.refs_0_), custom_call_target="tpu_custom_call" | custom-call | tf_op jit(solution)/shard_map/attend/pallas_call | solution.py:320
  106.3 39.5 %all_to_all.11.in_ref = bf16[256,16,128]{2,1,0:T(8,128)(2,1)S(1)} all-to-all(bf16[256,16,128]{2,1,0:T(8,128)(2,1)S(1)} %bitcast.4), channel_id=1, replica_groups=mesh['snap'=64,'feat'=4] {'feat','snap'}, dimensions={0} | all-to-all | bytes 2097152 | tf_op jit(solution)/shard_map/all_to_all | solution.py:386
  145.8 1.2 place.1
  (46 shorter events, 5.6 us)
Async XLA Ops:
  3.4 12.9 %collective-permute-start.1 = (bf16[2,64,1024]{2,1,0:T(8,128)(2,1)}, bf16[2,64,1024]{2,1,0:T(8,128)(2,1)S(1)}, u32[]{:S(2)}, u32[]{:S(2)}) collective-permute-start(bf16[2,64,1024]{2,1,0:T(8,128)(2,1)} %get-tuple-element.36), channel_id=1, source_target_pairs={{0,1},{1,2},{2,3},{3,0},{4,5},{5,6},{6,7},{7,4},{8,9},{9,10},{10,1... | collective-permute-start | bytes 786440 | tf_op jit(solution)/shard_map/ppermute | solution.py:51
  5.6 13.9 %collective-permute-start.2 = (bf16[2,64,1024]{2,1,0:T(8,128)(2,1)}, bf16[2,64,1024]{2,1,0:T(8,128)(2,1)S(1)}, u32[]{:S(2)}, u32[]{:S(2)}) collective-permute-start(bf16[2,64,1024]{2,1,0:T(8,128)(2,1)} %get-tuple-element.37), channel_id=1, source_target_pairs={{0,2},{1,3},{2,0},{3,1},{4,6},{5,7},{6,4},{7,5},{8,10},{9,11},{10,... | collective-permute-start | bytes 786440 | tf_op jit(solution)/shard_map/ppermute | solution.py:51
  8.2 11.3 %copy-start.10 = (bf16[2,64,1024]{2,1,0:T(8,128)(2,1)S(1)}, bf16[2,64,1024]{2,1,0:T(8,128)(2,1)}, u32[]{:S(2)}) copy-start(bf16[2,64,1024]{2,1,0:T(8,128)(2,1)} %get-tuple-element.35.refs_0_) | copy-start | bytes 786436
  8.2 11.3 %collective-permute-start.3 = (bf16[2,64,1024]{2,1,0:T(8,128)(2,1)}, bf16[2,64,1024]{2,1,0:T(8,128)(2,1)S(1)}, u32[]{:S(2)}, u32[]{:S(2)}) collective-permute-start(bf16[2,64,1024]{2,1,0:T(8,128)(2,1)} %get-tuple-element.38), channel_id=1, source_target_pairs={{0,3},{1,0},{2,1},{3,2},{4,7},{5,4},{6,5},{7,6},{8,11},{9,8},{10,9... | collective-permute-start | bytes 786440 | tf_op jit(solution)/shard_map/ppermute | solution.py:51
  13.5 23.7 %copy-start.4 = (bf16[2,64,128,128]{3,2,1,0:T(8,128)(2,1)S(1)}, bf16[2,64,128,128]{3,2,1,0:T(8,128)(2,1)}, u32[]{:S(2)}) copy-start(bf16[2,64,128,128]{3,2,1,0:T(8,128)(2,1)} %refs_4_.7) | copy-start | bytes 12582916
  13.5 14.1 %collective-permute-start = (bf16[2,64,1024]{2,1,0:T(8,128)(2,1)S(1)}, bf16[2,64,1024]{2,1,0:T(8,128)(2,1)S(1)}, u32[]{:S(2)}, u32[]{:S(2)}) collective-permute-start(bf16[2,64,1024]{2,1,0:T(8,128)(2,1)S(1)} %get-tuple-element.33), channel_id=1, source_target_pairs={{0,1},{1,2},{2,3},{3,0},{4,5},{5,6},{6,7},{7,4},{8,9},{9,10},{10,1... | collective-permute-start | bytes 786440 | tf_op jit(solution)/shard_map/ppermute | solution.py:51
  14.0 13.6 %collective-permute-start.5 = (bf16[2,64,1024]{2,1,0:T(8,128)(2,1)S(1)}, bf16[2,64,1024]{2,1,0:T(8,128)(2,1)S(1)}, u32[]{:S(2)}, u32[]{:S(2)}) collective-permute-start(bf16[2,64,1024]{2,1,0:T(8,128)(2,1)S(1)} %get-tuple-element.41), channel_id=1, source_target_pairs={{0,3},{1,0},{2,1},{3,2},{4,7},{5,4},{6,5},{7,6},{8,11},{9,8},{10,9... | collective-permute-start | bytes 786440 | tf_op jit(solution)/shard_map/ppermute | solution.py:51
  19.9 10.1 %collective-permute-start.4 = (bf16[2,64,1024]{2,1,0:T(8,128)(2,1)S(1)}, bf16[2,64,1024]{2,1,0:T(8,128)(2,1)S(1)}, u32[]{:S(2)}, u32[]{:S(2)}) collective-permute-start(bf16[2,64,1024]{2,1,0:T(8,128)(2,1)S(1)} %get-tuple-element.40), channel_id=1, source_target_pairs={{0,2},{1,3},{2,0},{3,1},{4,6},{5,7},{6,4},{7,5},{8,10},{9,11},{10,... | collective-permute-start | bytes 786440 | tf_op jit(solution)/shard_map/ppermute | solution.py:51
  22.0 14.0 %collective-permute-start.12 = (bf16[64,1024]{1,0:T(8,128)(2,1)S(1)}, bf16[64,1024]{1,0:T(8,128)(2,1)S(1)}, u32[]{:S(2)}, u32[]{:S(2)}) collective-permute-start(bf16[64,1024]{1,0:T(8,128)(2,1)S(1)} %get-tuple-element.51), channel_id=1, source_target_pairs={{0,1},{1,2},{2,3},{3,0},{4,5},{5,6},{6,7},{7,4},{8,9},{9,10},{10,1... | collective-permute-start | bytes 393224 | tf_op jit(solution)/shard_map/ppermute | solution.py:51
  23.0 13.0 %collective-permute-start.13 = (bf16[64,1024]{1,0:T(8,128)(2,1)S(1)}, bf16[64,1024]{1,0:T(8,128)(2,1)S(1)}, u32[]{:S(2)}, u32[]{:S(2)}) collective-permute-start(bf16[64,1024]{1,0:T(8,128)(2,1)S(1)} %get-tuple-element.52), channel_id=1, source_target_pairs={{0,2},{1,3},{2,0},{3,1},{4,6},{5,7},{6,4},{7,5},{8,10},{9,11},{10,... | collective-permute-start | bytes 393224 | tf_op jit(solution)/shard_map/ppermute | solution.py:51
  27.6 9.6 %collective-permute-start.14 = (bf16[64,1024]{1,0:T(8,128)(2,1)S(1)}, bf16[64,1024]{1,0:T(8,128)(2,1)S(1)}, u32[]{:S(2)}, u32[]{:S(2)}) collective-permute-start(bf16[64,1024]{1,0:T(8,128)(2,1)S(1)} %get-tuple-element.53), channel_id=1, source_target_pairs={{0,3},{1,0},{2,1},{3,2},{4,7},{5,4},{6,5},{7,6},{8,11},{9,8},{10,9... | collective-permute-start | bytes 393224 | tf_op jit(solution)/shard_map/ppermute | solution.py:51
  30.4 12.9 %collective-permute-start.6 = (bf16[64,1024]{1,0:T(8,128)(2,1)S(1)}, bf16[64,1024]{1,0:T(8,128)(2,1)S(1)}, u32[]{:S(2)}, u32[]{:S(2)}) collective-permute-start(bf16[64,1024]{1,0:T(8,128)(2,1)S(1)} %get-tuple-element.43), channel_id=1, source_target_pairs={{0,1},{1,2},{2,3},{3,0},{4,5},{5,6},{6,7},{7,4},{8,9},{9,10},{10,1... | collective-permute-start | bytes 393224 | tf_op jit(solution)/shard_map/ppermute | solution.py:51
  32.7 10.6 %collective-permute-start.7 = (bf16[64,1024]{1,0:T(8,128)(2,1)S(1)}, bf16[64,1024]{1,0:T(8,128)(2,1)S(1)}, u32[]{:S(2)}, u32[]{:S(2)}) collective-permute-start(bf16[64,1024]{1,0:T(8,128)(2,1)S(1)} %get-tuple-element.44), channel_id=1, source_target_pairs={{0,2},{1,3},{2,0},{3,1},{4,6},{5,7},{6,4},{7,5},{8,10},{9,11},{10,... | collective-permute-start | bytes 393224 | tf_op jit(solution)/shard_map/ppermute | solution.py:51
  36.0 7.3 %collective-permute-start.8 = (bf16[64,1024]{1,0:T(8,128)(2,1)S(1)}, bf16[64,1024]{1,0:T(8,128)(2,1)S(1)}, u32[]{:S(2)}, u32[]{:S(2)}) collective-permute-start(bf16[64,1024]{1,0:T(8,128)(2,1)S(1)} %get-tuple-element.45), channel_id=1, source_target_pairs={{0,3},{1,0},{2,1},{3,2},{4,7},{5,4},{6,5},{7,6},{8,11},{9,8},{10,9... | collective-permute-start | bytes 393224 | tf_op jit(solution)/shard_map/ppermute | solution.py:51
  38.3 9.6 %collective-permute-start.15 = (bf16[64,1024]{1,0:T(8,128)(2,1)S(1)}, bf16[64,1024]{1,0:T(8,128)(2,1)S(1)}, u32[]{:S(2)}, u32[]{:S(2)}) collective-permute-start(bf16[64,1024]{1,0:T(8,128)(2,1)S(1)} %get-tuple-element.55), channel_id=1, source_target_pairs={{0,1},{1,2},{2,3},{3,0},{4,5},{5,6},{6,7},{7,4},{8,9},{9,10},{10,1... | collective-permute-start | bytes 393224 | tf_op jit(solution)/shard_map/ppermute | solution.py:51
  38.6 11.8 %collective-permute-start.16 = (bf16[64,1024]{1,0:T(8,128)(2,1)S(1)}, bf16[64,1024]{1,0:T(8,128)(2,1)S(1)}, u32[]{:S(2)}, u32[]{:S(2)}) collective-permute-start(bf16[64,1024]{1,0:T(8,128)(2,1)S(1)} %get-tuple-element.56), channel_id=1, source_target_pairs={{0,2},{1,3},{2,0},{3,1},{4,6},{5,7},{6,4},{7,5},{8,10},{9,11},{10,... | collective-permute-start | bytes 393224 | tf_op jit(solution)/shard_map/ppermute | solution.py:51
  43.3 7.1 %collective-permute-start.17 = (bf16[64,1024]{1,0:T(8,128)(2,1)S(1)}, bf16[64,1024]{1,0:T(8,128)(2,1)S(1)}, u32[]{:S(2)}, u32[]{:S(2)}) collective-permute-start(bf16[64,1024]{1,0:T(8,128)(2,1)S(1)} %get-tuple-element.57), channel_id=1, source_target_pairs={{0,3},{1,0},{2,1},{3,2},{4,7},{5,4},{6,5},{7,6},{8,11},{9,8},{10,9... | collective-permute-start | bytes 393224 | tf_op jit(solution)/shard_map/ppermute | solution.py:51
  46.4 5.6 %collective-permute-start.9 = (bf16[64,1024]{1,0:T(8,128)(2,1)S(1)}, bf16[64,1024]{1,0:T(8,128)(2,1)S(1)}, u32[]{:S(2)}, u32[]{:S(2)}) collective-permute-start(bf16[64,1024]{1,0:T(8,128)(2,1)S(1)} %get-tuple-element.47), channel_id=1, source_target_pairs={{0,1},{1,2},{2,3},{3,0},{4,5},{5,6},{6,7},{7,4},{8,9},{9,10},{10,1... | collective-permute-start | bytes 393224 | tf_op jit(solution)/shard_map/ppermute | solution.py:51
  47.9 5.9 %collective-permute-start.10 = (bf16[64,1024]{1,0:T(8,128)(2,1)S(1)}, bf16[64,1024]{1,0:T(8,128)(2,1)S(1)}, u32[]{:S(2)}, u32[]{:S(2)}) collective-permute-start(bf16[64,1024]{1,0:T(8,128)(2,1)S(1)} %get-tuple-element.48), channel_id=1, source_target_pairs={{0,2},{1,3},{2,0},{3,1},{4,6},{5,7},{6,4},{7,5},{8,10},{9,11},{10,... | collective-permute-start | bytes 393224 | tf_op jit(solution)/shard_map/ppermute | solution.py:51
  47.9 5.9 %collective-permute-start.11 = (bf16[64,1024]{1,0:T(8,128)(2,1)S(1)}, bf16[64,1024]{1,0:T(8,128)(2,1)S(1)}, u32[]{:S(2)}, u32[]{:S(2)}) collective-permute-start(bf16[64,1024]{1,0:T(8,128)(2,1)S(1)} %get-tuple-element.49), channel_id=1, source_target_pairs={{0,3},{1,0},{2,1},{3,2},{4,7},{5,4},{6,5},{7,6},{8,11},{9,8},{10,9... | collective-permute-start | bytes 393224 | tf_op jit(solution)/shard_map/ppermute | solution.py:51
  50.4 49.0 %copy-start = (bf16[256,256]{1,0:T(8,128)(2,1)S(1)}, bf16[256,256]{1,0:T(8,128)(2,1)}, u32[]{:S(2)}) copy-start(bf16[256,256]{1,0:T(8,128)(2,1)} %wq_ref.1) | copy-start | bytes 393220
  50.4 49.0 %copy-start.1 = (bf16[256,256]{1,0:T(8,128)(2,1)S(1)}, bf16[256,256]{1,0:T(8,128)(2,1)}, u32[]{:S(2)}) copy-start(bf16[256,256]{1,0:T(8,128)(2,1)} %wk_ref.1) | copy-start | bytes 393220
  50.4 49.0 %copy-start.2 = (bf16[256,256]{1,0:T(8,128)(2,1)S(1)}, bf16[256,256]{1,0:T(8,128)(2,1)}, u32[]{:S(2)}) copy-start(bf16[256,256]{1,0:T(8,128)(2,1)} %wv_ref.1) | copy-start | bytes 393220
  50.4 49.0 %copy-start.3 = (bf16[256,256]{1,0:T(8,128)(2,1)S(1)}, bf16[256,256]{1,0:T(8,128)(2,1)}, u32[]{:S(2)}) copy-start(bf16[256,256]{1,0:T(8,128)(2,1)} %wo_ref.1) | copy-start | bytes 393220
  (5 other events, 46.3 us)

commit v7 on v4

--- a/solution.py
+++ b/solution.py
@@ -20,7 +20,7 @@
 F_W = D // F_DEV
 V_F = VERT // F_DEV
 V_S = V_F // S_DEV
-GROUP = 8
+GROUP = 16
 
 masked_score = -1e30
 LOG2_E = 1.4426950408889634

time: 147 us -> 145 us (0.986)
  Pallas kernels: 24.2 us -> 19.9 us
  blocking collectives: 80.6 us -> 83.7 us
  waiting for transfers between devices: 15.6 us -> 13.8 us
    all_to_all x1, blocking collectives: 41.1 us -> 44.6 us  [on_device(): lax.all_to_all(hidden[0], 'snap', split_axis=0, concat_axis=0, tiled=True)]
    pallas_call x2, Pallas kernels: 5.55 us -> 3.38 us  [spread_two(): pl.pallas_call(functools.partial(spread_two_kernel, t), grid=(1,), in_spe...]
    pallas_call x2, Pallas kernels: 9.02 us -> 6.95 us  [spread_one(): pl.pallas_call(functools.partial(spread_one_kernel, t), in_specs=[SMEM] *...]
    ppermute x18, waiting for transfers between devices: 15.6 us -> 13.8 us  [turn(): lax.ppermute(blocks[k], 'feat', [(i, (i + k) % F_DEV) for i in range(F_DE...]
  transfers between devices with their start and end apart: 18 -> 18, of which waited for: 5 -> 7; matrix products, arithmetic and copies ran while one was open for 0% -> 0% of each run, Pallas kernels for 7% -> 5%
where the time goes in v7:
time: 145 us; the launch traced here: 144 us
  blocking collectives  83.7 us (58%)
  starting transfers between devices  26.7 us (18%)
  Pallas kernels  19.9 us (14%)
  waiting for transfers between devices  13.8 us (10%)
    all_to_all x1, blocking collectives, on_device(): lax.all_to_all(hidden[0], 'snap', split_axis=0, concat_axis=0, tiled=True)  44.6 us
    all_to_all x1, blocking collectives, on_device(): lax.all_to_all(evolved.reshape(F_DEV * S_DEV, V_S, 2 * F_W), ('feat', 'sn...  39.1 us
    ppermute x18, starting transfers between devices, turn(): lax.ppermute(blocks[k], 'feat', [(i, (i + k) % F_DEV) for i in range(F_DE...  26.7 us
    ppermute x18, waiting for transfers between devices, turn(): lax.ppermute(blocks[k], 'feat', [(i, (i + k) % F_DEV) for i in range(F_DE...  13.8 us
    pallas_call x2, Pallas kernels, spread_one(): pl.pallas_call(functools.partial(spread_one_kernel, t), in_specs=[SMEM] *...  6.95 us
    pallas_call x1, Pallas kernels, attend(): pl.pallas_call(attend_kernel, out_shape=jax.ShapeDtypeStruct((F_DEV, S_DE...  6.81 us
    pallas_call x2, Pallas kernels, spread_two(): pl.pallas_call(functools.partial(spread_two_kernel, t), grid=(1,), in_spe...  3.38 us
  transfers between devices with their start and end apart: 18, of which 7 were waited for; matrix products, arithmetic and copies ran while one was open for 0% of the time, Pallas kernels for 5%

profile of v7, /device:TPU:1, one launch (start us, length us, event | category | flops | bytes accessed | tf_op | source)
XLA Modules:
  0.0 144.3 jit_solution(860303147420766684)
XLA Ops:
  0.0 3.6 %spread_one.3 = (bf16[2,64,1024]{2,1,0:T(8,128)(2,1)}, bf16[2,64,1024]{2,1,0:T(8,128)(2,1)}, bf16[2,64,1024]{2,1,0:T(8,128)(2,1)}, bf16[2,64,1024]{2,1,0:T(8,128)(2,1)}) custom-call(s32[1]{0:T(128)} %bitcast.me_ref, s32[2]{0:T(128)} %counts.7, s32[2,64]{1,0:T(2,128)} %rows.7, s32[2,64]{1,0:T(2,128)} %cols.7, bf16[2,64,4096]{2,1,0:T(8,128)(2,1)} %bitcast.5, ...), custom_call_target="tpu_custom_call" | custom-call | flops 4000000000 | bytes 1048576 | tf_op jit(solution)/shard_map/spread_one/pallas_call | solution.py:112
  3.6 2.2 %collective-permute-start.9 = (bf16[2,64,1024]{2,1,0:T(8,128)(2,1)}, bf16[2,64,1024]{2,1,0:T(8,128)(2,1)S(1)}, u32[]{:S(2)}, u32[]{:S(2)}) collective-permute-start(bf16[2,64,1024]{2,1,0:T(8,128)(2,1)} %get-tuple-element.45), channel_id=1, source_target_pairs={{0,1},{1,2},{2,3},{3,0},{4,5},{5,6},{6,7},{7,4},{8,9},{9,10},{10,1... | collective-permute-start | bytes 786440 | tf_op jit(solution)/shard_map/ppermute | solution.py:51
  5.8 2.6 %collective-permute-start.10 = (bf16[2,64,1024]{2,1,0:T(8,128)(2,1)}, bf16[2,64,1024]{2,1,0:T(8,128)(2,1)S(1)}, u32[]{:S(2)}, u32[]{:S(2)}) collective-permute-start(bf16[2,64,1024]{2,1,0:T(8,128)(2,1)} %get-tuple-element.46), channel_id=1, source_target_pairs={{0,2},{1,3},{2,0},{3,1},{4,6},{5,7},{6,4},{7,5},{8,10},{9,11},{10,... | collective-permute-start | bytes 786440 | tf_op jit(solution)/shard_map/ppermute | solution.py:51
  8.5 1.1 collective-permute-start.11
  9.6 3.3 %spread_one.2 = (bf16[2,64,1024]{2,1,0:T(8,128)(2,1)S(1)}, bf16[2,64,1024]{2,1,0:T(8,128)(2,1)S(1)}, bf16[2,64,1024]{2,1,0:T(8,128)(2,1)S(1)}, bf16[2,64,1024]{2,1,0:T(8,128)(2,1)S(1)}) custom-call(s32[1]{0:T(128)} %bitcast.me_ref, s32[2]{0:T(128)S(1)} %copy-done.9, s32[2,64]{1,0:T(2,128)S(1)} %copy-done.7, s32[2,64]{1,0:T(2,128)S(1)} %copy-done.8, ...), custom_call_target="tpu_custom_call" | custom-call | flops 4000000000 | bytes 1048576 | tf_op jit(solution)/shard_map/spread_one/pallas_call | solution.py:112
  14.2 1.7 %collective-permute-start.2 = (bf16[2,64,1024]{2,1,0:T(8,128)(2,1)S(1)}, bf16[2,64,1024]{2,1,0:T(8,128)(2,1)S(1)}, u32[]{:S(2)}, u32[]{:S(2)}) collective-permute-start(bf16[2,64,1024]{2,1,0:T(8,128)(2,1)S(1)} %get-tuple-element.34), channel_id=1, source_target_pairs={{0,3},{1,0},{2,1},{3,2},{4,7},{5,4},{6,5},{7,6},{8,11},{9,8},{10,9... | collective-permute-start | bytes 786440 | tf_op jit(solution)/shard_map/ppermute | solution.py:51
  15.9 4.2 %collective-permute-done.10.refs_2_ = bf16[2,64,1024]{2,1,0:T(8,128)(2,1)S(1)} collective-permute-done((bf16[2,64,1024]{2,1,0:T(8,128)(2,1)}, bf16[2,64,1024]{2,1,0:T(8,128)(2,1)S(1)}, u32[]{:S(2)}, u32[]{:S(2)}) %collective-permute-start.10) | collective-permute-done | bytes 262176 | tf_op jit(solution)/shard_map/ppermute | solution.py:51
  20.0 1.1 collective-permute-done.11.refs_3_
  21.7 4.9 %collective-permute-start.13 = (bf16[64,1024]{1,0:T(8,128)(2,1)S(1)}, bf16[64,1024]{1,0:T(8,128)(2,1)S(1)}, u32[]{:S(2)}, u32[]{:S(2)}) collective-permute-start(bf16[64,1024]{1,0:T(8,128)(2,1)S(1)} %get-tuple-element.50), channel_id=1, source_target_pairs={{0,2},{1,3},{2,0},{3,1},{4,6},{5,7},{6,4},{7,5},{8,10},{9,11},{10,... | collective-permute-start | bytes 393224 | tf_op jit(solution)/shard_map/ppermute | solution.py:51
  26.6 1.1 collective-permute-done.refs_1_
  27.7 3.6 %collective-permute-done.1.refs_2_ = bf16[2,64,1024]{2,1,0:T(8,128)(2,1)S(1)} collective-permute-done((bf16[2,64,1024]{2,1,0:T(8,128)(2,1)S(1)}, bf16[2,64,1024]{2,1,0:T(8,128)(2,1)S(1)}, u32[]{:S(2)}, u32[]{:S(2)}) %collective-permute-start.1) | collective-permute-done | bytes 262176 | tf_op jit(solution)/shard_map/ppermute | solution.py:51
  32.0 1.0 collective-permute-start.3
  33.0 3.8 %collective-permute-start.4 = (bf16[64,1024]{1,0:T(8,128)(2,1)S(1)}, bf16[64,1024]{1,0:T(8,128)(2,1)S(1)}, u32[]{:S(2)}, u32[]{:S(2)}) collective-permute-start(bf16[64,1024]{1,0:T(8,128)(2,1)S(1)} %get-tuple-element.37), channel_id=1, source_target_pairs={{0,2},{1,3},{2,0},{3,1},{4,6},{5,7},{6,4},{7,5},{8,10},{9,11},{10,... | collective-permute-start | bytes 393224 | tf_op jit(solution)/shard_map/ppermute | solution.py:51
  36.9 1.2 spread_two.3
  38.2 1.4 collective-permute-start.15
  39.6 2.3 %collective-permute-start.16 = (bf16[64,1024]{1,0:T(8,128)(2,1)S(1)}, bf16[64,1024]{1,0:T(8,128)(2,1)S(1)}, u32[]{:S(2)}, u32[]{:S(2)}) collective-permute-start(bf16[64,1024]{1,0:T(8,128)(2,1)S(1)} %get-tuple-element.54), channel_id=1, source_target_pairs={{0,2},{1,3},{2,0},{3,1},{4,6},{5,7},{6,4},{7,5},{8,10},{9,11},{10,... | collective-permute-start | bytes 393224 | tf_op jit(solution)/shard_map/ppermute | solution.py:51
  42.3 2.2 %spread_two.2 = (bf16[64,1024]{1,0:T(8,128)(2,1)S(1)}, bf16[64,1024]{1,0:T(8,128)(2,1)S(1)}, bf16[64,1024]{1,0:T(8,128)(2,1)S(1)}, bf16[64,1024]{1,0:T(8,128)(2,1)S(1)}) custom-call(s32[1]{0:T(128)} %bitcast.me_ref, s32[2]{0:T(128)S(1)} %copy-done.9, s32[2,64]{1,0:T(2,128)S(1)} %copy-done.7, s32[2,64]{1,0:T(2,128)S(1)} %copy-done.8, ...), custom_call_target="tpu_custom_call" | custom-call | flops 3000000000 | bytes 1048576 | tf_op jit(solution)/shard_map/spread_two/pallas_call | solution.py:158
  44.5 1.1 collective-permute-start.6
  46.3 2.0 %collective-permute-start.8 = (bf16[64,1024]{1,0:T(8,128)(2,1)S(1)}, bf16[64,1024]{1,0:T(8,128)(2,1)S(1)}, u32[]{:S(2)}, u32[]{:S(2)}) collective-permute-start(bf16[64,1024]{1,0:T(8,128)(2,1)S(1)} %get-tuple-element.42), channel_id=1, source_target_pairs={{0,3},{1,0},{2,1},{3,2},{4,7},{5,4},{6,5},{7,6},{8,11},{9,8},{10,9... | collective-permute-start | bytes 393224 | tf_op jit(solution)/shard_map/ppermute | solution.py:51
  48.8 3.4 %collective-permute-done.6.refs_1_ = bf16[64,1024]{1,0:T(8,128)(2,1)S(1)} collective-permute-done((bf16[64,1024]{1,0:T(8,128)(2,1)S(1)}, bf16[64,1024]{1,0:T(8,128)(2,1)S(1)}, u32[]{:S(2)}, u32[]{:S(2)}) %collective-permute-start.6) | collective-permute-done | bytes 131104 | tf_op jit(solution)/shard_map/ppermute | solution.py:51
  52.6 44.6 %all_to_all.10.refs_0_ = bf16[64,32,256]{2,1,0:T(8,128)(2,1)S(1)} all-to-all(bf16[64,32,256]{2,1,0:T(8,128)(2,1)S(1)} %mix_two.3), channel_id=1, replica_groups=mesh['snap'=64,'feat'=4] {'snap'}, dimensions={0} | all-to-all | bytes 2097152 | tf_op jit(solution)/shard_map/all_to_all | solution.py:380
  97.2 6.8 %attend.1 = bf16[4,64,16,128]{3,2,1,0:T(8,128)(2,1)S(1)} custom-call(bf16[256,256]{1,0:T(8,128)(2,1)S(1)} %copy-done, bf16[256,256]{1,0:T(8,128)(2,1)S(1)} %copy-done.1, bf16[256,256]{1,0:T(8,128)(2,1)S(1)} %copy-done.2, bf16[256,256]{1,0:T(8,128)(2,1)S(1)} %copy-done.3, bf16[64,32,256]{2,1,0:T(8,128)(2,1)S(1)} %all_to_all.10.refs_0_), custom_call_target="tpu_custom_call" | custom-call | tf_op jit(solution)/shard_map/attend/pallas_call | solution.py:320
  104.0 39.1 %all_to_all.11.in_ref = bf16[256,16,128]{2,1,0:T(8,128)(2,1)S(1)} all-to-all(bf16[256,16,128]{2,1,0:T(8,128)(2,1)S(1)} %bitcast.4), channel_id=1, replica_groups=mesh['snap'=64,'feat'=4] {'feat','snap'}, dimensions={0} | all-to-all | bytes 2097152 | tf_op jit(solution)/shard_map/all_to_all | solution.py:382
  143.1 1.2 place.1
  (46 shorter events, 4.8 us)
Async XLA Ops:
  3.6 10.5 %collective-permute-start.9 = (bf16[2,64,1024]{2,1,0:T(8,128)(2,1)}, bf16[2,64,1024]{2,1,0:T(8,128)(2,1)S(1)}, u32[]{:S(2)}, u32[]{:S(2)}) collective-permute-start(bf16[2,64,1024]{2,1,0:T(8,128)(2,1)} %get-tuple-element.45), channel_id=1, source_target_pairs={{0,1},{1,2},{2,3},{3,0},{4,5},{5,6},{6,7},{7,4},{8,9},{9,10},{10,1... | collective-permute-start | bytes 786440 | tf_op jit(solution)/shard_map/ppermute | solution.py:51
  5.8 14.2 %collective-permute-start.10 = (bf16[2,64,1024]{2,1,0:T(8,128)(2,1)}, bf16[2,64,1024]{2,1,0:T(8,128)(2,1)S(1)}, u32[]{:S(2)}, u32[]{:S(2)}) collective-permute-start(bf16[2,64,1024]{2,1,0:T(8,128)(2,1)} %get-tuple-element.46), channel_id=1, source_target_pairs={{0,2},{1,3},{2,0},{3,1},{4,6},{5,7},{6,4},{7,5},{8,10},{9,11},{10,... | collective-permute-start | bytes 786440 | tf_op jit(solution)/shard_map/ppermute | solution.py:51
  8.5 12.7 %copy-start.10 = (bf16[2,64,1024]{2,1,0:T(8,128)(2,1)S(1)}, bf16[2,64,1024]{2,1,0:T(8,128)(2,1)}, u32[]{:S(2)}) copy-start(bf16[2,64,1024]{2,1,0:T(8,128)(2,1)} %get-tuple-element.44.refs_0_) | copy-start | bytes 786436
  8.5 12.7 %collective-permute-start.11 = (bf16[2,64,1024]{2,1,0:T(8,128)(2,1)}, bf16[2,64,1024]{2,1,0:T(8,128)(2,1)S(1)}, u32[]{:S(2)}, u32[]{:S(2)}) collective-permute-start(bf16[2,64,1024]{2,1,0:T(8,128)(2,1)} %get-tuple-element.47), channel_id=1, source_target_pairs={{0,3},{1,0},{2,1},{3,2},{4,7},{5,4},{6,5},{7,6},{8,11},{9,8},{10,9... | collective-permute-start | bytes 786440 | tf_op jit(solution)/shard_map/ppermute | solution.py:51
  12.9 24.1 %copy-start.4 = (bf16[2,64,128,128]{3,2,1,0:T(8,128)(2,1)S(1)}, bf16[2,64,128,128]{3,2,1,0:T(8,128)(2,1)}, u32[]{:S(2)}) copy-start(bf16[2,64,128,128]{3,2,1,0:T(8,128)(2,1)} %refs_4_.7) | copy-start | bytes 12582916
  12.9 14.8 %collective-permute-start = (bf16[2,64,1024]{2,1,0:T(8,128)(2,1)S(1)}, bf16[2,64,1024]{2,1,0:T(8,128)(2,1)S(1)}, u32[]{:S(2)}, u32[]{:S(2)}) collective-permute-start(bf16[2,64,1024]{2,1,0:T(8,128)(2,1)S(1)} %get-tuple-element.32), channel_id=1, source_target_pairs={{0,1},{1,2},{2,3},{3,0},{4,5},{5,6},{6,7},{7,4},{8,9},{9,10},{10,1... | collective-permute-start | bytes 786440 | tf_op jit(solution)/shard_map/ppermute | solution.py:51
  13.4 18.0 %collective-permute-start.1 = (bf16[2,64,1024]{2,1,0:T(8,128)(2,1)S(1)}, bf16[2,64,1024]{2,1,0:T(8,128)(2,1)S(1)}, u32[]{:S(2)}, u32[]{:S(2)}) collective-permute-start(bf16[2,64,1024]{2,1,0:T(8,128)(2,1)S(1)} %get-tuple-element.33), channel_id=1, source_target_pairs={{0,2},{1,3},{2,0},{3,1},{4,6},{5,7},{6,4},{7,5},{8,10},{9,11},{10,... | collective-permute-start | bytes 786440 | tf_op jit(solution)/shard_map/ppermute | solution.py:51
  14.2 17.4 %collective-permute-start.2 = (bf16[2,64,1024]{2,1,0:T(8,128)(2,1)S(1)}, bf16[2,64,1024]{2,1,0:T(8,128)(2,1)S(1)}, u32[]{:S(2)}, u32[]{:S(2)}) collective-permute-start(bf16[2,64,1024]{2,1,0:T(8,128)(2,1)S(1)} %get-tuple-element.34), channel_id=1, source_target_pairs={{0,3},{1,0},{2,1},{3,2},{4,7},{5,4},{6,5},{7,6},{8,11},{9,8},{10,9... | collective-permute-start | bytes 786440 | tf_op jit(solution)/shard_map/ppermute | solution.py:51
  21.6 15.2 %collective-permute-start.12 = (bf16[64,1024]{1,0:T(8,128)(2,1)S(1)}, bf16[64,1024]{1,0:T(8,128)(2,1)S(1)}, u32[]{:S(2)}, u32[]{:S(2)}) collective-permute-start(bf16[64,1024]{1,0:T(8,128)(2,1)S(1)} %get-tuple-element.49), channel_id=1, source_target_pairs={{0,1},{1,2},{2,3},{3,0},{4,5},{5,6},{6,7},{7,4},{8,9},{9,10},{10,1... | collective-permute-start | bytes 393224 | tf_op jit(solution)/shard_map/ppermute | solution.py:51
  21.7 15.2 %collective-permute-start.13 = (bf16[64,1024]{1,0:T(8,128)(2,1)S(1)}, bf16[64,1024]{1,0:T(8,128)(2,1)S(1)}, u32[]{:S(2)}, u32[]{:S(2)}) collective-permute-start(bf16[64,1024]{1,0:T(8,128)(2,1)S(1)} %get-tuple-element.50), channel_id=1, source_target_pairs={{0,2},{1,3},{2,0},{3,1},{4,6},{5,7},{6,4},{7,5},{8,10},{9,11},{10,... | collective-permute-start | bytes 393224 | tf_op jit(solution)/shard_map/ppermute | solution.py:51
  27.7 9.3 %collective-permute-start.14 = (bf16[64,1024]{1,0:T(8,128)(2,1)S(1)}, bf16[64,1024]{1,0:T(8,128)(2,1)S(1)}, u32[]{:S(2)}, u32[]{:S(2)}) collective-permute-start(bf16[64,1024]{1,0:T(8,128)(2,1)S(1)} %get-tuple-element.51), channel_id=1, source_target_pairs={{0,3},{1,0},{2,1},{3,2},{4,7},{5,4},{6,5},{7,6},{8,11},{9,8},{10,9... | collective-permute-start | bytes 393224 | tf_op jit(solution)/shard_map/ppermute | solution.py:51
  32.0 9.9 %collective-permute-start.3 = (bf16[64,1024]{1,0:T(8,128)(2,1)S(1)}, bf16[64,1024]{1,0:T(8,128)(2,1)S(1)}, u32[]{:S(2)}, u32[]{:S(2)}) collective-permute-start(bf16[64,1024]{1,0:T(8,128)(2,1)S(1)} %get-tuple-element.36), channel_id=1, source_target_pairs={{0,1},{1,2},{2,3},{3,0},{4,5},{5,6},{6,7},{7,4},{8,9},{9,10},{10,1... | collective-permute-start | bytes 393224 | tf_op jit(solution)/shard_map/ppermute | solution.py:51
  33.0 9.3 %collective-permute-start.4 = (bf16[64,1024]{1,0:T(8,128)(2,1)S(1)}, bf16[64,1024]{1,0:T(8,128)(2,1)S(1)}, u32[]{:S(2)}, u32[]{:S(2)}) collective-permute-start(bf16[64,1024]{1,0:T(8,128)(2,1)S(1)} %get-tuple-element.37), channel_id=1, source_target_pairs={{0,2},{1,3},{2,0},{3,1},{4,6},{5,7},{6,4},{7,5},{8,10},{9,11},{10,... | collective-permute-start | bytes 393224 | tf_op jit(solution)/shard_map/ppermute | solution.py:51
  36.8 5.5 %collective-permute-start.5 = (bf16[64,1024]{1,0:T(8,128)(2,1)S(1)}, bf16[64,1024]{1,0:T(8,128)(2,1)S(1)}, u32[]{:S(2)}, u32[]{:S(2)}) collective-permute-start(bf16[64,1024]{1,0:T(8,128)(2,1)S(1)} %get-tuple-element.38), channel_id=1, source_target_pairs={{0,3},{1,0},{2,1},{3,2},{4,7},{5,4},{6,5},{7,6},{8,11},{9,8},{10,9... | collective-permute-start | bytes 393224 | tf_op jit(solution)/shard_map/ppermute | solution.py:51
  38.2 8.2 %collective-permute-start.15 = (bf16[64,1024]{1,0:T(8,128)(2,1)S(1)}, bf16[64,1024]{1,0:T(8,128)(2,1)S(1)}, u32[]{:S(2)}, u32[]{:S(2)}) collective-permute-start(bf16[64,1024]{1,0:T(8,128)(2,1)S(1)} %get-tuple-element.53), channel_id=1, source_target_pairs={{0,1},{1,2},{2,3},{3,0},{4,5},{5,6},{6,7},{7,4},{8,9},{9,10},{10,1... | collective-permute-start | bytes 393224 | tf_op jit(solution)/shard_map/ppermute | solution.py:51
  39.6 8.8 %collective-permute-start.16 = (bf16[64,1024]{1,0:T(8,128)(2,1)S(1)}, bf16[64,1024]{1,0:T(8,128)(2,1)S(1)}, u32[]{:S(2)}, u32[]{:S(2)}) collective-permute-start(bf16[64,1024]{1,0:T(8,128)(2,1)S(1)} %get-tuple-element.54), channel_id=1, source_target_pairs={{0,2},{1,3},{2,0},{3,1},{4,6},{5,7},{6,4},{7,5},{8,10},{9,11},{10,... | collective-permute-start | bytes 393224 | tf_op jit(solution)/shard_map/ppermute | solution.py:51
  41.8 6.5 %collective-permute-start.17 = (bf16[64,1024]{1,0:T(8,128)(2,1)S(1)}, bf16[64,1024]{1,0:T(8,128)(2,1)S(1)}, u32[]{:S(2)}, u32[]{:S(2)}) collective-permute-start(bf16[64,1024]{1,0:T(8,128)(2,1)S(1)} %get-tuple-element.55), channel_id=1, source_target_pairs={{0,3},{1,0},{2,1},{3,2},{4,7},{5,4},{6,5},{7,6},{8,11},{9,8},{10,9... | collective-permute-start | bytes 393224 | tf_op jit(solution)/shard_map/ppermute | solution.py:51
  44.5 7.7 %collective-permute-start.6 = (bf16[64,1024]{1,0:T(8,128)(2,1)S(1)}, bf16[64,1024]{1,0:T(8,128)(2,1)S(1)}, u32[]{:S(2)}, u32[]{:S(2)}) collective-permute-start(bf16[64,1024]{1,0:T(8,128)(2,1)S(1)} %get-tuple-element.40), channel_id=1, source_target_pairs={{0,1},{1,2},{2,3},{3,0},{4,5},{5,6},{6,7},{7,4},{8,9},{9,10},{10,1... | collective-permute-start | bytes 393224 | tf_op jit(solution)/shard_map/ppermute | solution.py:51
  45.6 6.6 %collective-permute-start.7 = (bf16[64,1024]{1,0:T(8,128)(2,1)S(1)}, bf16[64,1024]{1,0:T(8,128)(2,1)S(1)}, u32[]{:S(2)}, u32[]{:S(2)}) collective-permute-start(bf16[64,1024]{1,0:T(8,128)(2,1)S(1)} %get-tuple-element.41), channel_id=1, source_target_pairs={{0,2},{1,3},{2,0},{3,1},{4,6},{5,7},{6,4},{7,5},{8,10},{9,11},{10,... | collective-permute-start | bytes 393224 | tf_op jit(solution)/shard_map/ppermute | solution.py:51
  46.3 5.8 %collective-permute-start.8 = (bf16[64,1024]{1,0:T(8,128)(2,1)S(1)}, bf16[64,1024]{1,0:T(8,128)(2,1)S(1)}, u32[]{:S(2)}, u32[]{:S(2)}) collective-permute-start(bf16[64,1024]{1,0:T(8,128)(2,1)S(1)} %get-tuple-element.42), channel_id=1, source_target_pairs={{0,3},{1,0},{2,1},{3,2},{4,7},{5,4},{6,5},{7,6},{8,11},{9,8},{10,9... | collective-permute-start | bytes 393224 | tf_op jit(solution)/shard_map/ppermute | solution.py:51
  48.3 48.9 %copy-start = (bf16[256,256]{1,0:T(8,128)(2,1)S(1)}, bf16[256,256]{1,0:T(8,128)(2,1)}, u32[]{:S(2)}) copy-start(bf16[256,256]{1,0:T(8,128)(2,1)} %wq_ref.1) | copy-start | bytes 393220
  48.3 48.9 %copy-start.1 = (bf16[256,256]{1,0:T(8,128)(2,1)S(1)}, bf16[256,256]{1,0:T(8,128)(2,1)}, u32[]{:S(2)}) copy-start(bf16[256,256]{1,0:T(8,128)(2,1)} %wk_ref.1) | copy-start | bytes 393220
  48.4 48.9 %copy-start.2 = (bf16[256,256]{1,0:T(8,128)(2,1)S(1)}, bf16[256,256]{1,0:T(8,128)(2,1)}, u32[]{:S(2)}) copy-start(bf16[256,256]{1,0:T(8,128)(2,1)} %wv_ref.1) | copy-start | bytes 393220
  48.4 48.9 %copy-start.3 = (bf16[256,256]{1,0:T(8,128)(2,1)S(1)}, bf16[256,256]{1,0:T(8,128)(2,1)}, u32[]{:S(2)}) copy-start(bf16[256,256]{1,0:T(8,128)(2,1)} %wo_ref.1) | copy-start | bytes 393220
  (5 other events, 47.3 us)
